TPU v7x, 32 devices: a whole 2x2x4 slice. The times are simulated.
32 devices in a mesh: dp: 8 (over z, x), mp: 4 (over y, core).
Axes of the slice: x: 2, y: 2, z: 4, core: 2. Of those that a mesh axis runs over, the one named last changes fastest.
Arguments:
- latents: bfloat16 [16, 1024, 32], P('dp', 'mp'), may hold values from -6 to 6
- noise: bfloat16 [16, 1024, 32], P('dp', 'mp'), may hold values from -6 to 6
- captions: bfloat16 [16, 512, 2304], P('dp', 'mp'), may hold values from -6 to 6
- res_ids: int32 [16], P('dp'), may hold values from 0 to 1, as said below
- timesteps: int32 [16, 4], P('dp'), may hold values from 0 to 999
- caption_lengths: int32 [16, 4], P('dp'), may hold values from 0 to 300, as said below
- in_proj: float32 [1152, 6, 1152], P('dp', None, 'mp'), may hold values from -0.1875 to 0.1875
- out_proj: float32 [2, 1152, 1152], P(None, 'mp', 'dp'), may hold values from -0.75 to 0.75
- w_up: float32 [1152, 2, 2880], P('dp', None, 'mp'), may hold values from -0.1875 to 0.1875
- w_down: float32 [2880, 1152], P('mp', 'dp'), may hold values from -0.109375 to 0.109375
- cond: float32 [11776, 1152], P(('dp', 'mp')), may hold values from -0.1875 to 0.1875
- conv: float32 [2, 10, 2880], replicated, may hold values from -0.4 to 0.4
- tables: float32 [73, 1152], replicated
- mom_in: float32 [1152, 6, 1152], P('dp', None, 'mp'), may hold values from -9.536743e-07 to 9.536743e-07
- mom_out: float32 [2, 1152, 1152], P(None, 'mp', 'dp'), may hold values from -9.536743e-07 to 9.536743e-07
- mom_up: float32 [1152, 2, 2880], P('dp', None, 'mp'), may hold values from -9.536743e-07 to 9.536743e-07
- mom_down: float32 [2880, 1152], P('mp', 'dp'), may hold values from -9.536743e-07 to 9.536743e-07
- mom_cond: float32 [11776, 1152], P(('dp', 'mp')), may hold values from -9.536743e-07 to 9.536743e-07
- mom_conv: float32 [2, 10, 2880], replicated, may hold values from -2.861023e-06 to 2.861023e-06
- mom_tables: float32 [73, 1152], replicated, may hold values from -2.861023e-06 to 2.861023e-06
- avg_in: float32 [1152, 6, 1152], P('dp', None, 'mp'), may hold values from -0.1875 to 0.1875
- avg_out: float32 [2, 1152, 1152], P(None, 'mp', 'dp'), may hold values from -0.75 to 0.75
- avg_up: float32 [1152, 2, 2880], P('dp', None, 'mp'), may hold values from -0.1875 to 0.1875
- avg_down: float32 [2880, 1152], P('mp', 'dp'), may hold values from -0.109375 to 0.109375
- avg_cond: float32 [11776, 1152], P(('dp', 'mp')), may hold values from -0.1875 to 0.1875
- avg_conv: float32 [2, 10, 2880], replicated, may hold values from -0.4 to 0.4
- avg_tables: float32 [73, 1152], replicated, may hold values from -1.75 to 1.75
Outputs:
- loss: float32 [], replicated
- grad_norm: float32 [], replicated
- new_in_proj: float32 [1152, 6, 1152], P('dp', None, 'mp')
- new_out_proj: float32 [2, 1152, 1152], P(None, 'mp', 'dp')
- new_w_up: float32 [1152, 2, 2880], P('dp', None, 'mp')
- new_w_down: float32 [2880, 1152], P('mp', 'dp')
- new_cond: float32 [11776, 1152], P(('dp', 'mp'))
- new_conv: float32 [2, 10, 2880], replicated
- new_tables: float32 [73, 1152], replicated
- new_mom_in: float32 [1152, 6, 1152], P('dp', None, 'mp')
- new_mom_out: float32 [2, 1152, 1152], P(None, 'mp', 'dp')
- new_mom_up: float32 [1152, 2, 2880], P('dp', None, 'mp')
- new_mom_down: float32 [2880, 1152], P('mp', 'dp')
- new_mom_cond: float32 [11776, 1152], P(('dp', 'mp'))
- clipped_conv: float32 [2, 10, 2880], replicated
- new_mom_tables: float32 [73, 1152], replicated
- new_avg_in: float32 [1152, 6, 1152], P('dp', None, 'mp')
- new_avg_out: float32 [2, 1152, 1152], P(None, 'mp', 'dp')
- new_avg_up: float32 [1152, 2, 2880], P('dp', None, 'mp')
- new_avg_down: float32 [2880, 1152], P('mp', 'dp')
- new_avg_cond: float32 [11776, 1152], P(('dp', 'mp'))
- new_avg_conv: float32 [2, 10, 2880], replicated
- new_avg_tables: float32 [73, 1152], replicated
Inputs may be any that keep to these rules, and one draw needn't show every extreme that they name: `res_ids`: 0 or 1; both occur. `caption_lengths`: for res 0 all four slots have lengths of 1 to 128; for res 1 slot 0 has 75 to 300 and the others 0; some caption has exactly 300 tokens.
All inputs are finite; a program needn't handle non-finite values.
Results may differ from a plain program's by a relative error of at most 0.0059.
Values may be sent and summed in bfloat16 or wider, within the bound.
A program may use at most 512 MiB of HBM per device.

v0:
```python
from functools import partial
import math

import jax
import jax.numpy as jnp
from jax import lax
from jax.sharding import PartitionSpec as P

D = 1152
CAPD = 2304
CIN = 32
FREQ = 256
CANVAS = 32
TXT = 512
HEAD_DIM = 32
XHEAD_DIM = 72
PARAMS = 34277760


HIGH = lax.Precision.HIGHEST
EPS = 1e-06
CLIP = 0.001
MOMENTUM = 0.9
AVERAGE_RATE = 0.1
STEP_SCALE = 0.01
TMAX = 1000.0
MASKED = -1e30


def exact_dot(left, right):
    return jnp.dot(left, right, precision=HIGH, preferred_element_type=jnp.float32)


def half_dot(left, right):
    return jnp.dot(left, right, preferred_element_type=jnp.float32)


def narrow(value):
    return value.astype(jnp.bfloat16)


def widen(value):
    return value.astype(jnp.float32)


def gather_rows(value):
    return lax.all_gather(value, "mp", axis=0, tiled=True)


def scatter_rows(value):
    return lax.psum_scatter(value, "mp", scatter_dimension=0, tiled=True)


def layer_norm(value):
    centred = value - jnp.mean(value, -1, keepdims=True)
    return centred * lax.rsqrt(jnp.mean(centred * centred, -1, keepdims=True) + EPS)


def modulate(value, shift, scale):
    return layer_norm(value) * (1.0 + scale) + shift


def rms_norm(value, gain):
    return value * lax.rsqrt(jnp.mean(value * value, -1, keepdims=True) + EPS) * gain


def gelu_tanh(value):
    return jax.nn.gelu(value, approximate=True)


def time_embed(steps_t):
    half_size = FREQ // 2
    freqs = jnp.exp(-math.log(10000.0) * jnp.arange(half_size, dtype=jnp.float32) / half_size)
    angles = steps_t.astype(jnp.float32)[:, None] * freqs[None, :]
    return jnp.concatenate([jnp.cos(angles), jnp.sin(angles)], axis=1)


def geometry(resolution, lengths):
    position = jnp.arange(CANVAS * CANVAS, dtype=jnp.int32)
    half_side = CANVAS // 2
    quadrant = position // CANVAS // half_side * 2 + position % CANVAS // half_side
    segment = jnp.where(resolution == 0, quadrant, 0)
    length_ends = jnp.cumsum(lengths)
    text_pos = jnp.arange(TXT, dtype=jnp.int32)
    text_segment = jnp.sum((text_pos[:, None] >= length_ends[None, :]).astype(jnp.int32), axis=1)
    return (segment, text_segment)


def depthwise(activity, kernel, segment):
    channels = activity.shape[2]
    grid_act = activity.reshape(CANVAS, CANVAS, 2, channels)
    grid_seg = segment.reshape(CANVAS, CANVAS)
    padded = jnp.pad(grid_act, ((1, 1), (1, 1), (0, 0), (0, 0)))
    seg_pad = jnp.pad(grid_seg, 1, constant_values=-1)
    total = jnp.zeros_like(grid_act) + kernel[:, 9][None, None]
    for row_off in range(3):
        for col_off in range(3):
            nearby = padded[row_off : row_off + CANVAS, col_off : col_off + CANVAS]
            same_img = (
                seg_pad[row_off : row_off + CANVAS, col_off : col_off + CANVAS] == grid_seg
            ).astype(jnp.float32)
            total = (
                total
                + nearby * same_img[:, :, None, None] * kernel[:, row_off * 3 + col_off][None, None]
            )
    return total.reshape(activity.shape)


def conv_glu(segment, upper, kernel):
    mixed = depthwise(jax.nn.silu(upper), kernel, segment)
    return mixed[:, 0] * jax.nn.silu(mixed[:, 1])


def linear_attention(onehot, query, keys, values):
    state = jnp.einsum("ps,phd,phe->shde", onehot, keys, values, precision=HIGH)
    key_sum = jnp.einsum("ps,phd->shd", onehot, keys, precision=HIGH)
    numer = jnp.einsum("ps,phd,shde->phe", onehot, query, state, precision=HIGH)
    denom = jnp.einsum("ps,phd,shd->ph", onehot, query, key_sum, precision=HIGH) + 1.0
    return numer / denom[:, :, None]


def mod_table(local_hot, table_rows, time_mod):
    return table_rows[None] + exact_dot(local_hot, time_mod).reshape(local_hot.shape[0], 6, D)


def final_loss(local_hot, target, loss_weight, state, final_rows, time_emb, out_rows):
    shift_scale = final_rows[None] + exact_dot(local_hot, time_emb)[:, None]
    normed = modulate(state, shift_scale[:, 0], shift_scale[:, 1])
    output = jnp.einsum("pd,cd->pc", normed, out_rows, precision=HIGH)
    error = output - target
    return jnp.sum(error * error) * loss_weight


def cross_scores(query_h, keys_h, match):
    scores = jnp.einsum(
        "phd,thd->hpt", query_h, keys_h, preferred_element_type=jnp.float32
    ) * XHEAD_DIM ** (-0.5)
    return jnp.where(match[None], scores, MASKED)


def layer_forward(weights, latent, noise_c, caption, resolution, steps_t, lengths, count):
    w_in, w_out, w_upper, w_lower, w_cond, kernel, tables = weights
    rank = lax.axis_index("mp")
    local_rows = latent.shape[0]
    tokens_all = CANVAS * CANVAS
    cap_at = FREQ + D
    block_at = FREQ + CAPD + 2 * D
    segment, text_segment = geometry(resolution, lengths)
    slot_ids = jnp.arange(4, dtype=jnp.int32)
    onehot = (segment[:, None] == slot_ids[None, :]).astype(jnp.float32)
    local_seg = lax.dynamic_slice_in_dim(segment, rank * local_rows, local_rows)
    local_hot = (local_seg[:, None] == slot_ids[None, :]).astype(jnp.float32)
    sigma = exact_dot(local_hot, widen(steps_t)[:, None] / TMAX)
    clean = widen(latent)
    noisy = widen(noise_c)
    mixed_in = (1.0 - sigma) * clean + sigma * noisy
    target = noisy - clean
    image_tokens = jnp.where(resolution == 0, (CANVAS // 2) ** 2, tokens_all).astype(jnp.float32)
    loss_weight = 1.0 / (CIN * image_tokens * count)
    freq_b = narrow(time_embed(steps_t))
    time_hidden = half_dot(freq_b, w_cond[:FREQ])
    hidden_b = narrow(jax.nn.silu(time_hidden))
    time_emb = half_dot(hidden_b, w_cond[FREQ : FREQ + D])
    silu_b = narrow(jax.nn.silu(time_emb))
    w_block = w_cond[block_at:]
    time_mod = jnp.einsum("id,kd->ik", silu_b, w_block, preferred_element_type=jnp.float32)
    cap_hidden = half_dot(caption, w_cond[cap_at : cap_at + CAPD])
    cap_act_b = narrow(gelu_tanh(cap_hidden))
    text_raw = half_dot(cap_act_b, w_cond[cap_at + CAPD : block_at])
    text_norm, rms_pull = jax.vjp(rms_norm, text_raw, tables[8])
    text_big = gather_rows(narrow(text_norm))
    text_kv = narrow(
        jnp.einsum("td,dke->tke", text_big, w_in[:, 4:6], preferred_element_type=jnp.float32)
    )
    mods, mods_pull = jax.vjp(partial(mod_table, local_hot), tables[0:6], time_mod)
    embed = exact_dot(mixed_in, tables[9 : 9 + CIN])
    normed_a, norm_a_pull = jax.vjp(modulate, embed, mods[:, 0], mods[:, 1])
    normed_big = gather_rows(narrow(normed_a))
    qkv_raw = jnp.einsum(
        "pd,dke->pke", normed_big, w_in[:, 0:3], preferred_element_type=jnp.float32
    )
    qkv_b = narrow(jax.nn.relu(qkv_raw))
    self_heads = qkv_b.shape[2] // HEAD_DIM
    qkv_f = widen(qkv_b).reshape(tokens_all, 3, self_heads, HEAD_DIM)
    attn_out, attn_pull = jax.vjp(
        partial(linear_attention, onehot), qkv_f[:, 0], qkv_f[:, 1], qkv_f[:, 2]
    )
    attn_b = narrow(attn_out.reshape(tokens_all, -1))
    branch_a = scatter_rows(half_dot(attn_b, w_out[0]))
    state_a = embed + mods[:, 2] * branch_a
    state_big = gather_rows(narrow(state_a))
    query_b = narrow(half_dot(state_big, w_in[:, 3]))
    cross_heads = query_b.shape[1] // XHEAD_DIM
    query_h = query_b.reshape(tokens_all, cross_heads, XHEAD_DIM)
    keys_h = text_kv[:, 0].reshape(TXT, cross_heads, XHEAD_DIM)
    values_h = text_kv[:, 1].reshape(TXT, cross_heads, XHEAD_DIM)
    match = segment[:, None] == text_segment[None, :]
    scores = cross_scores(query_h, keys_h, match)
    log_total = jax.nn.logsumexp(scores, axis=-1, keepdims=True)
    probs_b = narrow(jnp.exp(scores - log_total))
    cross_b = narrow(
        jnp.einsum("hpt,thd->phd", probs_b, values_h, preferred_element_type=jnp.float32).reshape(
            tokens_all, -1
        )
    )
    branch_c = scatter_rows(half_dot(cross_b, w_out[1]))
    state_c = state_a + branch_c
    normed_f, norm_f_pull = jax.vjp(modulate, state_c, mods[:, 3], mods[:, 4])
    normed_fbig = gather_rows(narrow(normed_f))
    upper = jnp.einsum("pd,dkf->pkf", normed_fbig, w_upper, preferred_element_type=jnp.float32)
    width_local = w_upper.shape[2]
    kernel_local = lax.dynamic_slice_in_dim(kernel, rank * width_local, width_local, 2)
    gated, gated_pull = jax.vjp(partial(conv_glu, segment), upper, kernel_local)
    gated_b = narrow(gated)
    branch_f = scatter_rows(half_dot(gated_b, w_lower))
    state_f = state_c + mods[:, 5] * branch_f
    loss_part, final_pull = jax.vjp(
        partial(final_loss, local_hot, target, loss_weight),
        state_f,
        tables[6:8],
        time_emb,
        tables[9 + CIN :],
    )
    return dict(
        loss=loss_part,
        final_pull=final_pull,
        mods=mods,
        mods_pull=mods_pull,
        branch_f=branch_f,
        gated_b=gated_b,
        gated_pull=gated_pull,
        normed_fbig=normed_fbig,
        norm_f_pull=norm_f_pull,
        cross_b=cross_b,
        query_h=query_h,
        keys_h=keys_h,
        values_h=values_h,
        match=match,
        log_total=log_total,
        probs_b=probs_b,
        state_big=state_big,
        text_big=text_big,
        branch_a=branch_a,
        attn_b=attn_b,
        attn_pull=attn_pull,
        qkv_raw=qkv_raw,
        normed_big=normed_big,
        norm_a_pull=norm_a_pull,
        mixed_in=mixed_in,
        rms_pull=rms_pull,
        silu_b=silu_b,
        time_emb=time_emb,
        freq_b=freq_b,
        width_local=width_local,
        time_hidden=time_hidden,
        hidden_b=hidden_b,
        cap_hidden=cap_hidden,
        cap_act_b=cap_act_b,
    )


def layer_backward(weights, kept, caption):
    w_in, w_out, w_upper, w_lower, w_cond, kernel, tables = weights
    rank = lax.axis_index("mp")
    tokens_all = CANVAS * CANVAS
    cap_at = FREQ + D
    block_at = FREQ + CAPD + 2 * D
    mods = kept["mods"]
    d_state_f, d_final_rows, d_time_final, d_out_rows = kept["final_pull"](
        jnp.ones((), jnp.float32)
    )
    d_gate_f = d_state_f * kept["branch_f"]
    d_branch_f = gather_rows(narrow(mods[:, 5] * d_state_f))
    g_lower = jnp.einsum(
        "pf,pd->fd", kept["gated_b"], d_branch_f, preferred_element_type=jnp.float32
    )
    d_gated = jnp.einsum("pd,fd->pf", d_branch_f, w_lower, preferred_element_type=jnp.float32)
    d_upper, d_kernel_local = kept["gated_pull"](d_gated)
    d_upper_b = narrow(d_upper)
    g_upper = jnp.einsum(
        "pd,pkf->dkf", kept["normed_fbig"], d_upper_b, preferred_element_type=jnp.float32
    )
    d_normed_f = scatter_rows(
        jnp.einsum("pkf,dkf->pd", d_upper_b, w_upper, preferred_element_type=jnp.float32)
    )
    d_state_c, d_shift_f, d_scale_f = kept["norm_f_pull"](d_normed_f)
    d_state_c = d_state_c + d_state_f
    d_branch_c = gather_rows(narrow(d_state_c))
    g_out_c = jnp.einsum(
        "pa,pd->ad", kept["cross_b"], d_branch_c, preferred_element_type=jnp.float32
    )
    query_h = kept["query_h"]
    keys_h = kept["keys_h"]
    values_h = kept["values_h"]
    d_cross = narrow(
        jnp.einsum("pd,ad->pa", d_branch_c, w_out[1], preferred_element_type=jnp.float32)
    ).reshape(query_h.shape)
    probs = jnp.exp(cross_scores(query_h, keys_h, kept["match"]) - kept["log_total"])
    d_probs = jnp.einsum("phd,thd->hpt", d_cross, values_h, preferred_element_type=jnp.float32)
    d_scores_b = narrow(probs * (d_probs - jnp.sum(probs * d_probs, -1, keepdims=True)))
    scale = XHEAD_DIM ** (-0.5)
    d_query = (
        jnp.einsum("hpt,thd->phd", d_scores_b, keys_h, preferred_element_type=jnp.float32) * scale
    )
    d_keys = (
        jnp.einsum("hpt,phd->thd", d_scores_b, query_h, preferred_element_type=jnp.float32) * scale
    )
    d_values = jnp.einsum(
        "hpt,phd->thd", kept["probs_b"], d_cross, preferred_element_type=jnp.float32
    )
    d_query_b = narrow(d_query.reshape(tokens_all, -1))
    d_kv_b = narrow(jnp.stack([d_keys.reshape(TXT, -1), d_values.reshape(TXT, -1)], axis=1))
    g_query = jnp.einsum(
        "pd,pa->da", kept["state_big"], d_query_b, preferred_element_type=jnp.float32
    )
    g_kv = jnp.einsum("td,tke->dke", kept["text_big"], d_kv_b, preferred_element_type=jnp.float32)
    d_state_a = d_state_c + scatter_rows(
        jnp.einsum("pa,da->pd", d_query_b, w_in[:, 3], preferred_element_type=jnp.float32)
    )
    d_text = scatter_rows(
        jnp.einsum("tke,dke->td", d_kv_b, w_in[:, 4:6], preferred_element_type=jnp.float32)
    )
    d_gate_a = d_state_a * kept["branch_a"]
    d_branch_a = gather_rows(narrow(mods[:, 2] * d_state_a))
    g_out_a = jnp.einsum(
        "pa,pd->ad", kept["attn_b"], d_branch_a, preferred_element_type=jnp.float32
    )
    d_attn = jnp.einsum(
        "pd,ad->pa", d_branch_a, w_out[0], preferred_element_type=jnp.float32
    ).reshape(tokens_all, -1, HEAD_DIM)
    d_qq, d_kk, d_vv = kept["attn_pull"](d_attn)
    d_qkv = jnp.stack([d_qq, d_kk, d_vv], axis=1).reshape(tokens_all, 3, -1)
    d_qkv_b = narrow(jnp.where(kept["qkv_raw"] > 0, d_qkv, 0.0))
    g_qkv = jnp.einsum(
        "pd,pke->dke", kept["normed_big"], d_qkv_b, preferred_element_type=jnp.float32
    )
    d_normed_a = scatter_rows(
        jnp.einsum("pke,dke->pd", d_qkv_b, w_in[:, 0:3], preferred_element_type=jnp.float32)
    )
    d_embed, d_shift_a, d_scale_a = kept["norm_a_pull"](d_normed_a)
    d_embed = d_embed + d_state_a
    g_patch = jnp.einsum("pc,pd->cd", kept["mixed_in"], d_embed, precision=HIGH)
    d_mods = jnp.stack([d_shift_a, d_scale_a, d_gate_a, d_shift_f, d_scale_f, d_gate_f], axis=1)
    d_rows_six, d_time_mod = kept["mods_pull"](d_mods)
    d_text_raw, d_gain = kept["rms_pull"](d_text)
    d_text_raw_b = narrow(d_text_raw)
    g_cap_second = jnp.einsum(
        "td,te->de", kept["cap_act_b"], d_text_raw_b, preferred_element_type=jnp.float32
    )
    d_cap_act = jnp.einsum(
        "te,de->td",
        d_text_raw_b,
        w_cond[cap_at + CAPD : block_at],
        preferred_element_type=jnp.float32,
    )
    _, gelu_pull = jax.vjp(gelu_tanh, kept["cap_hidden"])
    d_cap_hidden_b = narrow(gelu_pull(d_cap_act)[0])
    g_cap_first = jnp.einsum(
        "tc,td->cd", caption, d_cap_hidden_b, preferred_element_type=jnp.float32
    )
    g_block = jnp.einsum("ik,id->kd", d_time_mod, widen(kept["silu_b"]), precision=HIGH)
    d_silu = jnp.einsum("ik,kd->id", d_time_mod, widen(w_cond[block_at:]), precision=HIGH)
    _, silu_pull = jax.vjp(jax.nn.silu, kept["time_emb"])
    d_time = silu_pull(d_silu)[0] + d_time_final
    g_time_second = jnp.einsum("id,ie->de", widen(kept["hidden_b"]), d_time, precision=HIGH)
    d_hidden = jnp.einsum("ie,de->id", d_time, widen(w_cond[FREQ : FREQ + D]), precision=HIGH)
    _, hidden_pull = jax.vjp(jax.nn.silu, kept["time_hidden"])
    d_time_hidden = hidden_pull(d_hidden)[0]
    g_time_first = jnp.einsum("if,id->fd", widen(kept["freq_b"]), d_time_hidden, precision=HIGH)
    g_in = jnp.concatenate([g_qkv, g_query[:, None], g_kv], axis=1)
    g_out = jnp.stack([g_out_a, g_out_c])
    g_cond = jnp.concatenate(
        [g_time_first, g_time_second, g_cap_first, g_cap_second, g_block], axis=0
    )
    g_kernel = lax.dynamic_update_slice_in_dim(
        jnp.zeros(kernel.shape, jnp.float32), d_kernel_local, rank * kept["width_local"], 2
    )
    g_tables = jnp.concatenate(
        [d_rows_six, d_final_rows, d_gain[None], g_patch, d_out_rows], axis=0
    )
    return (g_in, g_out, g_upper, g_lower, g_cond, g_kernel, g_tables)


def fetch_weights(in_proj, out_proj, w_up, w_down, cond):
    layer = (
        lax.all_gather(narrow(in_proj), "dp", axis=0, tiled=True),
        lax.all_gather(narrow(out_proj), "dp", axis=2, tiled=True),
        lax.all_gather(narrow(w_up), "dp", axis=0, tiled=True),
        lax.all_gather(narrow(w_down), "dp", axis=1, tiled=True),
    )
    conds = lax.all_gather(narrow(cond), ("dp", "mp"), axis=0, tiled=True)
    return tuple(layer) + (conds,)


def reduce_grads(grads):
    layer = (
        lax.psum_scatter(grads[0], "dp", scatter_dimension=0, tiled=True),
        lax.psum_scatter(grads[1], "dp", scatter_dimension=2, tiled=True),
        lax.psum_scatter(grads[2], "dp", scatter_dimension=0, tiled=True),
        lax.psum_scatter(grads[3], "dp", scatter_dimension=1, tiled=True),
    )
    conds = lax.psum_scatter(grads[4], ("dp", "mp"), scatter_dimension=0, tiled=True)
    return tuple(layer) + (conds,)


def update(weight, grad, moment, average, factor, rate):
    clipped = factor * grad
    moment_new = MOMENTUM * moment + clipped
    weight_new = weight - rate * (clipped + MOMENTUM * moment_new)
    average_new = average + AVERAGE_RATE * (weight_new - average)
    return (weight_new, moment_new, average_new)


def local(
    latents,
    noise,
    captions,
    res_ids,
    timesteps,
    caption_lengths,
    in_proj,
    out_proj,
    w_up,
    w_down,
    cond,
    conv,
    tables,
    mom_in,
    mom_out,
    mom_up,
    mom_down,
    mom_cond,
    mom_conv,
    mom_tables,
    avg_in,
    avg_out,
    avg_up,
    avg_down,
    avg_cond,
    avg_conv,
    avg_tables,
):
    count = lax.psum(jnp.sum(jnp.where(res_ids == 0, 4.0, 1.0)), "dp")
    fetched = fetch_weights(in_proj, out_proj, w_up, w_down, cond)
    n_data = lax.axis_size("dp")
    n_every = lax.axis_size(("dp", "mp"))
    sums_init = (
        jnp.zeros((in_proj.shape[0] * n_data,) + in_proj.shape[1:], jnp.float32),
        jnp.zeros(out_proj.shape[:2] + (out_proj.shape[2] * n_data,), jnp.float32),
        jnp.zeros((w_up.shape[0] * n_data,) + w_up.shape[1:], jnp.float32),
        jnp.zeros((w_down.shape[0], w_down.shape[1] * n_data), jnp.float32),
        jnp.zeros((cond.shape[0] * n_every, cond.shape[1]), jnp.float32),
    )
    small_init = (jnp.zeros(conv.shape, jnp.float32), jnp.zeros(tables.shape, jnp.float32))

    def canvas_step(running, item):
        sums, small, loss_total = running
        latent, noise_c, caption, resolution, steps_t, lengths = item
        weights = fetched + (conv, tables)
        kept = layer_forward(weights, latent, noise_c, caption, resolution, steps_t, lengths, count)
        grads = layer_backward(weights, kept, caption)
        portion = grads[:5]
        sums = tuple((old + new for old, new in zip(sums, portion)))
        small = (small[0] + grads[5], small[1] + grads[6])
        return ((sums, small, loss_total + kept["loss"]), None)

    (sums, small, loss_total), _ = lax.scan(
        canvas_step,
        (sums_init, small_init, jnp.zeros((), jnp.float32)),
        (latents, noise, captions, res_ids, timesteps, caption_lengths),
    )
    owned = reduce_grads(sums)
    owned_sq = sum((jnp.sum(grad * grad) for grad in owned))
    conv_grad, tables_grad, squares, loss = lax.psum(
        (small[0], small[1], owned_sq, loss_total), ("dp", "mp")
    )
    norm = jnp.sqrt(squares + jnp.sum(conv_grad * conv_grad) + jnp.sum(tables_grad * tables_grad))
    factor = CLIP / jnp.maximum(norm, CLIP)
    rate = STEP_SCALE * math.sqrt(PARAMS) / CLIP
    grads_all = tuple(owned) + (conv_grad, tables_grad)
    weights_all = (in_proj, out_proj, w_up, w_down, cond, conv, tables)
    moments = (mom_in, mom_out, mom_up, mom_down, mom_cond, mom_conv, mom_tables)
    averages = (avg_in, avg_out, avg_up, avg_down, avg_cond, avg_conv, avg_tables)
    new_sets = [
        update(weights_all[index], grads_all[index], moments[index], averages[index], factor, rate)
        for index in range(7)
    ]
    clipped_conv = factor * conv_grad
    return (
        loss,
        norm,
        new_sets[0][0],
        new_sets[1][0],
        new_sets[2][0],
        new_sets[3][0],
        new_sets[4][0],
        new_sets[5][0],
        new_sets[6][0],
        new_sets[0][1],
        new_sets[1][1],
        new_sets[2][1],
        new_sets[3][1],
        new_sets[4][1],
        clipped_conv,
        new_sets[6][1],
        new_sets[0][2],
        new_sets[1][2],
        new_sets[2][2],
        new_sets[3][2],
        new_sets[4][2],
        new_sets[5][2],
        new_sets[6][2],
    )


def solution(mesh):
    in_specs = (
        P("dp", "mp", None),
        P("dp", "mp", None),
        P("dp", "mp", None),
        P("dp"),
        P("dp", None),
        P("dp", None),
        P("dp", None, "mp"),
        P(None, "mp", "dp"),
        P("dp", None, "mp"),
        P("mp", "dp"),
        P(("dp", "mp"), None),
        P(),
        P(),
        P("dp", None, "mp"),
        P(None, "mp", "dp"),
        P("dp", None, "mp"),
        P("mp", "dp"),
        P(("dp", "mp"), None),
        P(),
        P(),
        P("dp", None, "mp"),
        P(None, "mp", "dp"),
        P("dp", None, "mp"),
        P("mp", "dp"),
        P(("dp", "mp"), None),
        P(),
        P(),
    )
    out_specs = (
        P(),
        P(),
        P("dp", None, "mp"),
        P(None, "mp", "dp"),
        P("dp", None, "mp"),
        P("mp", "dp"),
        P(("dp", "mp"), None),
        P(),
        P(),
        P("dp", None, "mp"),
        P(None, "mp", "dp"),
        P("dp", None, "mp"),
        P("mp", "dp"),
        P(("dp", "mp"), None),
        P(),
        P(),
        P("dp", None, "mp"),
        P(None, "mp", "dp"),
        P("dp", None, "mp"),
        P("mp", "dp"),
        P(("dp", "mp"), None),
        P(),
        P(),
    )
    return jax.shard_map(local, mesh=mesh, in_specs=in_specs, out_specs=out_specs, check_vma=False)
```

profile of v0, /device:TPU:28, one launch (start us, length us, event | category | flops | bytes accessed | tf_op | source)
XLA Modules:
  0.0 3473.3 jit_solution(5565730024323909248)
XLA Ops:
  62.3 42.1 %all-gather.21.cloned.1.call-done = bf16[720,1152]{0,1:T(8,128)(2,1)} async-done(((bf16[720,144]{0,1:T(8,128)(2,1)}), bf16[720,1152]{0,1:T(8,128)(2,1)}) %all-gather.21.cloned.1.call-update) | async-done | bytes 1658896 | tf_op jit(solution)/shard_map/all_gather | solution.py:389
  108.3 62.7 %all-gather.19.cloned.1.call-done = bf16[1152,2,720]{2,1,0:T(2,128)(2,1)} async-done(((bf16[144,2,720]{2,1,0:T(2,128)(2,1)}), bf16[1152,2,720]{2,1,0:T(2,128)(2,1)}) %all-gather.19.cloned.1.call-update) | async-done | bytes 3317776 | tf_op jit(solution)/shard_map/all_gather | solution.py:388
  181.3 77.5 %all-gather.15.cloned.1.call-done = bf16[1152,6,288]{2,0,1:T(8,128)(2,1)} async-done(((bf16[144,6,288]{2,0,1:T(8,128)(2,1)}), bf16[1152,6,288]{2,0,1:T(8,128)(2,1)}) %all-gather.15.cloned.1.call-update) | async-done | bytes 3981328 | tf_op jit(solution)/shard_map/all_gather | solution.py:386
  265.5 158.9 %all-gather.13.cloned.1.call-done = bf16[11776,1152]{1,0:T(8,128)(2,1)} async-done(((bf16[368,1152]{1,0:T(8,128)(2,1)}), bf16[11776,1152]{1,0:T(8,128)(2,1)}) %all-gather.13.cloned.1.call-update) | async-done | bytes 27131920 | tf_op jit(solution)/shard_map/all_gather | solution.py:391
  425.2 1789.8 %while.28 = (s32[]{:T(128)}, f32[1152,6,288]{0,2,1:T(8,128)}, f32[2,288,1152]{2,1,0:T(8,128)}, f32[1152,2,720]{0,2,1:T(8,128)}, f32[720,1152]{1,0:T(8,128)}, /*i...) while((s32[]{:T(128)}, f32[1152,6,288]{0,2,1:T(8,128)}, ...), condition=%wide.region_45.46_spmd.clone, body=%wide.region_2.45_spmd.clone.sunk | while | flops 38608674816 | bytes 1673904512 | solution.py:467
  515.5 39.2 %reduce-scatter.22.cloned.1.call-done = f32[256,1152]{1,0:T(8,128)} async-done(((f32[1024,1152]{1,0:T(8,128)}), f32[256,1152]{1,0:T(8,128)}) %reduce-scatter.22.cloned.1.call-update) | async-done | bytes 1179664 | tf_op jit(solution)/shard_map/while/body/eval_jaxpr/reduce_scatter | solution.py:51
  615.3 48.0 %reduce-scatter.24.cloned.1.call-done = f32[256,1152]{1,0:T(8,128)} async-done(((f32[1024,1152]{1,0:T(8,128)}), f32[256,1152]{1,0:T(8,128)}) %reduce-scatter.24.cloned.1.call-update) | async-done | bytes 1179664 | tf_op jit(solution)/shard_map/while/body/eval_jaxpr/reduce_scatter | solution.py:51
  758.8 43.9 %reduce-scatter.26.cloned.1.call-done = f32[256,1152]{1,0:T(8,128)} async-done(((f32[1024,1152]{1,0:T(8,128)}), f32[256,1152]{1,0:T(8,128)}) %reduce-scatter.26.cloned.1.call-update) | async-done | bytes 1179664 | tf_op jit(solution)/shard_map/while/body/eval_jaxpr/reduce_scatter | solution.py:51
  920.4 47.9 %reduce-scatter.28.cloned.1.call-done = f32[256,1152]{1,0:T(8,128)} async-done(((f32[1024,1152]{1,0:T(8,128)}), f32[256,1152]{1,0:T(8,128)}) %reduce-scatter.28.cloned.1.call-update) | async-done | bytes 1179664 | tf_op jit(solution)/shard_map/while/body/eval_jaxpr/reduce_scatter | solution.py:51
  1017.1 47.9 %reduce-scatter.30.cloned.1.call-done = f32[256,1152]{1,0:T(8,128)} async-done(((f32[1024,1152]{1,0:T(8,128)}), f32[256,1152]{1,0:T(8,128)}) %reduce-scatter.30.cloned.1.call-update) | async-done | bytes 1179664 | tf_op jit(solution)/shard_map/while/body/eval_jaxpr/reduce_scatter | solution.py:51
  1269.5 35.3 %select_add_fusion.7 = f32[11776,1152]{1,0:T(8,128)} fusion(f32[11776,1152]{1,0:T(8,128)} %convolution_dynamic-update-slice_fusion.14, f32[11776,1152]{1,0:T(8,128)} %get-tuple-element.1033, pred[]{:T(512)S(6)} %compare.88), kind=kLoop, calls=%fused_computation.clone.1 | loop fusion | flops 27131904 | bytes 162791424 | tf_op jit(solution)/shard_map/while/body/eval_jaxpr/add | solution.py:463
  1395.9 39.2 %reduce-scatter.22.cloned.1.call-done = f32[256,1152]{1,0:T(8,128)} async-done(((f32[1024,1152]{1,0:T(8,128)}), f32[256,1152]{1,0:T(8,128)}) %reduce-scatter.22.cloned.1.call-update) | async-done | bytes 1179664 | tf_op jit(solution)/shard_map/while/body/eval_jaxpr/reduce_scatter | solution.py:51
  1495.6 48.0 %reduce-scatter.24.cloned.1.call-done = f32[256,1152]{1,0:T(8,128)} async-done(((f32[1024,1152]{1,0:T(8,128)}), f32[256,1152]{1,0:T(8,128)}) %reduce-scatter.24.cloned.1.call-update) | async-done | bytes 1179664 | tf_op jit(solution)/shard_map/while/body/eval_jaxpr/reduce_scatter | solution.py:51
  1639.1 43.9 %reduce-scatter.26.cloned.1.call-done = f32[256,1152]{1,0:T(8,128)} async-done(((f32[1024,1152]{1,0:T(8,128)}), f32[256,1152]{1,0:T(8,128)}) %reduce-scatter.26.cloned.1.call-update) | async-done | bytes 1179664 | tf_op jit(solution)/shard_map/while/body/eval_jaxpr/reduce_scatter | solution.py:51
  1800.7 48.0 %reduce-scatter.28.cloned.1.call-done = f32[256,1152]{1,0:T(8,128)} async-done(((f32[1024,1152]{1,0:T(8,128)}), f32[256,1152]{1,0:T(8,128)}) %reduce-scatter.28.cloned.1.call-update) | async-done | bytes 1179664 | tf_op jit(solution)/shard_map/while/body/eval_jaxpr/reduce_scatter | solution.py:51
  1897.4 47.9 %reduce-scatter.30.cloned.1.call-done = f32[256,1152]{1,0:T(8,128)} async-done(((f32[1024,1152]{1,0:T(8,128)}), f32[256,1152]{1,0:T(8,128)}) %reduce-scatter.30.cloned.1.call-update) | async-done | bytes 1179664 | tf_op jit(solution)/shard_map/while/body/eval_jaxpr/reduce_scatter | solution.py:51
  2155.4 52.7 %select_add_fusion.7 = f32[11776,1152]{1,0:T(8,128)} fusion(f32[11776,1152]{1,0:T(8,128)} %convolution_dynamic-update-slice_fusion.14, f32[11776,1152]{1,0:T(8,128)} %get-tuple-element.1033, pred[]{:T(512)S(6)} %compare.88), kind=kLoop, calls=%fused_computation.clone.1 | loop fusion | flops 27131904 | bytes 162791424 | tf_op jit(solution)/shard_map/while/body/eval_jaxpr/add | solution.py:463
  2248.5 102.3 %all-reduce.34.cloned.1.call-done = (f32[2,10,2880]{2,0,1:T(2,128)}, f32[73,1152]{1,0:T(8,128)}) async-done(((f32[2,10,2880]{2,0,1:T(2,128)}, f32[73,1152]{1,0:T(8,128)}), (f32[2,10,2880]{2,0,1:T(2,128)}, f32[73,1152]{1,0:T(8,128)})) %all-reduce.34.cloned.1.call-update) | async-done | bytes 566800 | tf_op jit(solution)/shard_map/psum | solution.py:474
  2354.3 78.3 %reduce-scatter.16.cloned.1.call-done = f32[2,288,144]{1,2,0:T(8,128)} async-done(((f32[2,288,1152]{1,2,0:T(8,128)}), f32[2,288,144]{1,2,0:T(8,128)}) %reduce-scatter.16.cloned.1.call-update) | async-done | bytes 331792 | tf_op jit(solution)/shard_map/reduce_scatter | solution.py:398
  2434.3 235.3 %all-reduce.32.cloned.1.call-done = f32[1152,2,720]{2,1,0:T(2,128)} async-done(((f32[1152,2,720]{2,1,0:T(2,128)}), f32[1152,2,720]{2,1,0:T(2,128)}) %all-reduce.32.cloned.1.call-update) | async-done | bytes 6635536
  2672.3 79.6 %reduce-scatter.18.cloned.1.call-done = f32[720,144]{0,1:T(8,128)} async-done(((f32[720,1152]{0,1:T(8,128)}), f32[720,144]{0,1:T(8,128)}) %reduce-scatter.18.cloned.1.call-update) | async-done | bytes 414736 | tf_op jit(solution)/shard_map/reduce_scatter | solution.py:400
  2753.6 180.9 %reduce-scatter.14.cloned.1.call-done = f32[144,6,288]{2,0,1:T(8,128)} async-done(((f32[1152,6,288]{2,0,1:T(8,128)}), f32[144,6,288]{2,0,1:T(8,128)}) %reduce-scatter.14.cloned.1.call-update) | async-done | bytes 995344 | tf_op jit(solution)/shard_map/reduce_scatter | solution.py:397
  2939.4 458.7 %reduce-scatter.20.cloned.1.call-done = f32[368,1152]{1,0:T(8,128)} async-done(((f32[11776,1152]{1,0:T(8,128)}), f32[368,1152]{1,0:T(8,128)}) %reduce-scatter.20.cloned.1.call-update) | async-done | bytes 1695760
  3401.2 42.0 %all-reduce.27 = (f32[]{:T(128)}, f32[]{:T(128)}) all-reduce(f32[]{:T(128)} %get-tuple-element.1363, f32[]{:T(128)S(6)} %add.731), channel_id=1, replica_groups=mesh['dp'=8,'mp'=4] {'dp','mp'}, use_global_device_ids=true, to_apply=%region_46.47 | all-reduce | flops 2 | bytes 16 | tf_op jit(solution)/shard_map/psum | solution.py:474
  (1162 shorter events, 1375.3 us)
Async XLA Ops:
  9.4 95.1 %all-gather.21.cloned.1.call-start = ((), (), s32[]{:S(2)}) async-start(), calls=%async_computation.15 | async-start | bytes 1990656 | tf_op jit(solution)/shard_map/all_gather | solution.py:389
  11.2 159.8 %all-gather.19.cloned.1.call-start = ((), (), s32[]{:S(2)}) async-start(), calls=%async_computation.14 | async-start | bytes 3981312 | tf_op jit(solution)/shard_map/all_gather | solution.py:388
  13.5 245.4 %all-gather.15.cloned.1.call-start = ((), (), s32[]{:S(2)}) async-start(), calls=%async_computation.12 | async-start | bytes 5971968 | tf_op jit(solution)/shard_map/all_gather | solution.py:386
  14.5 409.9 %all-gather.13.cloned.1.call-start = ((), (), s32[]{:S(2)}) async-start(), calls=%async_computation.11 | async-start | bytes 27979776 | tf_op jit(solution)/shard_map/all_gather | solution.py:391
  463.8 90.9 %reduce-scatter.22.cloned.1.call-start = ((), (), s32[]{:S(2)}) async-start(), calls=%async_computation.24 | async-start | bytes 5898240 | tf_op jit(solution)/shard_map/while/body/eval_jaxpr/reduce_scatter | solution.py:51
  557.3 105.9 %reduce-scatter.24.cloned.1.call-start = ((), (), s32[]{:S(2)}) async-start(), calls=%async_computation.26 | async-start | bytes 5898240 | tf_op jit(solution)/shard_map/while/body/eval_jaxpr/reduce_scatter | solution.py:51
  668.2 134.4 %reduce-scatter.26.cloned.1.call-start = ((), (), s32[]{:S(2)}) async-start(), calls=%async_computation.28 | async-start | bytes 5898240 | tf_op jit(solution)/shard_map/while/body/eval_jaxpr/reduce_scatter | solution.py:51
  814.6 153.7 %reduce-scatter.28.cloned.1.call-start = ((), (), s32[]{:S(2)}) async-start(), calls=%async_computation.30 | async-start | bytes 5898240 | tf_op jit(solution)/shard_map/while/body/eval_jaxpr/reduce_scatter | solution.py:51
  974.4 90.7 %reduce-scatter.30.cloned.1.call-start = ((), (), s32[]{:S(2)}) async-start(), calls=%async_computation.32 | async-start | bytes 5898240 | tf_op jit(solution)/shard_map/while/body/eval_jaxpr/reduce_scatter | solution.py:51
  1068.6 101.7 %reduce-scatter.34.cloned.1.call-start = ((), (), s32[]{:S(2)}) async-start(), calls=%async_computation.35 | async-start | bytes 2949120 | tf_op jit(solution)/shard_map/while/body/eval_jaxpr/reduce_scatter | solution.py:51
  1082.2 104.7 %reduce-scatter.32.cloned.1.call-start = ((), (), s32[]{:S(2)}) async-start(), calls=%async_computation.34 | async-start | bytes 5898240 | tf_op jit(solution)/shard_map/while/body/eval_jaxpr/reduce_scatter | solution.py:51
  1343.3 91.7 %reduce-scatter.22.cloned.1.call-start = ((), (), s32[]{:S(2)}) async-start(), calls=%async_computation.24 | async-start | bytes 5898240 | tf_op jit(solution)/shard_map/while/body/eval_jaxpr/reduce_scatter | solution.py:51
  1437.7 105.9 %reduce-scatter.24.cloned.1.call-start = ((), (), s32[]{:S(2)}) async-start(), calls=%async_computation.26 | async-start | bytes 5898240 | tf_op jit(solution)/shard_map/while/body/eval_jaxpr/reduce_scatter | solution.py:51
  1548.6 134.4 %reduce-scatter.26.cloned.1.call-start = ((), (), s32[]{:S(2)}) async-start(), calls=%async_computation.28 | async-start | bytes 5898240 | tf_op jit(solution)/shard_map/while/body/eval_jaxpr/reduce_scatter | solution.py:51
  1694.9 153.8 %reduce-scatter.28.cloned.1.call-start = ((), (), s32[]{:S(2)}) async-start(), calls=%async_computation.30 | async-start | bytes 5898240 | tf_op jit(solution)/shard_map/while/body/eval_jaxpr/reduce_scatter | solution.py:51
  1854.7 90.7 %reduce-scatter.30.cloned.1.call-start = ((), (), s32[]{:S(2)}) async-start(), calls=%async_computation.32 | async-start | bytes 5898240 | tf_op jit(solution)/shard_map/while/body/eval_jaxpr/reduce_scatter | solution.py:51
  1948.9 104.8 %reduce-scatter.34.cloned.1.call-start = ((), (), s32[]{:S(2)}) async-start(), calls=%async_computation.35 | async-start | bytes 2949120 | tf_op jit(solution)/shard_map/while/body/eval_jaxpr/reduce_scatter | solution.py:51
  1962.5 110.3 %reduce-scatter.32.cloned.1.call-start = ((), (), s32[]{:S(2)}) async-start(), calls=%async_computation.34 | async-start | bytes 5898240 | tf_op jit(solution)/shard_map/while/body/eval_jaxpr/reduce_scatter | solution.py:51
  2214.9 135.8 %all-reduce.34.cloned.1.call-start = ((), (), s32[]{:S(2)}) async-start(), calls=%async_computation.21 | async-start | bytes 1208320 | tf_op jit(solution)/shard_map/psum | solution.py:474
  2215.7 216.9 %reduce-scatter.16.cloned.1.call-start = ((), (), s32[]{:S(2)}) async-start(), calls=%async_computation.17 | async-start | bytes 3981312 | tf_op jit(solution)/shard_map/reduce_scatter | solution.py:398
  2219.4 450.2 %all-reduce.32.cloned.1.call-start = ((), (), s32[]{:S(2)}) async-start(), calls=%async_computation.19 | async-start | bytes 14155776
  2231.7 520.2 %reduce-scatter.18.cloned.1.call-start = ((), (), s32[]{:S(2)}) async-start(), calls=%async_computation.18 | async-start | bytes 3981312 | tf_op jit(solution)/shard_map/reduce_scatter | solution.py:400
  2236.9 697.6 %reduce-scatter.14.cloned.1.call-start = ((), (), s32[]{:S(2)}) async-start(), calls=%async_computation.16 | async-start | bytes 11943936 | tf_op jit(solution)/shard_map/reduce_scatter | solution.py:397
  2246.5 1151.5 %reduce-scatter.20.cloned.1.call-start = ((), (), s32[]{:S(2)}) async-start(), calls=%async_computation.20 | async-start | bytes 55959552
  (361 other events, 15335.1 us)
Sparse Core Ops, SparseCore 0:
  10.8 45.9 all-gather.16
  59.5 44.9 all-gather.20
  107.2 63.6 all-gather.18
  173.6 85.2 all-gather.14
  262.2 162.1 all-gather.12
  506.8 47.8 reduce-scatter.21
  615.3 47.8 reduce-scatter.23
  754.8 47.8 reduce-scatter.25
  920.5 47.8 reduce-scatter.27
  1017.2 47.8 reduce-scatter.29
  1095.2 33.0 reduce-scatter.33
  1131.0 47.8 reduce-scatter.31
  1387.2 47.8 reduce-scatter.21
  1495.7 47.8 reduce-scatter.23
  1635.1 47.8 reduce-scatter.25
  1800.8 47.8 reduce-scatter.27
  1897.5 47.8 reduce-scatter.29
  2011.3 47.8 reduce-scatter.31
  2221.7 128.9 all-reduce.33
  2354.8 77.7 reduce-scatter.15
  2436.7 232.8 all-reduce.31
  2673.1 78.7 reduce-scatter.17
  2755.5 178.9 reduce-scatter.13
  2941.9 456.0 reduce-scatter.19
  (15 shorter events, 355.2 us)
where the time goes:
time: 3480 us; the launch traced here: 3470 us
  waiting for transfers between devices  2230 us (64%)
  other arithmetic  464 us (13%)
  matrix products  453 us (13%)
  local copies, waits for them, and re-layouts  221 us (6%)
  blocking collectives  59.5 us (2%)
    unnamed x13, waiting for transfers between devices  695 us
    reduce_scatter x14, waiting for transfers between devices, scatter_rows(): return lax.psum_scatter(value, 'mp', scatter_dimension=0, tiled=True)  454 us
    all_gather x14, waiting for transfers between devices, gather_rows(): return lax.all_gather(value, 'mp', axis=0, tiled=True)  278 us
    reduce_scatter x1, waiting for transfers between devices, reduce_grads(): lax.psum_scatter(grads[0], 'dp', scatter_dimension=0, tiled=True)  181 us
    all_gather x1, waiting for transfers between devices, fetch_weights(): conds = lax.all_gather(narrow(cond), ('dp', 'mp'), axis=0, tiled=True)  159 us
    psum x1, waiting for transfers between devices, local(): lax.psum((small[0], small[1], owned_sq, loss_total), ('dp', 'mp'))  102 us
    add x6, other arithmetic, canvas_step(): sums = tuple((old + new for old, new in zip(sums, portion)))  99.9 us
    reduce_scatter x1, waiting for transfers between devices, reduce_grads(): lax.psum_scatter(grads[3], 'dp', scatter_dimension=1, tiled=True)  79.6 us
  transfers between devices with their start and end apart: 39, of which 35 were waited for; matrix products, arithmetic and copies ran while one was open for 10% of the time, Pallas kernels for 0%

commit v1 on v0

v1 whole, which is shorter than its diff:
```python
from functools import partial
import math

import jax
import jax.numpy as jnp
from jax import lax
from jax.experimental import pallas as pl
from jax.experimental.pallas import tpu as pltpu
from jax.sharding import PartitionSpec as P

D = 1152
FF = 2880
CAPD = 2304
CIN = 32
FREQ = 256
SIDE = 32
TXT = 512
HEAD = 32
XHEAD = 72
XHEADS = 16
PARAMS = 34277760
FFB = 768
FFP = 4 * FFB
TIME_ROWS = FREQ + D
CAP_ROWS = CAPD + D
BLOCK_AT = TIME_ROWS + CAP_ROWS

HIGH = lax.Precision.HIGHEST
EPS = 1e-06
CLIP = 0.001
MOMENTUM = 0.9
AVERAGE_RATE = 0.1
STEP_SCALE = 0.01
TMAX = 1000.0
MASKED = -1e30
AXES = ("dp", "mp")
F32 = jnp.float32
BF16 = jnp.bfloat16


def bf(value):
    return value.astype(BF16)


def wide(value):
    return value.astype(F32)


def dot(left, right, dims, precision=None):
    return lax.dot_general(
        left, right, (dims, ((), ())), precision=precision, preferred_element_type=F32
    )


def mm(left, right, precision=None):
    return dot(left, right, ((1,), (0,)), precision)


def mm_nt(left, right, precision=None):
    return dot(left, right, ((1,), (1,)), precision)


def mm_tn(left, right, precision=None):
    return dot(left, right, ((0,), (0,)), precision)


class Place:
    def __init__(self, n_dp, n_mp):
        self.n_dp, self.n_mp, self.n = n_dp, n_mp, n_dp * n_mp
        self.dp, self.mp = lax.axis_index("dp"), lax.axis_index("mp")
        self.me = self.dp * n_mp + self.mp
        self.y, self.c = self.mp // 2, self.mp % 2
        self.dp_bits = int(math.log2(n_dp))

    def bit(self, mask):
        return (self.me // mask) % 2

    def swap(self, value, mask):
        return lax.ppermute(value, AXES, [(i, i ^ mask) for i in range(self.n)])

    @property
    def far_masks(self):
        return [self.n_mp << b for b in range(1, self.dp_bits)]

    @property
    def x_mask(self):
        return self.n_mp


def ordered(bit, mine, theirs, axis):
    low = jnp.where(bit == 0, mine, theirs)
    high = jnp.where(bit == 0, theirs, mine)
    return jnp.concatenate([low, high], axis=axis)


def gather_far(place, block, axis):
    block = jnp.expand_dims(block, axis)
    for mask in place.far_masks:
        block = ordered(place.bit(mask), block, place.swap(block, mask), axis)
    return block


def gather_near(place, block, order):
    held = {0: block}
    for mask in order:
        held.update({key | mask: place.swap(value, mask) for key, value in held.items()})
    return held


def near_bits(place, key):
    flip = [1 if key & mask else 0 for mask in (place.x_mask, 2, 1)]
    own = (place.bit(place.x_mask), place.y, place.c)
    return [jnp.where(f == 1, 1 - o, o) for f, o in zip(flip, own)]


def gather_rows_all(place, block, order):
    rows, cols = block.shape
    held = gather_near(place, gather_far(place, block, 0), order)
    half = place.n_dp // 2
    out = jnp.zeros((half, 2, 2, 2, rows, cols), block.dtype)
    for key, value in held.items():
        x, y, c = near_bits(place, key)
        out = lax.dynamic_update_slice(out, value[:, None, None, None], (0, x, y, c, 0, 0))
    return out.reshape(place.n * rows, cols)


def spread_table(place, owner_rows, low, chunk):
    rounds = -(-owner_rows // chunk) + 1
    tables = []
    for step in range(rounds):
        pairs = []
        for owner in range(place.n):
            target = (owner_rows * owner - low) // chunk + step
            start = low + chunk * target - owner_rows * owner
            if 0 <= target < place.n and -chunk < start < owner_rows:
                pairs.append((owner, target))
        tables.append(pairs)
    return tables


def chunk_of(place, rows):
    chunk = -(-rows // place.n)
    return -(-chunk // 8) * 8


def spread_rows(place, held, low, rows):
    owner_rows = held.shape[0]
    chunk = chunk_of(place, rows)
    padded = jnp.pad(held, ((chunk, chunk), (0, 0)))
    first = (owner_rows * place.me - low) // chunk
    total = None
    for step, pairs in enumerate(spread_table(place, owner_rows, low, chunk)):
        start = low + chunk * (first + step) - owner_rows * place.me + chunk
        piece = lax.dynamic_slice_in_dim(padded, start, chunk, 0)
        got = lax.ppermute(piece, AXES, pairs)
        total = got if total is None else total + got
    return total


def collect_rows(place, block, owner_rows, low, rows):
    chunk = block.shape[0]
    first = (owner_rows * place.me - low) // chunk
    got = [
        lax.ppermute(block, AXES, [(target, owner) for owner, target in pairs])
        for pairs in spread_table(place, owner_rows, low, chunk)
    ]
    start = owner_rows * place.me - low - chunk * first
    mine = lax.dynamic_slice_in_dim(jnp.concatenate(got, axis=0), start, owner_rows, 0)
    row = owner_rows * place.me + jnp.arange(owner_rows, dtype=jnp.int32)[:, None]
    return jnp.where((row >= low) & (row < low + rows), mine, 0.0)


def halve(place, grad, stages):
    for axis, mask in stages:
        bit = place.bit(mask)
        half = grad.shape[axis] // 2
        away = lax.dynamic_slice_in_dim(grad, (1 - bit) * half, half, axis)
        keep = lax.dynamic_slice_in_dim(grad, bit * half, half, axis)
        grad = keep + wide(place.swap(bf(away), mask))
    return grad


def layer_norm(value):
    centred = value - jnp.mean(value, -1, keepdims=True)
    inverse = lax.rsqrt(jnp.mean(centred * centred, -1, keepdims=True) + EPS)
    return centred * inverse, inverse


def layer_norm_back(grad, normed, inverse):
    along = jnp.mean(grad * normed, -1, keepdims=True)
    return inverse * (grad - jnp.mean(grad, -1, keepdims=True) - normed * along)


def silu_grad(value):
    gate = jax.nn.sigmoid(value)
    return gate * (1.0 + value * (1.0 - gate))


def time_embed(steps_t):
    half_size = FREQ // 2
    freqs = jnp.exp(-math.log(10000.0) * jnp.arange(half_size, dtype=F32) / half_size)
    angles = wide(steps_t)[:, None] * freqs[None, :]
    return jnp.concatenate([jnp.cos(angles), jnp.sin(angles)], axis=1)


def to_ff(value):
    blocks = value.reshape(value.shape[:-1] + (4, FF // 4))
    pad = [(0, 0)] * (blocks.ndim - 1) + [(0, FFB - FF // 4)]
    blocks = jnp.pad(blocks, pad)
    blocks = jnp.stack([blocks[..., m, :] for m in (0, 2, 1, 3)], axis=-2)
    return blocks.reshape(value.shape[:-1] + (FFP,))


def from_ff(value):
    blocks = value.reshape(value.shape[:-1] + (4, FFB))[..., : FF // 4]
    blocks = jnp.stack([blocks[..., m, :] for m in (0, 2, 1, 3)], axis=-2)
    return blocks.reshape(value.shape[:-1] + (FF,))


def unit_split(place, units):
    units = units.reshape((2, 4) + units.shape[1:])

    def part(number):
        return lax.dynamic_index_in_dim(units, number, 1, False)

    got = [part(place.mp)] + [place.swap(part(place.mp ^ m), m) for m in (1, 2, 3)]
    stacked = jnp.stack(got)
    return jnp.concatenate(
        [lax.dynamic_index_in_dim(stacked, place.mp ^ m, 0, False) for m in range(4)], axis=-1
    )


def unit_join(place, block):
    cols = D // 4

    def part(number):
        return lax.dynamic_slice_in_dim(block, number * cols, cols, 2)

    got = [part(place.mp)] + [place.swap(part(place.mp ^ m), m) for m in (1, 2, 3)]
    stacked = jnp.stack(got)
    order = [lax.dynamic_index_in_dim(stacked, place.mp ^ m, 0, False) for m in range(4)]
    return jnp.stack(order, axis=1).reshape((8,) + order[0].shape[1:])


def as_units(in_w, out_w):
    inp = [in_w[:, k] for k in range(6)]
    outp = [out_w[j].T for j in range(2)]
    return jnp.stack([inp[0], inp[1], inp[2], outp[0], inp[3], outp[1], inp[4], inp[5]])


def from_units(units):
    g_in = jnp.stack([units[u] for u in (0, 1, 2, 4, 6, 7)], axis=1)
    g_out = jnp.stack([units[3].T, units[5].T])
    return g_in, g_out


class Flow:
    def __init__(self, place, sends, stages):
        self.place, self.stages = place, list(stages)
        self.keep = None
        self.moving = place.swap(sends, 1)
        self.sends = None

    def launch(self):
        self.moving = self.place.swap(self.sends, self.mask)
        self.sends = None

    def land(self):
        total = self.keep + wide(self.moving)
        self.moving = None
        if not self.stages:
            self.keep = total
            return
        kind, axis, self.mask = self.stages.pop(0)
        if kind == "rel":
            away = lax.slice_in_dim(total, 1, 2, axis=axis)
            self.keep = lax.slice_in_dim(total, 0, 1, axis=axis)
        else:
            bit = self.place.bit(self.mask)
            away = lax.dynamic_slice_in_dim(total, 1 - bit, 1, axis)
            self.keep = lax.dynamic_slice_in_dim(total, bit, 1, axis)
        self.sends = bf(away)

    def drain(self):
        while self.moving is not None:
            self.land()
            if self.sends is not None:
                self.launch()
        return self.keep


def tick(value, flows):
    moving = [flow for flow in flows if flow.moving is not None]
    value, landed = lax.optimization_barrier((value, [flow.moving for flow in moving]))
    for flow, arrived in zip(moving, landed):
        flow.moving = arrived
        flow.land()
    ready = [flow for flow in moving if flow.sends is not None]
    value, sends = lax.optimization_barrier((value, [flow.sends for flow in ready]))
    for flow, out in zip(ready, sends):
        flow.sends = out
        flow.launch()
    return value


CB = 256
ROW = SIDE
LIMIT = 48 * 1024 * 1024


def whole_spec(shape):
    return pl.BlockSpec(shape, lambda *_: (0,) * len(shape))


def ffn_forward_kernel(
    x_ref, w0_ref, w1_ref, wd_ref, taps_ref, left_ref, right_ref, on_ref,
    u_ref, z_ref, g_ref, out_ref, act, act_l, act_r
):
    rows = g_ref.shape[0] // ROW
    zero = jnp.zeros((ROW, CB), F32)
    x = x_ref[...]
    u_ref[0] = mm(x, w0_ref[...].reshape(D, CB))
    u_ref[1] = mm(x, w1_ref[...].reshape(D, CB))
    on = on_ref[0, 0]
    for k in range(2):
        for ref in (act, act_l, act_r):
            ref[k, pl.ds(0, ROW)] = zero

    def fill(r, scale):
        for k in range(2):
            u = u_ref[k, pl.ds(pl.multiple_of(r * ROW, ROW), ROW)]
            a = u * jax.nn.sigmoid(u) * scale
            at = pl.ds(pl.multiple_of(r * ROW + ROW, ROW), ROW)
            act[k, at] = a
            act_l[k, at] = pltpu.roll(a, 1, 0) * left_ref[...]
            act_r[k, at] = pltpu.roll(a, ROW - 1, 0) * right_ref[...]

    @pl.loop(0, rows)
    def _(r):
        fill(r, 1.0)

    fill(rows, on)

    @pl.loop(0, rows)
    def _(r):
        z = []
        for k in range(2):
            total = jnp.broadcast_to(taps_ref[k, pl.ds(9, 1)], (ROW, CB))
            for dr in range(3):
                at = pl.ds(pl.multiple_of(r * ROW + dr * ROW, ROW), ROW)
                for dc, ref in enumerate((act_l, act, act_r)):
                    total = total + ref[k, at] * taps_ref[k, pl.ds(dr * 3 + dc, 1)]
            z_ref[k, pl.ds(pl.multiple_of(r * ROW, ROW), ROW)] = total
            z.append(total)
        gated = z[0] * (z[1] * jax.nn.sigmoid(z[1]))
        g_ref[pl.ds(pl.multiple_of(r * ROW, ROW), ROW)] = bf(gated)

    part = mm_nt(g_ref[...], wd_ref[...].reshape(D, CB))

    @pl.when(pl.program_id(0) == 0)
    def _():
        out_ref[...] = part

    @pl.when(pl.program_id(0) > 0)
    def _():
        out_ref[...] += part


def ff_spec(ffw, k):
    groups, blocks, rows, lanes = ffw.shape
    per = lanes // CB

    def index(j):
        at = j // per
        return (0, at % 2 * 2 + at // 2 if blocks == 4 else 0, k, j % per)

    return pl.BlockSpec((groups, 1, rows // 3, CB), index)


def ffn_forward(x_ext, ffw, taps, left_ok, right_ok, on):
    n_ext = x_ext.shape[0]
    n_tok = n_ext - ROW
    weight = partial(ff_spec, ffw)
    pads = pltpu.VMEM((2, n_ext + ROW, CB), F32)
    return pl.pallas_call(
        ffn_forward_kernel,
        grid=(FFP // CB,),
        in_specs=[
            whole_spec((n_ext, D)), weight(0), weight(1), weight(2),
            pl.BlockSpec((2, 10, CB), lambda j: (0, 0, j)),
            whole_spec((ROW, CB)), whole_spec((ROW, CB)),
            pl.BlockSpec((1, 1), lambda j: (0, 0), memory_space=pltpu.SMEM),
        ],
        out_specs=[
            pl.BlockSpec((2, n_ext, CB), lambda j: (0, 0, j)),
            pl.BlockSpec((2, n_tok, CB), lambda j: (0, 0, j)),
            pl.BlockSpec((n_tok, CB), lambda j: (0, j)),
            whole_spec((n_tok, D)),
        ],
        out_shape=[
            jax.ShapeDtypeStruct((2, n_ext, FFP), F32),
            jax.ShapeDtypeStruct((2, n_tok, FFP), F32),
            jax.ShapeDtypeStruct((n_tok, FFP), BF16),
            jax.ShapeDtypeStruct((n_tok, D), F32),
        ],
        scratch_shapes=[pads, pads, pads],
        compiler_params=pltpu.CompilerParams(
            dimension_semantics=("arbitrary",), vmem_limit_bytes=LIMIT
        ),
        cost_estimate=pl.CostEstimate(
            flops=2 * n_ext * D * FFP * 3, bytes_accessed=50 * 2**20, transcendentals=n_ext * FFP * 3
        ),
    )(x_ext, ffw, ffw, ffw, taps, left_ok, right_ok, on)


def ffn_backward_kernel(
    d_ref, wd_ref, w0_ref, w1_ref, u_ref, z_ref, zh_ref, taps_ref, left_ref, right_ref, on_ref,
    du_ref, dt_ref, dn_ref, dg_buf, dz, dz_l, dz_r, acc
):
    n_tok = z_ref.shape[1]
    rows = n_tok // ROW
    zero = jnp.zeros((ROW, CB), F32)
    dg_buf[...] = mm(d_ref[...], wd_ref[...].reshape(D, CB))
    for k in range(2):
        for ref in (dz, dz_l, dz_r):
            ref[k, pl.ds(0, ROW)] = zero
    acc[...] = jnp.zeros_like(acc)

    def fill(r, z0, z1, scale, count):
        dg = dg_buf[pl.ds(pl.multiple_of(r * ROW, ROW), ROW)]
        gate = jax.nn.sigmoid(z1)
        soft = z1 * gate
        at = pl.ds(pl.multiple_of(r * ROW + ROW, ROW), ROW)
        d_both = (dg * soft, dg * z0 * (gate + soft * (1.0 - gate)))
        for k in range(2):
            value = d_both[k] * scale
            dz[k, at] = value
            dz_l[k, at] = pltpu.roll(value * left_ref[...], ROW - 1, 0)
            dz_r[k, at] = pltpu.roll(value * right_ref[...], 1, 0)
            if count:
                acc[k, 9] += fold(value)

    def fold(value):
        return value[0:8] + value[8:16] + value[16:24] + value[24:32]

    @pl.loop(0, rows)
    def _(r):
        at = pl.ds(pl.multiple_of(r * ROW, ROW), ROW)
        fill(r, z_ref[0, at], z_ref[1, at], 1.0, True)

    fill(rows, zh_ref[0], zh_ref[1], on_ref[0, 0], False)

    def back(r, taps_on):
        at = pl.ds(pl.multiple_of(r * ROW, ROW), ROW)
        for k in range(2):
            u = u_ref[k, at]
            gate = jax.nn.sigmoid(u)
            a = u * gate
            total = zero
            for dr in range(3):
                near = pl.ds(pl.multiple_of(r * ROW + (2 - dr) * ROW, ROW), ROW)
                for dc, ref in enumerate((dz_l, dz, dz_r)):
                    value = ref[k, near]
                    total = total + value * taps_ref[k, pl.ds(dr * 3 + dc, 1)]
                    if dr in taps_on:
                        acc[k, dr * 3 + dc] += fold(value * a)
            du_ref[k, at] = bf(total * (gate + a * (1.0 - gate)))

    @pl.loop(0, rows - 1)
    def _(r):
        back(r, (0, 1, 2))

    back(rows - 1, (1, 2))
    for k in range(2):
        u = u_ref[k, pl.ds(n_tok, ROW)]
        a = u * jax.nn.sigmoid(u) * on_ref[0, 0]
        for dc, ref in enumerate((dz_l, dz, dz_r)):
            acc[k, 6 + dc] += fold(ref[k, pl.ds(n_tok, ROW)] * a)
        for t in range(10):
            dt_ref[k, pl.ds(t, 1)] = jnp.sum(acc[k, t], axis=0, keepdims=True)

    part = mm_nt(du_ref[0], w0_ref[...].reshape(D, CB))
    part = part + mm_nt(du_ref[1], w1_ref[...].reshape(D, CB))

    @pl.when(pl.program_id(0) == 0)
    def _():
        dn_ref[...] = part

    @pl.when(pl.program_id(0) > 0)
    def _():
        dn_ref[...] += part


def ffn_backward(d_ext, ffw, upper, z, z_halo, taps, left_ok, right_ok, on):
    n_ext = d_ext.shape[0]
    n_tok = n_ext - ROW
    pads = pltpu.VMEM((2, n_ext + ROW, CB), F32)
    return pl.pallas_call(
        ffn_backward_kernel,
        grid=(FFP // CB,),
        in_specs=[
            whole_spec((n_ext, D)),
            ff_spec(ffw, 2), ff_spec(ffw, 0), ff_spec(ffw, 1),
            pl.BlockSpec((2, n_ext, CB), lambda j: (0, 0, j)),
            pl.BlockSpec((2, n_tok, CB), lambda j: (0, 0, j)),
            pl.BlockSpec((2, ROW, CB), lambda j: (0, 0, j)),
            pl.BlockSpec((2, 10, CB), lambda j: (0, 0, j)),
            whole_spec((ROW, CB)), whole_spec((ROW, CB)),
            pl.BlockSpec((1, 1), lambda j: (0, 0), memory_space=pltpu.SMEM),
        ],
        out_specs=[
            pl.BlockSpec((2, n_tok, CB), lambda j: (0, 0, j)),
            pl.BlockSpec((2, 10, CB), lambda j: (0, 0, j)),
            whole_spec((n_tok, D)),
        ],
        out_shape=[
            jax.ShapeDtypeStruct((2, n_tok, FFP), BF16),
            jax.ShapeDtypeStruct((2, 10, FFP), F32),
            jax.ShapeDtypeStruct((n_tok, D), F32),
        ],
        scratch_shapes=[
            pltpu.VMEM((n_ext, CB), F32), pads, pads, pads, pltpu.VMEM((2, 10, 8, CB), F32)
        ],
        compiler_params=pltpu.CompilerParams(
            dimension_semantics=("arbitrary",), vmem_limit_bytes=LIMIT
        ),
        cost_estimate=pl.CostEstimate(
            flops=2 * n_ext * D * FFP * 3, bytes_accessed=50 * 2**20, transcendentals=n_ext * FFP * 3
        ),
    )(d_ext, ffw, ffw, ffw, upper, z, z_halo, taps, left_ok, right_ok, on)


def ff_grad_kernel(spot_ref, left_ref, right_ref, out_ref):
    out_ref[0, 0] = mm_tn(left_ref[...], right_ref[0]).astype(out_ref.dtype)


def ff_grad(spot, left, right, away, dtype):
    n_tok = left.shape[0]
    count = right.shape[0]

    def lanes(k, r, spot_ref):
        return (k, 0, (spot_ref[1] + away) % 2 * 2 + (spot_ref[0] + r) % 2)

    return pl.pallas_call(
        ff_grad_kernel,
        grid_spec=pltpu.PrefetchScalarGridSpec(
            num_scalar_prefetch=1,
            grid=(count, 2),
            in_specs=[
                pl.BlockSpec((n_tok, D), lambda k, r, spot_ref: (0, 0)),
                pl.BlockSpec((1, n_tok, FFB), lanes),
            ],
            out_specs=pl.BlockSpec((1, 1, D, FFB), lambda k, r, spot_ref: (k, r, 0, 0)),
        ),
        out_shape=jax.ShapeDtypeStruct((count, 2, D, FFB), dtype),
        compiler_params=pltpu.CompilerParams(
            dimension_semantics=("arbitrary", "arbitrary"), vmem_limit_bytes=LIMIT
        ),
        cost_estimate=pl.CostEstimate(
            flops=4 * count * n_tok * D * FFB, bytes_accessed=6 * count * D * FFB, transcendentals=0
        ),
    )(spot, left, right)


def unit_grad_kernel(pairs, away, spot_ref, *refs):
    out_ref = refs[-1]
    unit = (spot_ref[0] + pl.program_id(0)) % 2 * 2 + (spot_ref[1] + away) % 2
    step = D // 3
    for number, (left, right) in enumerate(pairs):

        @pl.when(unit == number)
        def _():
            for i in range(3):
                rows = pl.ds(i * step, step)
                value = mm_tn(refs[left][:, rows], refs[right][...])
                out_ref[0, rows] = value.astype(out_ref.dtype)


def unit_grad(spot, arrays, pairs, away, dtype):
    n_tok = arrays[0].shape[0]
    return pl.pallas_call(
        partial(unit_grad_kernel, pairs, away),
        grid_spec=pltpu.PrefetchScalarGridSpec(
            num_scalar_prefetch=1,
            grid=(2,),
            in_specs=[pl.BlockSpec(a.shape, lambda r, spot_ref: (0, 0)) for a in arrays],
            out_specs=pl.BlockSpec((1, D, D), lambda r, spot_ref: (r, 0, 0)),
        ),
        out_shape=jax.ShapeDtypeStruct((2, D, D), dtype),
        compiler_params=pltpu.CompilerParams(
            dimension_semantics=("arbitrary",), vmem_limit_bytes=LIMIT
        ),
        cost_estimate=pl.CostEstimate(
            flops=4 * n_tok * D * D, bytes_accessed=16 * D * D, transcendentals=0
        ),
    )(spot, *arrays)


WIN = 256
QROWS = 512
BROWS = 256


def head_window(h):
    start = jnp.minimum(h * XHEAD // 128 * 128, D - WIN)
    lane = lax.broadcasted_iota(jnp.int32, (1, WIN), 1)
    mask = (lane >= h * XHEAD - start) & (lane < h * XHEAD - start + XHEAD)
    return pl.ds(pl.multiple_of(start, 128), WIN), mask


def cross_probs(q, keys, token_seg, text_seg):
    scores = mm_nt(q, keys) * XHEAD ** (-0.5)
    scores = jnp.where(token_seg == text_seg, scores, MASKED)
    top = jnp.max(scores, axis=-1, keepdims=True)
    probs = jnp.exp(scores - top)
    return probs * (1.0 / jnp.sum(probs, axis=-1, keepdims=True))


def cross_forward_kernel(q_ref, k_ref, v_ref, tok_ref, txt_ref, out_ref):
    win, mask = head_window(pl.program_id(0))
    keys, values = k_ref[:, win], v_ref[:, win]

    @pl.loop(0, q_ref.shape[0] // QROWS)
    def _(i):
        at = pl.ds(pl.multiple_of(i * QROWS, QROWS), QROWS)
        q = jnp.where(mask, q_ref[at, win], jnp.zeros((), BF16))
        probs = bf(cross_probs(q, keys, tok_ref[at, 0:1], txt_ref[...]))
        out_ref[at, win] = jnp.where(mask, bf(mm(probs, values)), out_ref[at, win])


def cross_forward(q, keys, values, token_seg, text_seg):
    n_tok = q.shape[0]
    n_txt = keys.shape[0]
    return pl.pallas_call(
        cross_forward_kernel,
        grid=(XHEADS,),
        in_specs=[
            whole_spec((n_tok, D)), whole_spec((n_txt, D)), whole_spec((n_txt, D)),
            whole_spec((n_tok, 1)), whole_spec((1, n_txt)),
        ],
        out_specs=whole_spec((n_tok, D)),
        out_shape=jax.ShapeDtypeStruct((n_tok, D), BF16),
        compiler_params=pltpu.CompilerParams(
            dimension_semantics=("arbitrary",), vmem_limit_bytes=LIMIT
        ),
        cost_estimate=pl.CostEstimate(
            flops=4 * n_tok * n_txt * WIN * XHEADS, bytes_accessed=5 * 2**20,
            transcendentals=n_tok * n_txt * XHEADS
        ),
    )(q, keys, values, token_seg, text_seg)


def cross_backward_kernel(
    q_ref, k_ref, v_ref, dc_ref, tok_ref, txt_ref, dq_ref, dk_ref, dv_ref, dk_acc, dv_acc
):
    win, mask = head_window(pl.program_id(0))
    keys, values = k_ref[:, win], v_ref[:, win]
    scale = XHEAD ** (-0.5)
    none = jnp.zeros((), BF16)
    dk_acc[...] = jnp.zeros_like(dk_acc)
    dv_acc[...] = jnp.zeros_like(dv_acc)

    @pl.loop(0, q_ref.shape[0] // BROWS)
    def _(i):
        at = pl.ds(pl.multiple_of(i * BROWS, BROWS), BROWS)
        q = jnp.where(mask, q_ref[at, win], none)
        dc = jnp.where(mask, dc_ref[at, win], none)
        probs = cross_probs(q, keys, tok_ref[at, 0:1], txt_ref[...])
        d_probs = mm_nt(dc, values)
        along = jnp.sum(probs * d_probs, axis=-1, keepdims=True)
        d_scores = bf(probs * (d_probs - along))
        dq_ref[at, win] = jnp.where(mask, bf(mm(d_scores, keys) * scale), dq_ref[at, win])
        dk_acc[...] += mm_tn(d_scores, q)
        dv_acc[...] += mm_tn(bf(probs), dc)

    dk_ref[:, win] = jnp.where(mask, dk_acc[...] * scale, dk_ref[:, win])
    dv_ref[:, win] = jnp.where(mask, dv_acc[...], dv_ref[:, win])


def cross_backward(q, keys, values, d_cross, token_seg, text_seg):
    n_tok = q.shape[0]
    n_txt = keys.shape[0]
    return pl.pallas_call(
        cross_backward_kernel,
        grid=(XHEADS,),
        in_specs=[
            whole_spec((n_tok, D)), whole_spec((n_txt, D)), whole_spec((n_txt, D)),
            whole_spec((n_tok, D)), whole_spec((n_tok, 1)), whole_spec((1, n_txt)),
        ],
        out_specs=[whole_spec((n_tok, D)), whole_spec((n_txt, D)), whole_spec((n_txt, D))],
        out_shape=[
            jax.ShapeDtypeStruct((n_tok, D), BF16),
            jax.ShapeDtypeStruct((n_txt, D), F32),
            jax.ShapeDtypeStruct((n_txt, D), F32),
        ],
        scratch_shapes=[pltpu.VMEM((n_txt, WIN), F32), pltpu.VMEM((n_txt, WIN), F32)],
        compiler_params=pltpu.CompilerParams(
            dimension_semantics=("arbitrary",), vmem_limit_bytes=LIMIT
        ),
        cost_estimate=pl.CostEstimate(
            flops=10 * n_tok * n_txt * WIN * XHEADS, bytes_accessed=12 * 2**20,
            transcendentals=n_tok * n_txt * XHEADS
        ),
    )(q, keys, values, d_cross, token_seg, text_seg)


GL = 128
GROUPS = D // GL


def parts(value):
    high = bf(value)
    return high, bf(value - wide(high))


def group_heads():
    row = lax.broadcasted_iota(jnp.int32, (GL, GL), 0) // HEAD
    col = lax.broadcasted_iota(jnp.int32, (GL, GL), 1) // HEAD
    return wide(row == col)


def both_segments(value, second):
    value = wide(value)
    late = value * second
    return bf(value - late), bf(late)


def state_kernel(k_ref, v_ref, sec_ref, kv_ref, ks_ref):
    same = group_heads()
    k0, k1 = both_segments(k_ref[...], sec_ref[...])
    kv_ref[0, 0] = mm_tn(k0, v_ref[...]) * same
    kv_ref[0, 1] = mm_tn(k1, v_ref[...]) * same
    ks_ref[0, 0] = jnp.broadcast_to(jnp.sum(wide(k0), axis=0, keepdims=True), (8, GL))
    ks_ref[0, 1] = jnp.broadcast_to(jnp.sum(wide(k1), axis=0, keepdims=True), (8, GL))


def attend(q_ref, sec_ref, kv_ref, ks_ref, same):
    q0, q1 = both_segments(q_ref[...], sec_ref[...])
    numer = 0.0
    denom = 1.0
    for i, q in enumerate((q0, q1)):
        for part in parts(kv_ref[0, i]):
            numer = numer + mm(q, part)
        sums = jnp.transpose(jnp.broadcast_to(ks_ref[0, i, 0:1], (GL, GL))) * same
        for part in parts(sums):
            denom = denom + mm(q, part)
    return q0, q1, numer, denom


def attend_kernel(q_ref, sec_ref, kv_ref, ks_ref, out_ref):
    _, _, numer, denom = attend(q_ref, sec_ref, kv_ref, ks_ref, group_heads())
    out_ref[...] = bf(numer / denom)


def attend_back_kernel(q_ref, da_ref, sec_ref, kv_ref, ks_ref, dq_ref, dkv_ref, dks_ref):
    same = group_heads()
    second = sec_ref[...]
    q0, q1, numer, denom = attend(q_ref, sec_ref, kv_ref, ks_ref, same)
    inverse = 1.0 / denom
    d_num = da_ref[...] * inverse
    high, low = parts(d_num * numer)
    ones = bf(same)
    d_den = -(mm(high, ones) + mm(low, ones)) * inverse
    d_parts = parts(d_num)
    back = []
    for i, q in enumerate((q0, q1)):
        total = 0.0
        grad = 0.0
        for part in d_parts:
            total = total + mm_tn(q, part)
        for part in parts(kv_ref[0, i]):
            for left in d_parts:
                grad = grad + mm_nt(left, part)
        dkv_ref[0, i] = total * same
        dks_ref[0, i] = jnp.broadcast_to(
            jnp.sum(wide(q) * d_den, axis=0, keepdims=True), (8, GL)
        )
        back.append(grad + d_den * ks_ref[0, i, 0:1])
    dq = jnp.where(second > 0, back[1], back[0])
    dq_ref[...] = bf(jnp.where(wide(q_ref[...]) > 0, dq, 0.0))


def state_back_kernel(k_ref, v_ref, sec_ref, dkv_ref, dks_ref, dk_ref, dv_ref):
    second = sec_ref[...] > 0
    k, v = k_ref[...], v_ref[...]
    dk, dv = [], []
    for i in range(2):
        grad_k = dks_ref[0, i, 0:1]
        grad_v = 0.0
        for part in parts(dkv_ref[0, i]):
            grad_k = grad_k + mm_nt(v, part)
            grad_v = grad_v + mm(k, part)
        dk.append(grad_k)
        dv.append(grad_v)
    dk_ref[...] = bf(jnp.where(wide(k) > 0, jnp.where(second, dk[1], dk[0]), 0.0))
    dv_ref[...] = bf(jnp.where(wide(v) > 0, jnp.where(second, dv[1], dv[0]), 0.0))


def by_group(kernel, n_tok, ins, outs, out_types):
    specs = dict(
        tok=pl.BlockSpec((n_tok, GL), lambda g: (0, g)),
        seg=whole_spec((n_tok, GL)),
        kv=pl.BlockSpec((1, 2, GL, GL), lambda g: (g, 0, 0, 0)),
        ks=pl.BlockSpec((1, 2, 8, GL), lambda g: (g, 0, 0, 0)),
    )
    shapes = dict(tok=(n_tok, D), kv=(GROUPS, 2, GL, GL), ks=(GROUPS, 2, 8, GL))
    return pl.pallas_call(
        kernel,
        grid=(GROUPS,),
        in_specs=[specs[i] for i in ins],
        out_specs=[specs[o] for o in outs],
        out_shape=[jax.ShapeDtypeStruct(shapes[o], t) for o, t in zip(outs, out_types)],
        compiler_params=pltpu.CompilerParams(
            dimension_semantics=("arbitrary",), vmem_limit_bytes=LIMIT
        ),
        cost_estimate=pl.CostEstimate(
            flops=16 * n_tok * D * GL, bytes_accessed=8 * 2**20, transcendentals=0
        ),
    )


def update(weight, grad, moment, average, factor, rate):
    clipped = factor * grad
    moment_new = MOMENTUM * moment + clipped
    weight_new = weight - rate * (clipped + MOMENTUM * moment_new)
    average_new = average + AVERAGE_RATE * (weight_new - average)
    return (weight_new, moment_new, average_new)


def local(
    n_dp, n_mp,
    latents, noise, captions, res_ids, timesteps, caption_lengths,
    in_proj, out_proj, w_up, w_down, cond, conv, tables,
    mom_in, mom_out, mom_up, mom_down, mom_cond, mom_conv, mom_tables,
    avg_in, avg_out, avg_up, avg_down, avg_cond, avg_conv, avg_tables,
):
    place = Place(n_dp, n_mp)
    y, c = place.y, place.c
    half_dp = n_dp // 2
    dl = D // n_dp
    spot = jnp.stack([y, c]).astype(jnp.int32)
    owner_rows = cond.shape[0]

    cond_b = bf(cond)
    units_b = unit_split(place, as_units(bf(in_proj), bf(out_proj)))
    cap_chunk = chunk_of(place, CAP_ROWS)
    cap_mine = spread_rows(place, cond_b, TIME_ROWS, CAP_ROWS)
    packed = jnp.concatenate([units_b.reshape(-1, D), cap_mine], axis=0)
    ff_b = jnp.stack([bf(w_up[:, 0]), bf(w_up[:, 1]), bf(w_down).T])
    ff_b = jnp.pad(ff_b, ((0, 0), (0, 0), (0, FFB - ff_b.shape[2])))
    packed, ff_b, cond_time = lax.optimization_barrier((packed, ff_b, cond_b))
    got = lax.all_gather(packed, AXES, axis=0)
    by_place = got.reshape((n_dp, 2, 2) + packed.shape)
    w_q, w_k, w_v, w_o0, w_xq, w_o1, w_xk, w_xv = [
        by_place[:, i, j, part * dl : (part + 1) * dl].reshape(D, D)
        for part in (0, 1) for i in (0, 1) for j in (0, 1)
    ]
    cap_w = got[:, 2 * dl :].reshape(-1, D)
    w_cap1, w_cap2 = cap_w[:CAPD], cap_w[CAPD:CAP_ROWS]
    ffw = lax.all_gather(ff_b.reshape(3 * dl, FFB), AXES, axis=0)
    if dl % 16 == 0:
        ffw = ffw.reshape(n_dp, 4, 3 * dl, FFB)
    else:
        ffw = ffw.reshape(n_dp, 2, 2, 3, dl, FFB).transpose(3, 0, 4, 2, 1, 5)
        ffw = ffw.reshape(1, 1, 3 * D, FFP)

    spread_time = spread_rows(place, cond_time, 0, TIME_ROWS)
    w_time = gather_rows_all(place, spread_time, (place.x_mask, 2, 1))[:TIME_ROWS]
    facts = jnp.concatenate([timesteps, res_ids[:, None]], axis=1)
    for b in range(place.dp_bits):
        mask = n_mp << b
        facts = ordered(place.bit(mask), facts, place.swap(facts, mask), 0)
    steps_all = facts[:, :4].reshape(-1)
    count = jnp.sum(jnp.where(facts[:, 4] == 0, 4.0, 1.0))
    slots = steps_all.shape[0]

    resolution = lax.dynamic_index_in_dim(res_ids, y, 0, False)
    lengths = lax.dynamic_index_in_dim(caption_lengths, y, 0, False)
    steps_t = lax.dynamic_index_in_dim(timesteps, y, 0, False)
    pair = jnp.stack([latents, noise])
    quarters = jnp.stack([pair] + [place.swap(pair, mask) for mask in (1, 2, 3)])
    parts = [lax.dynamic_index_in_dim(quarters, (2 * c + j) ^ place.mp, 0, False) for j in (0, 1)]
    tokens = jnp.concatenate(
        [lax.dynamic_index_in_dim(part, y, 1, False) for part in parts], axis=1
    )
    n_tok = tokens.shape[1]
    rows = n_tok // SIDE
    grid = tokens.reshape(2, rows, SIDE, CIN)
    tokens = jnp.where(c == 1, grid[:, ::-1], grid).reshape(2, n_tok, CIN)
    clean, noisy = wide(tokens[0]), wide(tokens[1])
    col = jnp.arange(n_tok, dtype=jnp.int32)[:, None] % SIDE
    second = (col >= SIDE // 2) & (resolution == 0)
    seg0 = jnp.where(resolution == 0, 2 * c, 0)
    seg1 = jnp.where(resolution == 0, 2 * c + 1, 0)
    token_seg = jnp.where(second, seg1, seg0)

    def pick(table):
        first = lax.dynamic_index_in_dim(table, seg0, 0, True)
        other = lax.dynamic_index_in_dim(table, seg1, 0, True)
        return jnp.where(second, other, first)

    def by_segment(value):
        late = jnp.sum(jnp.where(second, value, 0.0), axis=0)
        early = jnp.sum(jnp.where(second, 0.0, value), axis=0)
        slot = jnp.arange(4, dtype=jnp.int32)[:, None]
        table = jnp.where(slot == seg0, early, 0.0) + jnp.where(slot == seg1, late, 0.0)
        return table, early + late

    sigma = pick(wide(steps_t)[:, None] / TMAX)
    mixed_in = (1.0 - sigma) * clean + sigma * noisy
    target = noisy - clean
    image_tokens = jnp.where(resolution == 0, (SIDE // 2) ** 2, SIDE * SIDE).astype(F32)
    loss_weight = 1.0 / (CIN * image_tokens * count)

    freq_b = bf(time_embed(steps_all))
    time_hidden = mm(freq_b, w_time[:FREQ])
    hidden_b = bf(jax.nn.silu(time_hidden))
    time_emb = mm(hidden_b, w_time[FREQ:])
    silu_b = bf(jax.nn.silu(time_emb))
    mod_mine = mm_nt(silu_b, cond_b).reshape(n_dp, 2, 1, 4 * owner_rows)
    mod_send = jnp.broadcast_to(mod_mine, (n_dp, 2, 2, 4 * owner_rows))
    mod_got = lax.all_to_all(mod_send.reshape(place.n, 4 * owner_rows), AXES, 0, 0)
    time_mod = mod_got.reshape(place.n, 4, owner_rows).transpose(1, 0, 2).reshape(4, -1)
    time_mod = time_mod[:, BLOCK_AT:].reshape(4, 6, D)
    mod_table = tables[None, :6] + time_mod
    mods = [pick(mod_table[:, k]) for k in range(6)]
    canvas = place.dp * 2 + y
    emb_mine = lax.dynamic_slice_in_dim(time_emb, canvas * 4, 4, 0)
    emb_tok = pick(emb_mine)

    own_cap = lax.dynamic_index_in_dim(captions, y, 0, False)
    their_cap = lax.dynamic_index_in_dim(captions, 1 - y, 0, False)
    caption = jnp.concatenate([own_cap, place.swap(their_cap, 2)], axis=0)
    quarter = own_cap.shape[0]
    within = jnp.arange(quarter, dtype=jnp.int32)
    text_at = jnp.concatenate([(place.mp ^ m) * quarter + within for m in (0, 2, 1, 3)])
    ends = jnp.cumsum(lengths)
    text_segment = jnp.sum((text_at[:, None] >= ends[None, :]).astype(jnp.int32), axis=1)
    cap_hidden = mm(caption, w_cap1)
    cap_act, gelu_pull = jax.vjp(partial(jax.nn.gelu, approximate=True), cap_hidden)
    cap_act_b = bf(cap_act)
    text_raw = mm(cap_act_b, w_cap2)
    gain = tables[8]
    text_inv = lax.rsqrt(jnp.mean(text_raw * text_raw, -1, keepdims=True) + EPS)
    text_hat = text_raw * text_inv
    text_b = bf(text_hat * gain)
    text_k = bf(mm(text_b, w_xk))
    text_v = bf(mm(text_b, w_xv))
    keys = jnp.concatenate([text_k, place.swap(text_k, 1)], axis=0)
    values = jnp.concatenate([text_v, place.swap(text_v, 1)], axis=0)

    embed = mm(mixed_in, tables[9 : 9 + CIN], HIGH)
    hat_a, inv_a = layer_norm(embed)
    normed_a = bf(hat_a * (1.0 + mods[1]) + mods[0])
    q = bf(jax.nn.relu(mm(normed_a, w_q)))
    k = bf(jax.nn.relu(mm(normed_a, w_k)))
    v = bf(jax.nn.relu(mm(normed_a, w_v)))
    whole_image = wide(resolution == 1)
    second_wide = jnp.broadcast_to(wide(second), (n_tok, GL))

    def shared(state, sums):
        first = jnp.concatenate([state[:, 0], sums[:, 0]], axis=1)
        first = first + whole_image * place.swap(first, 1)
        state = jnp.stack([first[:, :GL], state[:, 1]], axis=1)
        return state, jnp.stack([first[:, GL:], sums[:, 1]], axis=1)

    group_call = partial(by_group, n_tok=n_tok)
    state, key_sum = group_call(
        state_kernel, ins=("tok", "tok", "seg"), outs=("kv", "ks"), out_types=(F32, F32)
    )(k, v, second_wide)
    state, key_sum = shared(state, key_sum)
    (attn_b,) = group_call(
        attend_kernel, ins=("tok", "seg", "kv", "ks"), outs=("tok",), out_types=(BF16,)
    )(q, second_wide, state, key_sum)
    branch_a = mm_nt(attn_b, w_o0)
    state_a = embed + mods[2] * branch_a

    state_b = bf(state_a)
    xq = bf(mm(state_b, w_xq))
    cross_b = cross_forward(xq, keys, values, token_seg, text_segment[None, :])
    state_c = state_a + mm_nt(cross_b, w_o1)

    hat_f, inv_f = layer_norm(state_c)
    normed_f = bf(hat_f * (1.0 + mods[4]) + mods[3])
    taps = to_ff(conv)
    flipped = jnp.concatenate([taps[:, 6:9], taps[:, 3:6], taps[:, 0:3], taps[:, 9:]], axis=1)
    taps = jnp.where(c == 1, flipped, taps)
    column = jnp.arange(SIDE, dtype=jnp.int32)[:, None]
    middle = SIDE // 2
    left_ok = (column != 0) & ((resolution == 1) | (column != middle))
    right_ok = (column != SIDE - 1) & ((resolution == 1) | (column != middle - 1))
    left_ok = jnp.broadcast_to(wide(left_ok), (SIDE, CB))
    right_ok = jnp.broadcast_to(wide(right_ok), (SIDE, CB))
    halo_on = whole_image.reshape(1, 1)
    edge = n_tok - SIDE
    x_ext = jnp.concatenate([normed_f, place.swap(normed_f[edge:], 1)], axis=0)
    upper, z, gated_b, branch_f = ffn_forward(
        x_ext, ffw, taps, left_ok, right_ok, halo_on
    )
    z_halo = place.swap(z[:, edge:], 1)
    state_f = state_c + mods[5] * branch_f

    hat_o, inv_o = layer_norm(state_f)
    shift_o = tables[6] + emb_tok
    scale_o = tables[7] + emb_tok
    final = hat_o * (1.0 + scale_o) + shift_o
    out_rows = tables[9 + CIN :]
    output = mm_nt(final, out_rows, HIGH)
    error = output - target
    loss = jnp.sum(error * error) * loss_weight

    d_output = 2.0 * loss_weight * error
    d_final = mm(d_output, out_rows, HIGH)
    d_out_rows = mm_tn(d_output, final, HIGH)
    d_shift_seg, d_shift_o = by_segment(d_final)
    d_scale_seg, d_scale_o = by_segment(d_final * hat_o)
    d_emb_mine = d_shift_seg + d_scale_seg
    d_state_f = layer_norm_back(d_final * (1.0 + scale_o), hat_o, inv_o)

    split_dp = (2,) * place.dp_bits
    far = [(b, n_mp << (place.dp_bits - 1 - b)) for b in range(place.dp_bits - 2, -1, -1)]

    def stages(lead, order):
        table = {
            "x": ("abs", lead + place.dp_bits - 1, place.x_mask),
            "y": ("rel", lead - 1, 2),
        }
        return [table[o] for o in order] + [("abs", lead + axis, mask) for axis, mask in far]

    def ff_flow(left, right, orders):
        shape = (1, 2) + split_dp + (dl, FFB)
        away = ff_grad(spot, left, right, 1, BF16)
        flows = [
            Flow(place, away[i].reshape(shape), stages(2, order)) for i, order in enumerate(orders)
        ]
        left, right, away = lax.optimization_barrier((left, right, away))
        for i, flow in enumerate(flows):
            flow.keep = ff_grad(spot, left, right[i : i + 1], 0, F32).reshape(shape)
        return flows

    def unit_flow(arrays, pairs, order):
        shape = (2,) + split_dp + (dl, D)
        away = unit_grad(spot, arrays, pairs, 1, BF16)
        flow = Flow(place, away.reshape(shape), stages(1, order))
        arrays, away = lax.optimization_barrier((arrays, away))
        flow.keep = unit_grad(spot, arrays, pairs, 0, F32).reshape(shape)
        return flow

    def settle(value, flows):
        value, keeps = lax.optimization_barrier((value, [flow.keep for flow in flows]))
        for flow, keep in zip(flows, keeps):
            flow.keep = keep
        return tick(value, flows)

    d_branch_f = bf(mods[5] * d_state_f)
    d_edge = place.swap(d_branch_f[edge:], 1)
    flow_dn, = ff_flow(d_branch_f, gated_b[None], ["yx"])
    d_ext = jnp.concatenate([d_branch_f, d_edge], axis=0)
    d_ext = settle(d_ext, [flow_dn])
    d_upper, d_taps, d_normed_f = tick(
        ffn_backward(d_ext, ffw, upper, z, z_halo, taps, left_ok, right_ok, halo_on), [flow_dn]
    )
    unflipped = jnp.concatenate(
        [d_taps[:, 6:9], d_taps[:, 3:6], d_taps[:, 0:3], d_taps[:, 9:]], axis=1
    )
    conv_grad = from_ff(jnp.where(c == 1, unflipped, d_taps))
    flow_up = ff_flow(normed_f, d_upper, ["xy", "yx"])
    ffn_flows = [flow_dn] + flow_up
    d_normed_f = settle(d_normed_f, flow_up)
    d_state_c = d_state_f + layer_norm_back(d_normed_f * (1.0 + mods[4]), hat_f, inv_f)
    d_mods = [None] * 6
    d_mods[5] = by_segment(d_state_f * branch_f)
    d_mods[3] = by_segment(d_normed_f)
    d_mods[4] = by_segment(d_normed_f * hat_f)

    d_branch_c = bf(d_state_c)
    d_cross = bf(mm(d_branch_c, w_o1))
    conv_sent = place.swap(conv_grad, 1)
    d_xq_b, d_keys, d_values, conv_sent = tick(
        tuple(cross_backward(xq, keys, values, d_cross, token_seg, text_segment[None, :]))
        + (conv_sent,),
        ffn_flows,
    )
    conv_grad = conv_grad + conv_sent
    half_txt = TXT // 2
    d_kv = jnp.stack([d_keys, d_values])
    d_kv = d_kv[:, :half_txt] + place.swap(d_kv[:, half_txt:], 1)
    d_kv_b = bf(d_kv)
    early = unit_flow(
        [state_b, d_xq_b, d_branch_c, cross_b, text_b, d_kv_b[0], d_kv_b[1]],
        ((0, 1), (2, 3), (4, 5), (4, 6)),
        "yx",
    )
    d_state_a = d_state_c + mm_nt(d_xq_b, w_xq)
    d_state_a = settle(d_state_a, [early])

    d_text = mm_nt(d_kv_b[0], w_xk) + mm_nt(d_kv_b[1], w_xv)
    d_gain = jnp.sum(d_text * text_hat, axis=0)
    d_hat = d_text * gain
    d_text_raw = text_inv * (d_hat - text_hat * jnp.mean(d_hat * text_hat, -1, keepdims=True))
    d_text_raw_b = bf(d_text_raw)
    g_cap2 = mm_tn(cap_act_b, d_text_raw_b)
    d_cap_b = bf(gelu_pull(mm_nt(d_text_raw_b, w_cap2))[0])
    conv_sent = place.swap(conv_grad, 2)
    d_cap_b, conv_sent, d_state_a = tick((d_cap_b, conv_sent, d_state_a), ffn_flows)
    conv_grad = conv_grad + conv_sent
    g_cap1 = mm_tn(caption, d_cap_b)
    g_cap = jnp.concatenate(
        [g_cap1, g_cap2, jnp.zeros((place.n * cap_chunk - CAP_ROWS, D), F32)], axis=0
    ).reshape(split_dp + (2, 2, cap_chunk, D))
    b = place.dp_bits
    cap_flow = Flow(
        place,
        bf(lax.dynamic_slice_in_dim(g_cap, 1 - c, 1, b + 1)),
        [("abs", b - 1, place.x_mask), ("abs", b, 2)] + [("abs",) + pair_ for pair_ in far],
    )
    cap_flow.keep = lax.dynamic_slice_in_dim(g_cap, c, 1, b + 1)
    d_state_a = settle(d_state_a, [cap_flow])

    d_branch_a = bf(mods[2] * d_state_a)
    d_mods[2] = by_segment(d_state_a * branch_a)
    d_attn = mm(d_branch_a, w_o0)
    conv_sent = place.swap(conv_grad, place.x_mask)
    dq_b, d_state, d_sum, conv_sent = tick(
        tuple(group_call(
            attend_back_kernel,
            ins=("tok", "tok", "seg", "kv", "ks"),
            outs=("tok", "kv", "ks"),
            out_types=(BF16, F32, F32),
        )(q, d_attn, second_wide, state, key_sum)) + (conv_sent,),
        ffn_flows + [early],
    )
    conv_grad = conv_grad + conv_sent
    d_state, d_sum = shared(d_state, d_sum)
    dk_b, dv_b = group_call(
        state_back_kernel,
        ins=("tok", "tok", "seg", "kv", "ks"),
        outs=("tok", "tok"),
        out_types=(BF16, BF16),
    )(k, v, second_wide, d_state, d_sum)
    dk_b, dv_b = tick((dk_b, dv_b), flow_up)
    late = unit_flow(
        [normed_a, dq_b, dk_b, dv_b, d_branch_a, attn_b],
        ((0, 1), (0, 2), (0, 3), (4, 5)),
        "xy",
    )
    dq_b, dk_b, dv_b = settle((dq_b, dk_b, dv_b), [late])
    dq_b, dk_b, dv_b = tick((dq_b, dk_b, dv_b), [early, cap_flow])
    d_normed_a = mm_nt(dq_b, w_q) + mm_nt(dk_b, w_k) + mm_nt(dv_b, w_v)
    d_mods[0] = by_segment(d_normed_a)
    d_mods[1] = by_segment(d_normed_a * hat_a)
    d_embed = d_state_a + layer_norm_back(d_normed_a * (1.0 + mods[1]), hat_a, inv_a)
    g_patch = mm_tn(mixed_in, d_embed, HIGH)
    d_rows_six = jnp.stack([total for _, total in d_mods])
    tables_grad = jnp.concatenate(
        [d_rows_six, d_shift_o[None], d_scale_o[None], d_gain[None], g_patch, d_out_rows], axis=0
    )
    for b in range(place.dp_bits + 2):
        tables_grad = tables_grad + place.swap(tables_grad, 1 << b)
        if (1 << b) > place.x_mask:
            conv_grad = conv_grad + place.swap(conv_grad, 1 << b)

    d_mod = jnp.stack([table for table, _ in d_mods], axis=1).reshape(4, 6 * D)
    d_mod = jnp.pad(d_mod, ((0, 0), (BLOCK_AT, 0)))
    d_mod = d_mod.reshape(4, place.n, owner_rows).transpose(1, 0, 2)
    d_mod = lax.all_to_all(d_mod, AXES, 0, 0)
    d_mod = d_mod.reshape(slots // 4, 2, 4, owner_rows).sum(1).reshape(slots, owner_rows)
    g_block = mm_tn(d_mod, wide(silu_b), HIGH)
    d_silu = mm(d_mod, wide(cond_b), HIGH)
    d_silu = d_silu.reshape(split_dp + (2, 4, D))
    for axis, mask in [(place.dp_bits, 2), (place.dp_bits - 1, place.x_mask)] + far:
        bit = place.bit(mask)
        away = lax.dynamic_slice_in_dim(d_silu, 1 - bit, 1, axis)
        d_silu = lax.dynamic_slice_in_dim(d_silu, bit, 1, axis) + place.swap(away, mask)
    d_silu = d_silu.reshape(4, D)
    pair_sum = jnp.stack([d_silu, d_emb_mine])
    d_silu, d_emb = pair_sum + place.swap(pair_sum, 1)
    d_time = d_silu * silu_grad(emb_mine) + d_emb
    d_hidden = mm_nt(d_time, wide(w_time[FREQ:]), HIGH)
    hidden_mine = lax.dynamic_slice_in_dim(time_hidden, canvas * 4, 4, 0)
    d_times = jnp.stack([d_time, d_hidden * silu_grad(hidden_mine)])
    for mask in [2] + [n_mp << b for b in range(place.dp_bits)]:
        d_times = ordered(place.bit(mask), d_times, place.swap(d_times, mask), 1)
    g_time2 = mm_tn(wide(hidden_b), d_times[0], HIGH)
    g_time1 = mm_tn(wide(freq_b), d_times[1], HIGH)
    spots = -(-TIME_ROWS // owner_rows)
    g_time = jnp.concatenate(
        [g_time1, g_time2, jnp.zeros(((spots + 1) * owner_rows - TIME_ROWS, D), F32)], axis=0
    )
    g_time = lax.dynamic_slice_in_dim(
        g_time, jnp.minimum(place.me, spots) * owner_rows, owner_rows, 0
    )

    ff_own = [flow.drain().reshape(dl, FFB)[:, : FF // 4] for flow in ffn_flows]
    early_own = early.drain().reshape(dl, D)
    g_cap = collect_rows(
        place, cap_flow.drain().reshape(cap_chunk, D), owner_rows, TIME_ROWS, CAP_ROWS
    )
    g_cond = g_cap + g_block + g_time
    mine = jnp.stack([late.drain().reshape(dl, D), early_own])
    owned_sq = sum(jnp.sum(grad * grad) for grad in [mine, g_cond] + ff_own)
    g_in, g_out = from_units(unit_join(place, mine))
    g_upper = jnp.stack(ff_own[1:], axis=1)
    g_lower = ff_own[0].T
    owned = (g_in, g_out, g_upper, g_lower, g_cond)

    sums = jnp.stack([owned_sq, loss]).reshape(1, 2)
    for b in range(place.dp_bits + 2):
        sums = sums + place.swap(sums, 1 << b)
    squares, loss = sums[0, 0], sums[0, 1]
    norm = jnp.sqrt(squares + jnp.sum(conv_grad * conv_grad) + jnp.sum(tables_grad * tables_grad))
    factor = CLIP / jnp.maximum(norm, CLIP)
    rate = STEP_SCALE * math.sqrt(PARAMS) / CLIP
    grads = owned + (conv_grad, tables_grad)
    weights = (in_proj, out_proj, w_up, w_down, cond, conv, tables)
    moments = (mom_in, mom_out, mom_up, mom_down, mom_cond, mom_conv, mom_tables)
    averages = (avg_in, avg_out, avg_up, avg_down, avg_cond, avg_conv, avg_tables)
    new = [
        update(weights[i], grads[i], moments[i], averages[i], factor, rate) for i in range(7)
    ]
    moments_out = [new[i][1] for i in range(5)] + [factor * conv_grad, new[6][1]]
    return (loss, norm, *[n[0] for n in new], *moments_out, *[n[2] for n in new])


def solution(mesh):
    tokens = P("dp", "mp", None)
    weights = (
        P("dp", None, "mp"),
        P(None, "mp", "dp"),
        P("dp", None, "mp"),
        P("mp", "dp"),
        P(("dp", "mp"), None),
        P(),
        P(),
    )
    in_specs = (tokens, tokens, tokens, P("dp"), P("dp", None), P("dp", None)) + weights * 3
    out_specs = (P(), P()) + weights * 3
    body = partial(local, mesh.shape["dp"], mesh.shape["mp"])
    return jax.shard_map(body, mesh=mesh, in_specs=in_specs, out_specs=out_specs, check_vma=False)
```

time: 3480 us -> 1290 us (0.37)
  waiting for transfers between devices: 2230 us -> 470 us
  matrix products: 453 us -> 88.2 us
  other arithmetic: 464 us -> 160 us
  Pallas kernels: 0 us -> 245 us
  starting transfers between devices: 5 us -> 145 us
  local copies, waits for them, and re-layouts: 221 us -> 139 us
  blocking collectives: 59.5 us -> 0 us
    reduce_scatter x17 -> x0, waiting for transfers between devices: 793 us -> none  [the longest x14 454 us: scatter_rows(): return lax.psum_scatter(value, 'mp', scatter_dimension=0, tiled=True)]
    unnamed x13 -> x2, waiting for transfers between devices: 695 us -> 0.71 us
    all_gather x19 -> x2, waiting for transfers between devices: 642 us -> 95.6 us  [the longest x1 51.9 us: local(): ffw = lax.all_gather(ff_b.reshape(3 * dl, FFB), AXES, axis=0)]
    dot_general x120 -> x34, matrix products: 453 us -> 88.2 us  [dot(): lax.dot_general(left, right, (dims, ((), ())), precision=precision, prefe...]
    ppermute x0 -> x103, waiting for transfers between devices: none -> 363 us  [the longest x84 338 us: swap(): return lax.ppermute(value, AXES, [(i, i ^ mask) for i in range(self.n)])]
    pallas_call x0 -> x17, Pallas kernels: none -> 245 us  [the longest x1 60.3 us: ffn_backward(): pl.pallas_call(ffn_backward_kernel, grid=(FFP // CB,), in_specs=[whole_sp...]
    ppermute x0 -> x103, starting transfers between devices: none -> 131 us  [the longest x84 113 us: swap(): return lax.ppermute(value, AXES, [(i, i ^ mask) for i in range(self.n)])]
    psum x1 -> x0, waiting for transfers between devices: 102 us -> none  [local(): lax.psum((small[0], small[1], owned_sq, loss_total), ('dp', 'mp'))]
  transfers between devices with their start and end apart: 39 -> 107, of which waited for: 35 -> 45; matrix products, arithmetic and copies ran while one was open for 10% -> 22% of each run, Pallas kernels for 0% -> 14%
where the time goes in v1:
time: 1290 us; the launch traced here: 1280 us
  waiting for transfers between devices  470 us (36%)
  Pallas kernels  245 us (19%)
  other arithmetic  160 us (12%)
  starting transfers between devices  145 us (11%)
  local copies, waits for them, and re-layouts  139 us (11%)
  matrix products  88.2 us (7%)
  between operations  28.5 us (2%)
    ppermute x84, waiting for transfers between devices, swap(): return lax.ppermute(value, AXES, [(i, i ^ mask) for i in range(self.n)])  338 us
    ppermute x84, starting transfers between devices, swap(): return lax.ppermute(value, AXES, [(i, i ^ mask) for i in range(self.n)])  113 us
    dot_general x34, matrix products, dot(): lax.dot_general(left, right, (dims, ((), ())), precision=precision, prefe...  88.2 us
    add x24, other arithmetic, land(): total = self.keep + wide(self.moving)  74.8 us
    pallas_call x1, Pallas kernels, ffn_backward(): pl.pallas_call(ffn_backward_kernel, grid=(FFP // CB,), in_specs=[whole_sp...  60.3 us
    all_gather x1, waiting for transfers between devices, local(): ffw = lax.all_gather(ff_b.reshape(3 * dl, FFB), AXES, axis=0)  51.9 us
    pallas_call x1, Pallas kernels, ffn_forward(): pl.pallas_call(ffn_forward_kernel, grid=(FFP // CB,), in_specs=[whole_spe...  45.7 us
    all_gather x1, waiting for transfers between devices, local(): got = lax.all_gather(packed, AXES, axis=0)  43.8 us
  transfers between devices with their start and end apart: 107, of which 45 were waited for; matrix products, arithmetic and copies ran while one was open for 22% of the time, Pallas kernels for 14%

profile of v1, /device:TPU:28, one launch (start us, length us, event | category | flops | bytes accessed | tf_op | source)
XLA Modules:
  0.0 1275.2 jit_solution(7912477446320388400)
XLA Ops:
  28.3 9.6 collective-permute-done.12
  102.0 17.1 %collective-permute-start.24 = (bf16[2,48,1152]{2,1,0:T(8,128)(2,1)S(1)}, bf16[2,48,1152]{2,1,0:T(8,128)(2,1)S(1)}, u32[]{:S(2)}, u32[]{:S(2)}) collective-permute-start(bf16[2,48,1152]{2,1,0:T(8,128)(2,1)S(1)} %pad_maximum_fusion.23), channel_id=1, source_target_pairs={{0,16},{1,17},{2,18},{3,19},{4,20},{5,21},{6,22},{7,23},{8,24},{9,... | collective-permute-start | bytes 663560 | tf_op jit(solution)/shard_map/ppermute | solution.py:79
  122.6 20.0 %collective-permute-done.24 = bf16[2,48,1152]{2,1,0:T(8,128)(2,1)S(1)} collective-permute-done((bf16[2,48,1152]{2,1,0:T(8,128)(2,1)S(1)}, bf16[2,48,1152]{2,1,0:T(8,128)(2,1)S(1)}, u32[]{:S(2)}, u32[]{:S(2)}) %collective-permute-start.24) | collective-permute-done | bytes 221216 | tf_op jit(solution)/shard_map/ppermute | solution.py:79
  153.9 20.3 %collective-permute-done.27 = bf16[4,48,1152]{2,1,0:T(8,128)(2,1)S(1)} collective-permute-done((bf16[4,48,1152]{2,1,0:T(8,128)(2,1)S(1)}, bf16[4,48,1152]{2,1,0:T(8,128)(2,1)S(1)}, u32[]{:S(2)}, u32[]{:S(2)}) %collective-permute-start.27) | collective-permute-done | bytes 442400 | tf_op jit(solution)/shard_map/ppermute | solution.py:79
  204.2 43.8 %all-gather.6.cloned.1.call-done = bf16[12800,1152]{1,0:T(8,128)(2,1)} async-done(((bf16[400,1152]{1,0:T(8,128)(2,1)}), bf16[12800,1152]{1,0:T(8,128)(2,1)}) %all-gather.6.cloned.1.call-update) | async-done | bytes 29491216 | tf_op jit(solution)/shard_map/all_gather | solution.py:852
  263.3 13.6 %fusion.180 = (bf16[8,1,1,144,1152]{4,3,2,1,0:T(8,128)(2,1)}, bf16[8,1,1,144,1152]{4,3,2,1,0:T(8,128)(2,1)}, bf16[8,1,1,144,1152]{4,3,2,1,0:T(8,128)(2,1)S(1)}, ...) fusion(bf16[8,2,2,400,1152]{4,3,2,1,0:T(8,128)(2,1)} %bitcast.367), kind=kLoop, calls=%fused_computation.562 | loop fusion | bytes 42467328 | tf_op jit(solution)/shard_map/slice | solution.py:855
  307.4 17.9 %shard_map.436.refs_3_ = bf16[512,1152]{1,0:T(8,128)(2,1)S(1)} custom-call(bf16[512,1152]{1,0:T(8,128)(2,1)S(1)} %convolution_convert_fusion.1.q_ref, bf16[512,1152]{1,0:T(8,128)(2,1)S(1)} %pad_maximum_fusion.8.k_ref, bf16[512,1152]{1,0:T(8,128)(2,1)S(1)} %pad_maximum_fusion.9.v_ref, s32[512,1]{1,0:T(8,128)S(1)} %fusion.98.tok_ref, s32[1,512]{1,0:T(1,128)S(1)} %bitcast.352), custom_call_target="tpu_custom_call" | custom-call | flops 4294967296 | bytes 5242880 | tf_op jit(solution)/shard_map/pallas_call | solution.py:634
  334.7 51.9 %all-gather.4.cloned.1.call-done = bf16[32,432,768]{2,1,0:T(8,128)(2,1)} async-done(((bf16[1,432,768]{2,1,0:T(8,128)(2,1)}), bf16[32,432,768]{2,1,0:T(8,128)(2,1)}) %all-gather.4.cloned.1.call-update) | async-done | bytes 21233680 | tf_op jit(solution)/shard_map/all_gather | solution.py:860
  386.7 45.7 %shard_map.437 = (f32[2,544,3072]{2,1,0:T(8,128)}, f32[2,512,3072]{2,1,0:T(8,128)}, bf16[512,3072]{1,0:T(8,128)(2,1)}, f32[512,1152]{1,0:T(8,128)S(1)}) custom-call(bf16[544,1152]{1,0:T(8,128)(2,1)S(1)} %pad_maximum_fusion.4.x_ref, bf16[8,4,432,768]{3,2,1,0:T(8,128)(2,1)} %bitcast.354, bf16[8,4,432,768]{3,2,1,0:T(8,128)(2,1)} %bitcast.355, ...), custom_call_target="tpu_custom_call" | custom-call | flops 11551113216 | bytes 52428800 | tf_op jit(solution)/shard_map/pallas_call | solution.py:385
  463.7 60.3 %shard_map.440 = (bf16[2,512,3072]{2,1,0:T(8,128)(2,1)}, f32[2,10,3072]{2,1,0:T(8,128)S(1)}, f32[512,1152]{1,0:T(8,128)S(1)}) custom-call(bf16[544,1152]{1,0:T(8,128)(2,1)S(1)} %pad_maximum_fusion.5.d_ref, bf16[8,4,432,768]{3,2,1,0:T(8,128)(2,1)} %bitcast.357, bf16[8,4,432,768]{3,2,1,0:T(8,128)(2,1)} %bitcast.358, bf16[8,4,432,768]{3,2,1,0:T(8,128)(2,1)} %bitcast.359, ...), custom_call_target="tpu_custom_call" | custom-call | flops 11551113216 | bytes 52428800 | tf_op jit(solution)/shard_map/pallas_call | solution.py:498
  595.7 37.9 %shard_map.444 = (bf16[512,1152]{1,0:T(8,128)(2,1)S(1)}, f32[512,1152]{1,0:T(8,128)}, f32[512,1152]{1,0:T(8,128)}) custom-call(bf16[512,1152]{1,0:T(8,128)(2,1)S(1)} %copy-done.44, bf16[512,1152]{1,0:T(8,128)(2,1)S(1)} %copy-done.30, bf16[512,1152]{1,0:T(8,128)(2,1)S(1)} %copy-done.32, bf16[512,1152]{1,0:T(8,128)(2,1)S(1)} %convolution_convert_fusion.dc_ref, ...), custom_call_target="tpu_custom_call" | custom-call | flops 10737418240 | bytes 12582912 | tf_op jit(solution)/shard_map/pallas_call | solution.py:683
  692.5 10.5 convert_add_fusion.1
  750.3 11.6 shard_map.447
  761.9 33.0 %collective-permute-done.58 = bf16[1,2,2,2,144,1152]{5,4,3,2,1,0:T(8,128)(2,1)} collective-permute-done((bf16[1,2,2,2,144,1152]{5,4,3,2,1,0:T(8,128)(2,1)}, bf16[1,2,2,2,144,1152]{5,4,3,2,1,0:T(8,128)(2,1)}, u32[]{:S(2)}, u32[]{:S(2)}) %collective-permute-start.58) | collective-permute-done | bytes 2654240 | tf_op jit(solution)/shard_map/ppermute | solution.py:79
  865.3 10.5 convert_add_fusion
  880.4 43.8 %collective-permute-done.68 = bf16[2,2,1,2,1,112,1152]{6,5,4,3,2,1,0:T(8,128)(2,1)} collective-permute-done((bf16[2,2,1,2,1,112,1152]{6,5,4,3,2,1,0:T(8,128)(2,1)}, bf16[2,2,1,2,1,112,1152]{6,5,4,3,2,1,0:T(8,128)(2,1)}, u32[]{:S(2)}, u32[]{:S(2)}) %collective-permute-start.68) | collective-permute-done | bytes 2064416 | tf_op jit(solution)/shard_map/ppermute | solution.py:79
  1016.0 44.1 %collective-permute-done.85 = f32[2,8,1152]{2,1,0:T(8,128)S(1)} collective-permute-done((f32[2,8,1152]{2,1,0:T(8,128)S(1)}, f32[2,8,1152]{2,1,0:T(8,128)S(1)}, u32[]{:S(2)}, u32[]{:S(2)}) %collective-permute-start.85) | collective-permute-done | bytes 73760 | tf_op jit(solution)/shard_map/ppermute | solution.py:79
  1069.3 16.0 %collective-permute-done.70 = bf16[1,1,1,1,144,1152]{5,4,3,2,1,0:T(8,128)(2,1)S(1)} collective-permute-done((bf16[1,1,1,1,144,1152]{5,4,3,2,1,0:T(8,128)(2,1)S(1)}, bf16[1,1,1,1,144,1152]{5,4,3,2,1,0:T(8,128)(2,1)S(1)}, u32[]{:S(2)}, u32[]{:S(2)}) %collective-permute-start.70) | collective-permute-done | bytes 331808 | tf_op jit(solution)/shard_map/ppermute | solution.py:79
  1098.6 13.9 %collective-permute-done.72 = bf16[2,1,1,1,1,112,1152]{6,5,4,3,2,1,0:T(8,128)(2,1)S(1)} collective-permute-done((bf16[2,1,1,1,1,112,1152]{6,5,4,3,2,1,0:T(8,128)(2,1)S(1)}, bf16[2,1,1,1,1,112,1152]{6,5,4,3,2,1,0:T(8,128)(2,1)S(1)}, u32[]{:S(2)}, u32[]{:S(2)}) %collective-permute-start.72) | collective-permute-done | bytes 516128 | tf_op jit(solution)/shard_map/ppermute | solution.py:79
  1116.7 11.7 collective-permute-done.73
  1148.7 14.8 %collective-permute-done.65 = bf16[1,2,1,1,144,1152]{5,4,3,2,1,0:T(8,128)(2,1)S(1)} collective-permute-done((bf16[1,2,1,1,144,1152]{5,4,3,2,1,0:T(8,128)(2,1)S(1)}, bf16[1,2,1,1,144,1152]{5,4,3,2,1,0:T(8,128)(2,1)S(1)}, u32[]{:S(2)}, u32[]{:S(2)}) %collective-permute-start.65) | collective-permute-done | bytes 663584 | tf_op jit(solution)/shard_map/ppermute | solution.py:79
  1163.6 24.0 %collective-permute-start.66 = (bf16[1,1,1,1,144,1152]{5,4,3,2,1,0:T(8,128)(2,1)S(1)}, bf16[1,1,1,1,144,1152]{5,4,3,2,1,0:T(8,128)(2,1)S(1)}, u32[]{:S(2)}, u32[]{:S(2)}) collective-permute-start(bf16[1,1,1,1,144,1152]{5,4,3,2,1,0:T(8,128)(2,1)S(1)} %dynamic-slice_convert_fusion.15), channel_id=1, source_target_pairs={{0,16},{1,17},{2,18},{3,19},{4,20},{5,21},{6,22},{7,23},{8,24},{9,... | collective-permute-start | bytes 995336 | tf_op jit(solution)/shard_map/ppermute | solution.py:79
  1189.8 10.5 collective-permute-done.66
  1210.9 14.4 %collective-permute-done.89 = f32[1,2]{1,0:T(1,128)S(1)} collective-permute-done((f32[1,2]{1,0:T(1,128)S(1)}, f32[1,2]{1,0:T(1,128)S(1)}, u32[]{:S(2)}, u32[]{:S(2)}) %collective-permute-start.89) | collective-permute-done | bytes 40 | tf_op jit(solution)/shard_map/ppermute | solution.py:79
  (1082 shorter events, 649.9 us)
Async XLA Ops:
  7.2 240.8 %all-gather.6.cloned.1.call-start = ((), (), s32[]{:S(2)}) async-start(), calls=%async_computation.3 | async-start | bytes 30412800 | tf_op jit(solution)/shard_map/all_gather | solution.py:852
  44.8 341.7 %all-gather.4.cloned.1.call-start = ((), (), s32[]{:S(2)}) async-start(), calls=%async_computation.2 | async-start | bytes 21897216 | tf_op jit(solution)/shard_map/all_gather | solution.py:860
  86.2 169.0 %collective-permute-start.32 = (bf16[128,2304]{1,0:T(8,128)(2,1)}, bf16[128,2304]{1,0:T(8,128)(2,1)}, u32[]{:S(2)}, u32[]{:S(2)}) collective-permute-start(bf16[128,2304]{1,0:T(8,128)(2,1)} %get-tuple-element.546), channel_id=1, source_target_pairs={{0,2},{1,3},{2,0},{3,1},{4,6},{5,7},{6,4},{7,5},{8,10},{9,11},{10,... | collective-permute-start | bytes 1769480 | tf_op jit(solution)/shard_map/ppermute | solution.py:79
  102.0 40.6 %collective-permute-start.24 = (bf16[2,48,1152]{2,1,0:T(8,128)(2,1)S(1)}, bf16[2,48,1152]{2,1,0:T(8,128)(2,1)S(1)}, u32[]{:S(2)}, u32[]{:S(2)}) collective-permute-start(bf16[2,48,1152]{2,1,0:T(8,128)(2,1)S(1)} %pad_maximum_fusion.23), channel_id=1, source_target_pairs={{0,16},{1,17},{2,18},{3,19},{4,20},{5,21},{6,22},{7,23},{8,24},{9,... | collective-permute-start | bytes 663560 | tf_op jit(solution)/shard_map/ppermute | solution.py:79
  463.2 60.8 %collective-permute-start.40 = (bf16[1,1,2,2,2,144,768]{6,5,4,3,2,1,0:T(8,128)(2,1)}, bf16[1,1,2,2,2,144,768]{6,5,4,3,2,1,0:T(8,128)(2,1)}, u32[]{:S(2)}, u32[]{:S(2)}) collective-permute-start(bf16[1,1,2,2,2,144,768]{6,5,4,3,2,1,0:T(8,128)(2,1)} %slice.653), channel_id=1, source_target_pairs={{0,2},{1,3},{2,0},{3,1},{4,6},{5,7},{6,4},{7,5},{8,10},{9,11},{10,... | collective-permute-start | bytes 5308424 | tf_op jit(solution)/shard_map/ppermute | solution.py:79
  554.5 79.1 %collective-permute-start.43 = (f32[2,10,2880]{2,0,1:T(2,128)}, f32[2,10,2880]{2,0,1:T(2,128)}, u32[]{:S(2)}, u32[]{:S(2)}) collective-permute-start(f32[2,10,2880]{2,0,1:T(2,128)} %reshape.1223), channel_id=1, source_target_pairs={{0,1},{1,0},{2,3},{3,2},{4,5},{5,4},{6,7},{7,6},{8,9},{9,8},{10,11... | collective-permute-start | bytes 691208 | tf_op jit(solution)/shard_map/ppermute | solution.py:79
  554.5 79.1 %collective-permute-start.44 = (bf16[1,1,2,2,1,144,768]{6,5,4,3,2,1,0:T(8,128)(2,1)}, bf16[1,1,2,2,1,144,768]{6,5,4,3,2,1,0:T(8,128)(2,1)}, u32[]{:S(2)}, u32[]{:S(2)}) collective-permute-start(bf16[1,1,2,2,1,144,768]{6,5,4,3,2,1,0:T(8,128)(2,1)} %dynamic-slice_convert_fusion.7), channel_id=1, source_target_pairs={{0,4},{1,5},{2,6},{3,7},{4,0},{5,1},{6,2},{7,3},{8,12},{9,13},{10,... | collective-permute-start | bytes 2654216 | tf_op jit(solution)/shard_map/ppermute | solution.py:79
  588.9 44.7 %collective-permute-start.45 = (bf16[1,2,2,2,1,144,768]{6,5,4,3,2,1,0:T(8,128)(2,1)}, bf16[1,2,2,2,1,144,768]{6,5,4,3,2,1,0:T(8,128)(2,1)S(1)}, u32[]{:S(2)}, u32[]{:S(2)}) collective-permute-start(bf16[1,2,2,2,1,144,768]{6,5,4,3,2,1,0:T(8,128)(2,1)} %dynamic-slice_convert_fusion.3), channel_id=1, source_target_pairs={{0,4},{1,5},{2,6},{3,7},{4,0},{5,1},{6,2},{7,3},{8,12},{9,13},{10,... | collective-permute-start | bytes 5308424 | tf_op jit(solution)/shard_map/ppermute | solution.py:79
  589.5 44.1 %collective-permute-start.46 = (bf16[1,1,2,2,2,144,768]{6,5,4,3,2,1,0:T(8,128)(2,1)}, bf16[1,1,2,2,2,144,768]{6,5,4,3,2,1,0:T(8,128)(2,1)S(1)}, u32[]{:S(2)}, u32[]{:S(2)}) collective-permute-start(bf16[1,1,2,2,2,144,768]{6,5,4,3,2,1,0:T(8,128)(2,1)} %slice.652), channel_id=1, source_target_pairs={{0,2},{1,3},{2,0},{3,1},{4,6},{5,7},{6,4},{7,5},{8,10},{9,11},{10,... | collective-permute-start | bytes 5308424 | tf_op jit(solution)/shard_map/ppermute | solution.py:79
  662.8 44.7 %collective-permute-start.48 = (f32[2,10,2880]{2,0,1:T(2,128)S(1)}, f32[2,10,2880]{2,0,1:T(2,128)S(1)}, u32[]{:S(2)}, u32[]{:S(2)}) collective-permute-start(f32[2,10,2880]{2,0,1:T(2,128)S(1)} %add.1257), channel_id=1, source_target_pairs={{0,2},{1,3},{2,0},{3,1},{4,6},{5,7},{6,4},{7,5},{8,10},{9,11},{10,... | collective-permute-start | bytes 691208 | tf_op jit(solution)/shard_map/ppermute | solution.py:79
  663.4 44.1 %collective-permute-start.50 = (bf16[1,1,2,1,1,144,768]{6,5,4,3,2,1,0:T(8,128)(2,1)}, bf16[1,1,2,1,1,144,768]{6,5,4,3,2,1,0:T(8,128)(2,1)}, u32[]{:S(2)}, u32[]{:S(2)}) collective-permute-start(bf16[1,1,2,1,1,144,768]{6,5,4,3,2,1,0:T(8,128)(2,1)} %dynamic-slice_convert_fusion.13), channel_id=1, source_target_pairs={{0,8},{1,9},{2,10},{3,11},{4,12},{5,13},{6,14},{7,15},{8,0},{9,1},... | collective-permute-start | bytes 1327112 | tf_op jit(solution)/shard_map/ppermute | solution.py:79
  665.0 42.5 %collective-permute-start.51 = (bf16[1,1,2,2,1,144,768]{6,5,4,3,2,1,0:T(8,128)(2,1)}, bf16[1,1,2,2,1,144,768]{6,5,4,3,2,1,0:T(8,128)(2,1)}, u32[]{:S(2)}, u32[]{:S(2)}) collective-permute-start(bf16[1,1,2,2,1,144,768]{6,5,4,3,2,1,0:T(8,128)(2,1)} %slice.655), channel_id=1, source_target_pairs={{0,2},{1,3},{2,0},{3,1},{4,6},{5,7},{6,4},{7,5},{8,10},{9,11},{10,... | collective-permute-start | bytes 2654216 | tf_op jit(solution)/shard_map/ppermute | solution.py:79
  666.5 41.1 %collective-permute-start.52 = (bf16[1,1,2,2,1,144,768]{6,5,4,3,2,1,0:T(8,128)(2,1)}, bf16[1,1,2,2,1,144,768]{6,5,4,3,2,1,0:T(8,128)(2,1)}, u32[]{:S(2)}, u32[]{:S(2)}) collective-permute-start(bf16[1,1,2,2,1,144,768]{6,5,4,3,2,1,0:T(8,128)(2,1)} %dynamic-slice_convert_fusion.6), channel_id=1, source_target_pairs={{0,4},{1,5},{2,6},{3,7},{4,0},{5,1},{6,2},{7,3},{8,12},{9,13},{10,... | collective-permute-start | bytes 2654216 | tf_op jit(solution)/shard_map/ppermute | solution.py:79
  735.5 59.4 %collective-permute-start.58 = (bf16[1,2,2,2,144,1152]{5,4,3,2,1,0:T(8,128)(2,1)}, bf16[1,2,2,2,144,1152]{5,4,3,2,1,0:T(8,128)(2,1)}, u32[]{:S(2)}, u32[]{:S(2)}) collective-permute-start(bf16[1,2,2,2,144,1152]{5,4,3,2,1,0:T(8,128)(2,1)} %slice.651), channel_id=1, source_target_pairs={{0,2},{1,3},{2,0},{3,1},{4,6},{5,7},{6,4},{7,5},{8,10},{9,11},{10,... | collective-permute-start | bytes 7962632 | tf_op jit(solution)/shard_map/ppermute | solution.py:79
  848.9 75.2 %collective-permute-start.68 = (bf16[2,2,1,2,1,112,1152]{6,5,4,3,2,1,0:T(8,128)(2,1)}, bf16[2,2,1,2,1,112,1152]{6,5,4,3,2,1,0:T(8,128)(2,1)}, u32[]{:S(2)}, u32[]{:S(2)}) collective-permute-start(bf16[2,2,1,2,1,112,1152]{6,5,4,3,2,1,0:T(8,128)(2,1)} %dynamic-slice_convert_fusion.2), channel_id=1, source_target_pairs={{0,4},{1,5},{2,6},{3,7},{4,0},{5,1},{6,2},{7,3},{8,12},{9,13},{10,... | collective-permute-start | bytes 6193160 | tf_op jit(solution)/shard_map/ppermute | solution.py:79
  856.9 98.3 %collective-permute-start.94 = (f32[2,10,2880]{2,0,1:T(2,128)}, f32[2,10,2880]{2,0,1:T(2,128)}, u32[]{:S(2)}, u32[]{:S(2)}) collective-permute-start(f32[2,10,2880]{2,0,1:T(2,128)} %add.1327), channel_id=1, source_target_pairs={{0,16},{1,17},{2,18},{3,19},{4,20},{5,21},{6,22},{7,23},{8,24},{9,... | collective-permute-start | bytes 691208 | tf_op jit(solution)/shard_map/ppermute | solution.py:79
  999.1 86.5 %collective-permute-start.71 = (bf16[2,2,1,1,1,112,1152]{6,5,4,3,2,1,0:T(8,128)(2,1)}, bf16[2,2,1,1,1,112,1152]{6,5,4,3,2,1,0:T(8,128)(2,1)}, u32[]{:S(2)}, u32[]{:S(2)}) collective-permute-start(bf16[2,2,1,1,1,112,1152]{6,5,4,3,2,1,0:T(8,128)(2,1)} %dynamic-slice_convert_fusion.5), channel_id=1, source_target_pairs={{0,2},{1,3},{2,0},{3,1},{4,6},{5,7},{6,4},{7,5},{8,10},{9,11},{10,... | collective-permute-start | bytes 3096584 | tf_op jit(solution)/shard_map/ppermute | solution.py:79
  999.7 113.0 %collective-permute-start.63 = (bf16[2,2,2,1,144,1152]{5,4,3,2,1,0:T(8,128)(2,1)}, bf16[2,2,2,1,144,1152]{5,4,3,2,1,0:T(8,128)(2,1)}, u32[]{:S(2)}, u32[]{:S(2)}) collective-permute-start(bf16[2,2,2,1,144,1152]{5,4,3,2,1,0:T(8,128)(2,1)} %dynamic-slice_convert_fusion.1), channel_id=1, source_target_pairs={{0,4},{1,5},{2,6},{3,7},{4,0},{5,1},{6,2},{7,3},{8,12},{9,13},{10,... | collective-permute-start | bytes 7962632 | tf_op jit(solution)/shard_map/ppermute | solution.py:79
  1000.4 63.1 %collective-permute-start.96 = (f32[73,1152]{1,0:T(8,128)S(1)}, f32[73,1152]{1,0:T(8,128)S(1)}, u32[]{:S(2)}, u32[]{:S(2)}) collective-permute-start(f32[73,1152]{1,0:T(8,128)S(1)} %add.1347), channel_id=1, source_target_pairs={{0,2},{1,3},{2,0},{3,1},{4,6},{5,7},{6,4},{7,5},{8,10},{9,11},{10,... | collective-permute-start | bytes 1009160 | tf_op jit(solution)/shard_map/ppermute | solution.py:79
  1003.5 56.7 %collective-permute-start.85 = (f32[2,8,1152]{2,1,0:T(8,128)S(1)}, f32[2,8,1152]{2,1,0:T(8,128)S(1)}, u32[]{:S(2)}, u32[]{:S(2)}) collective-permute-start(f32[2,8,1152]{2,1,0:T(8,128)S(1)} %pad_maximum_fusion.27), channel_id=1, source_target_pairs={{0,4},{1,5},{2,6},{3,7},{4,0},{5,1},{6,2},{7,3},{8,12},{9,13},{10,... | collective-permute-start | bytes 221192 | tf_op jit(solution)/shard_map/ppermute | solution.py:79
  1134.9 52.7 %collective-permute-start.78 = (f32[112,1152]{1,0:T(8,128)S(1)}, f32[112,1152]{1,0:T(8,128)S(1)}, u32[]{:S(2)}, u32[]{:S(2)}) collective-permute-start(f32[112,1152]{1,0:T(8,128)S(1)} %add_bitcast_fusion.2), channel_id=1, source_target_pairs={{7,5},{30,12}} | collective-permute-start | bytes 1548296 | tf_op jit(solution)/shard_map/ppermute | solution.py:164
  1203.0 56.6 %collective-permute-start.100 = (f32[2,144,288]{2,1,0:T(8,128)}, f32[2,144,288]{2,1,0:T(8,128)}, u32[]{:S(2)}, u32[]{:S(2)}) collective-permute-start(f32[2,144,288]{2,1,0:T(8,128)} %get-tuple-element.538), channel_id=1, source_target_pairs={{0,1},{1,0},{2,3},{3,2},{4,5},{5,4},{6,7},{7,6},{8,9},{9,8},{10,11... | collective-permute-start | bytes 995336 | tf_op jit(solution)/shard_map/ppermute | solution.py:79
  1203.0 56.6 %collective-permute-start.101 = (f32[2,144,288]{2,1,0:T(8,128)}, f32[2,144,288]{2,1,0:T(8,128)}, u32[]{:S(2)}, u32[]{:S(2)}) collective-permute-start(f32[2,144,288]{2,1,0:T(8,128)} %get-tuple-element.539), channel_id=1, source_target_pairs={{0,2},{1,3},{2,0},{3,1},{4,6},{5,7},{6,4},{7,5},{8,10},{9,11},{10,... | collective-permute-start | bytes 995336 | tf_op jit(solution)/shard_map/ppermute | solution.py:79
  1204.5 55.1 %collective-permute-start.102 = (f32[2,144,288]{2,1,0:T(8,128)}, f32[2,144,288]{2,1,0:T(8,128)}, u32[]{:S(2)}, u32[]{:S(2)}) collective-permute-start(f32[2,144,288]{2,1,0:T(8,128)} %get-tuple-element.540), channel_id=1, source_target_pairs={{0,3},{1,2},{2,1},{3,0},{4,7},{5,6},{6,5},{7,4},{8,11},{9,10},{10,... | collective-permute-start | bytes 995336 | tf_op jit(solution)/shard_map/ppermute | solution.py:79
  (334 other events, 6058.3 us)
Sparse Core Ops, SparseCore 0:
  44.9 203.0 all-gather.5
  251.5 135.0 all-gather.3

commit v2 on v1

--- a/solution.py
+++ b/solution.py
@@ -140,7 +140,8 @@
 
 def chunk_of(place, rows):
     chunk = -(-rows // place.n)
-    return -(-chunk // 8) * 8
+    unit = 128 if chunk > 64 else 8
+    return -(-chunk // unit) * unit
 
 
 def spread_rows(place, held, low, rows):
@@ -161,7 +162,7 @@
     chunk = block.shape[0]
     first = (owner_rows * place.me - low) // chunk
     got = [
-        lax.ppermute(block, AXES, [(target, owner) for owner, target in pairs])
+        wide(lax.ppermute(bf(block), AXES, [(target, owner) for owner, target in pairs]))
         for pairs in spread_table(place, owner_rows, low, chunk)
     ]
     start = owner_rows * place.me - low - chunk * first
@@ -265,21 +266,33 @@
         self.moving = self.place.swap(self.sends, self.mask)
         self.sends = None
 
+    def part(self, take):
+        return take(self.keep) + wide(take(self.moving))
+
     def land(self):
-        total = self.keep + wide(self.moving)
-        self.moving = None
         if not self.stages:
-            self.keep = total
+            self.keep = self.part(lambda value: value)
+            self.moving = None
             return
         kind, axis, self.mask = self.stages.pop(0)
         if kind == "rel":
-            away = lax.slice_in_dim(total, 1, 2, axis=axis)
-            self.keep = lax.slice_in_dim(total, 0, 1, axis=axis)
+            away = self.part(lambda value: lax.slice_in_dim(value, 1, 2, axis=axis))
+            keep = self.part(lambda value: lax.slice_in_dim(value, 0, 1, axis=axis))
         else:
             bit = self.place.bit(self.mask)
-            away = lax.dynamic_slice_in_dim(total, 1 - bit, 1, axis)
-            self.keep = lax.dynamic_slice_in_dim(total, bit, 1, axis)
-        self.sends = bf(away)
+            away = self.part(lambda value: lax.dynamic_slice_in_dim(value, 1 - bit, 1, axis))
+            keep = self.part(lambda value: lax.dynamic_slice_in_dim(value, bit, 1, axis))
+        self.sends, self.keep, self.moving = bf(away), keep, None
+
+    def split(self, axis, orders):
+        flows = []
+        for i, order in enumerate(orders):
+            flow = Flow.__new__(Flow)
+            flow.place, flow.stages, flow.sends = self.place, list(order), None
+            flow.keep = lax.slice_in_dim(self.keep, i, i + 1, axis=axis)
+            flow.moving = lax.slice_in_dim(self.moving, i, i + 1, axis=axis)
+            flows.append(flow)
+        return flows
 
     def drain(self):
         while self.moving is not None:
@@ -306,6 +319,7 @@
 CB = 256
 ROW = SIDE
 LIMIT = 48 * 1024 * 1024
+QUICK = pl.CostEstimate(flops=2**20, bytes_accessed=2**16, transcendentals=0)
 
 
 def whole_spec(shape):
@@ -407,9 +421,7 @@
         compiler_params=pltpu.CompilerParams(
             dimension_semantics=("arbitrary",), vmem_limit_bytes=LIMIT
         ),
-        cost_estimate=pl.CostEstimate(
-            flops=2 * n_ext * D * FFP * 3, bytes_accessed=50 * 2**20, transcendentals=n_ext * FFP * 3
-        ),
+        cost_estimate=QUICK,
     )(x_ext, ffw, ffw, ffw, taps, left_ok, right_ok, on)
 
 
@@ -524,9 +536,7 @@
         compiler_params=pltpu.CompilerParams(
             dimension_semantics=("arbitrary",), vmem_limit_bytes=LIMIT
         ),
-        cost_estimate=pl.CostEstimate(
-            flops=2 * n_ext * D * FFP * 3, bytes_accessed=50 * 2**20, transcendentals=n_ext * FFP * 3
-        ),
+        cost_estimate=QUICK,
     )(d_ext, ffw, ffw, ffw, upper, z, z_halo, taps, left_ok, right_ok, on)
 
 
@@ -534,12 +544,12 @@
     out_ref[0, 0] = mm_tn(left_ref[...], right_ref[0]).astype(out_ref.dtype)
 
 
-def ff_grad(spot, left, right, away, dtype):
+def ff_grad(spot, left, right, which, away, dtype):
     n_tok = left.shape[0]
-    count = right.shape[0]
+    count = 1
 
     def lanes(k, r, spot_ref):
-        return (k, 0, (spot_ref[1] + away) % 2 * 2 + (spot_ref[0] + r) % 2)
+        return (which, 0, (spot_ref[1] + away) % 2 * 2 + (spot_ref[0] + r) % 2)
 
     return pl.pallas_call(
         ff_grad_kernel,
@@ -556,9 +566,7 @@
         compiler_params=pltpu.CompilerParams(
             dimension_semantics=("arbitrary", "arbitrary"), vmem_limit_bytes=LIMIT
         ),
-        cost_estimate=pl.CostEstimate(
-            flops=4 * count * n_tok * D * FFB, bytes_accessed=6 * count * D * FFB, transcendentals=0
-        ),
+        cost_estimate=QUICK,
     )(spot, left, right)
 
 
@@ -590,9 +598,371 @@
         compiler_params=pltpu.CompilerParams(
             dimension_semantics=("arbitrary",), vmem_limit_bytes=LIMIT
         ),
-        cost_estimate=pl.CostEstimate(
-            flops=4 * n_tok * D * D, bytes_accessed=16 * D * D, transcendentals=0
+        cost_estimate=QUICK,
+    )(spot, *arrays)
+
+
+class Course:
+    def __init__(self, flow):
+        shape = flow.keep.shape
+        self.block = shape[-2:]
+        self.count = math.prod(shape[:-2])
+        self.sends = flow.sends.reshape((self.count,) + self.block)
+        self.keep = flow.keep.reshape((self.count,) + self.block)
+        self.first = flow.mask
+        self.stages = [
+            (kind, math.prod(shape[axis + 1 : -2]), mask) for kind, axis, mask in flow.stages
+        ]
+
+    def sizes(self):
+        return [self.count >> i for i in range(len(self.stages) + 1)]
+
+
+def finish_kernel(n_mp, courses, top, sum_masks, gather_masks, *refs):
+    count = len(courses)
+    dp, mp = lax.axis_index("dp"), lax.axis_index("mp")
+
+    def bit(mask):
+        return mp // mask % 2 if mask < n_mp else dp // (mask // n_mp) % 2
+
+    def partner(mask):
+        if mask < n_mp:
+            return {"mp": mp + mask * (1 - 2 * bit(mask))}
+        return {"dp": dp + mask // n_mp * (1 - 2 * bit(mask))}
+
+    sends, keeps = refs[:count], refs[count : 2 * count]
+    part_ref, mine_ref, scalar_ref = refs[2 * count : 2 * count + 3]
+    join_ref, cap_ref, sum_ref, all_ref, total_ref = refs[2 * count + 3 : 2 * count + 8]
+    scratch = list(refs[2 * count + 8 :])
+    (
+        send_sem, recv_sem, sum_send, sum_recv, all_send, all_recv, one_send, one_recv,
+        join_send, join_recv
+    ) = scratch[-10:]
+    sum_got, sum_buf, owns, cap_owns, one_got, one_buf, join_buf = scratch[-17:-10]
+    merges = [
+        (owns, owns.at[3], scratch[-21], scratch[-20]),
+        (cap_owns, cap_ref, scratch[-19], scratch[-18]),
+    ]
+    outs = [owns.at[0], owns.at[1], cap_owns.at[0], cap_owns.at[1], owns.at[2]]
+    accs, gots, packs = [], [], []
+    for course in courses:
+        accs.append(scratch.pop(0))
+        gots.append([scratch.pop(0) for _ in course.sizes()])
+        packs.append([None] + [scratch.pop(0) for _ in course.sizes()[1:]])
+
+    def across():
+        return {"mp": mp + 1 - 2 * bit(1) + 2 * (1 - 2 * bit(2))}
+
+    barrier = pltpu.get_barrier_semaphore()
+    for target in [partner(mask) for mask in sum_masks] + [across()]:
+        pl.semaphore_signal(
+            barrier, inc=1, device_id=target, device_id_type=pl.DeviceIdType.MESH
+        )
+    pl.semaphore_wait(barrier, len(sum_masks) + 1)
+
+    def copy(f, stage):
+        course = courses[f]
+        mask = course.first if stage == 0 else course.stages[stage - 1][2]
+        return pltpu.make_async_remote_copy(
+            src_ref=sends[f] if stage == 0 else packs[f][stage],
+            dst_ref=gots[f][stage],
+            send_sem=send_sem.at[f, stage],
+            recv_sem=recv_sem.at[f, stage],
+            device_id=partner(mask),
+            device_id_type=pl.DeviceIdType.MESH,
+        )
+
+    def each_rows(rows, act):
+        if rows % 16:
+            act(slice(None))
+        else:
+
+            @pl.loop(0, rows // 16)
+            def _(i):
+                act(pl.ds(pl.multiple_of(i * 16, 16), 16))
+
+    def spots(strides, at):
+        found = [(at, 0)]
+        for stride in strides:
+            found = [
+                (block + value * stride, slot * 2 + value)
+                for block, slot in found for value in (0, 1)
+            ]
+        return found
+
+    def absorb(f, stage, fixed, strides):
+        course = courses[f]
+        base = keeps[f] if stage == 0 else accs[f]
+        got = gots[f][stage]
+        rows = course.block[0]
+        if stage == len(course.stages):
+
+            def close(at):
+                outs[f][at, :] = base[fixed, at, :] + wide(got[0, at, :])
+
+            each_rows(rows, close)
+            return None
+        kind, cut, mask = course.stages[stage]
+        own = bit(mask) if kind == "abs" else 0
+        other = 1 - own
+        place_of = strides.index(cut)
+        weight = 1 << (len(strides) - 1 - place_of)
+        rest = [stride for stride in strides if stride != cut]
+
+        for number, (block, slot) in enumerate(spots(rest, fixed)):
+            low = slot % weight
+            slot = (slot // weight) * 2 * weight + low
+
+            def act(at, block=block, slot=slot, number=number):
+                packs[f][stage + 1][number, at, :] = bf(
+                    base[block + other * cut, at, :] + wide(got[slot + other * weight, at, :])
+                )
+
+            each_rows(rows, act)
+        copy(f, stage + 1).start()
+        for number, (block, slot) in enumerate(spots(rest, fixed)):
+            low = slot % weight
+            slot = (slot // weight) * 2 * weight + low
+
+            def act(at, block=block, slot=slot):
+                accs[f][block + own * cut, at, :] = (
+                    base[block + own * cut, at, :] + wide(got[slot + own * weight, at, :])
+                )
+
+            each_rows(rows, act)
+        return fixed + own * cut, rest
+
+    def sum_copy(stage):
+        return pltpu.make_async_remote_copy(
+            src_ref=part_ref if stage == 0 else sum_buf.at[stage - 1],
+            dst_ref=sum_got.at[stage],
+            send_sem=sum_send.at[stage],
+            recv_sem=sum_recv.at[stage],
+            device_id=partner(sum_masks[stage]),
+            device_id_type=pl.DeviceIdType.MESH,
+        )
+
+    def all_copy(stage):
+        held = canvas // (1 << stage) * (1 << stage)
+        return pltpu.make_async_remote_copy(
+            src_ref=mine_ref if stage == 0 else all_ref.at[pl.ds(held, 1 << stage)],
+            dst_ref=all_ref.at[pl.ds(held, 1 << stage)],
+            send_sem=all_send.at[stage],
+            recv_sem=all_recv.at[stage],
+            device_id=partner(gather_masks[stage]),
+            device_id_type=pl.DeviceIdType.MESH,
+        )
+
+    def merge_copy(pair):
+        return pltpu.make_async_remote_copy(
+            src_ref=merges[pair][2],
+            dst_ref=merges[pair][3],
+            send_sem=send_sem.at[2 * pair, merge_at[pair] + 1],
+            recv_sem=recv_sem.at[2 * pair, merge_at[pair] + 1],
+            device_id=partner(top),
+            device_id_type=pl.DeviceIdType.MESH,
+        )
+
+    def one_copy(stage):
+        return pltpu.make_async_remote_copy(
+            src_ref=one_buf.at[stage],
+            dst_ref=one_got.at[stage],
+            send_sem=one_send.at[stage],
+            recv_sem=one_recv.at[stage],
+            device_id=partner(sum_masks[stage]),
+            device_id_type=pl.DeviceIdType.MESH,
+        )
+
+    def join_copy(number):
+        return pltpu.make_async_remote_copy(
+            src_ref=join_buf.at[number],
+            dst_ref=join_ref.at[mp],
+            send_sem=join_send.at[number],
+            recv_sem=join_recv.at[number],
+            device_id=across() if number == 2 else partner(number + 1),
+            device_id_type=pl.DeviceIdType.MESH,
+        )
+
+    def lanes_of(number):
+        cols = D // 4
+
+        def cut(ref):
+            value = ref[:, :cols]
+            for m in range(1, 4):
+                value = jnp.where(number == m, ref[:, m * cols : (m + 1) * cols], value)
+            return value
+
+        return cut
+
+    merge_at = [len(courses[0].stages), len(courses[2].stages)]
+    canvas = dp * 2 + mp // 2
+    sum_copy(0).start()
+    all_copy(0).start()
+    state = []
+    turns = (0, 1, 4, 2, 3)
+    lag = (0, 0, 1, 1, 0)
+    for f, course in enumerate(courses):
+        if not lag[f]:
+            copy(f, 0).start()
+        strides = [course.count >> (i + 1) for i in range(course.count.bit_length() - 1)]
+        state.append((0, strides))
+    all_ref[pl.ds(canvas, 1)] = mine_ref[...]
+    high = bit(top) == 1
+    for turn in range(max(len(sum_masks), *[len(course.stages) + 3 for course in courses])):
+        for f in turns:
+            stage = turn - lag[f]
+            if stage == -1:
+                copy(f, 0).start()
+            elif stage <= len(courses[f].stages):
+                copy(f, stage).wait_recv()
+                state[f] = absorb(f, stage, *state[f])
+            if f % 2 == 1 and stage == merge_at[f // 2]:
+                both, _, pack, _ = merges[f // 2]
+                pack[...] = bf(jnp.where(high, both[0], both[1]))
+                merge_copy(f // 2).start()
+        for pair, (both, own, pack, came) in enumerate(merges):
+            if turn == merge_at[pair] + lag[2 * pair] + 1:
+                merge_copy(pair).wait_recv()
+                own[...] = jnp.where(high, both[1], both[0]) + wide(came[...])
+        if turn < len(sum_masks):
+            sum_copy(turn).wait_recv()
+            total = (part_ref[...] if turn == 0 else sum_buf[turn - 1]) + sum_got[turn]
+            if turn + 1 < len(sum_masks):
+                sum_buf[turn] = total
+                sum_copy(turn + 1).start()
+            else:
+                sum_ref[...] = total
+        if turn < len(gather_masks):
+            all_copy(turn).wait_recv()
+            if turn + 1 < len(gather_masks):
+                all_copy(turn + 1).start()
+    square = jnp.sum(owns[2] * owns[2]) + jnp.sum(owns[3] * owns[3])
+    square = square + jnp.sum(cap_ref[...] * cap_ref[...])
+    row = lax.broadcasted_iota(jnp.int32, (8, 128), 0)
+    one_buf[0] = scalar_ref[...] + jnp.where(row == 0, square, 0.0)
+    one_copy(0).start()
+    b0, b1 = bit(1), bit(2)
+    for number, (f0, f1) in enumerate(((1, 0), (0, 1), (1, 1))):
+        other = b0 + f0 * (1 - 2 * b0) + 2 * (b1 + f1 * (1 - 2 * b1))
+        cut = lanes_of(other)
+        join_buf[number, 0] = cut(owns.at[3])
+        join_buf[number, 1] = cut(owns.at[2])
+        join_copy(number).start()
+    cut = lanes_of(mp)
+    join_ref[mp, 0] = cut(owns.at[3])
+    join_ref[mp, 1] = cut(owns.at[2])
+    for stage in range(len(sum_masks)):
+        one_copy(stage).wait_recv()
+        total = one_buf[stage] + one_got[stage]
+        if stage + 1 < len(sum_masks):
+            one_buf[stage + 1] = total
+            one_copy(stage + 1).start()
+        else:
+            total_ref[...] = total
+    for number in range(3):
+        join_copy(number).wait_recv()
+        join_copy(number).wait_send()
+    for stage in range(len(sum_masks)):
+        one_copy(stage).wait_send()
+        sum_copy(stage).wait_send()
+    for stage in range(len(gather_masks)):
+        all_copy(stage).wait_send()
+    for pair in range(2):
+        merge_copy(pair).wait_send()
+    for f, course in enumerate(courses):
+        for stage in range(len(course.stages) + 1):
+            copy(f, stage).wait_send()
+
+
+def finish(n_mp, flows, top, masks, part, mine, scalars):
+    budget = 3000
+    height = lambda flow: flow.keep.size // D // flow.keep.shape[-2] * (-(-flow.keep.shape[-2] // 16) * 16)
+    while sum(height(flow) for flow in flows) > budget:
+        flow = max(flows, key=height)
+        flow.launch()
+        flow.land()
+    courses = [Course(flow) for flow in flows]
+    canvases = 1 << len(masks) - 1
+    scratch = []
+    for course in courses:
+        scratch.append(pltpu.VMEM((course.count,) + course.block, F32))
+        scratch += [pltpu.VMEM((size,) + course.block, BF16) for size in course.sizes()]
+        scratch += [pltpu.VMEM((size,) + course.block, BF16) for size in course.sizes()[1:]]
+    most = max(len(course.stages) for course in courses) + 2
+    late = courses[0].block
+    for block in (late, courses[2].block):
+        scratch += [pltpu.VMEM(block, BF16), pltpu.VMEM(block, BF16)]
+    scratch += [
+        pltpu.VMEM((len(masks),) + part.shape, F32),
+        pltpu.VMEM((len(masks) - 1,) + part.shape, F32),
+        pltpu.VMEM((4,) + late, F32),
+        pltpu.VMEM((2,) + courses[2].block, F32),
+        pltpu.VMEM((len(masks), 8, 128), F32),
+        pltpu.VMEM((len(masks), 8, 128), F32),
+        pltpu.VMEM((3, 2, late[0], D // 4), F32),
+    ]
+    scratch += [pltpu.SemaphoreType.DMA((len(courses), most))] * 2
+    scratch += [pltpu.SemaphoreType.DMA((len(masks),))] * 6
+    scratch += [pltpu.SemaphoreType.DMA((3,))] * 2
+    plan = [
+        Plan(course.count, course.block, course.first, tuple(course.stages)) for course in courses
+    ]
+    vmem = pl.BlockSpec(memory_space=pltpu.VMEM)
+    outs = [(4, 2, late[0], D // 4), courses[2].block, part.shape]
+    outs += [(canvases,) + mine.shape[1:], (8, 128)]
+    return pl.pallas_call(
+        partial(finish_kernel, n_mp, plan, top, masks, masks[1:]),
+        in_specs=[pl.BlockSpec(memory_space=pl.ANY)] * len(courses) + [vmem] * (len(courses) + 3),
+        out_specs=[vmem] * len(outs),
+        out_shape=[jax.ShapeDtypeStruct(shape, F32) for shape in outs],
+        scratch_shapes=scratch,
+        compiler_params=pltpu.CompilerParams(
+            collective_id=0, has_side_effects=True, vmem_limit_bytes=58 * 1024 * 1024
         ),
+    )(*[course.sends for course in courses], *[course.keep for course in courses], part, mine, scalars)
+
+
+class Plan:
+    def __init__(self, count, block, first, stages):
+        self.count, self.block, self.first, self.stages = count, block, first, stages
+
+    def sizes(self):
+        return [self.count >> i for i in range(len(self.stages) + 1)]
+
+
+def cap_grad_kernel(away, spot_ref, cap_ref, act_ref, dcap_ref, draw_ref, out_ref):
+    block = pl.program_id(0) * 2 + (spot_ref[1] + away) % 2
+    first, both = cap_ref.shape[1] // GL, (cap_ref.shape[1] + act_ref.shape[1]) // GL
+
+    @pl.when(block < first)
+    def _():
+        rows = pl.ds(pl.multiple_of(block * GL, GL), GL)
+        out_ref[0] = mm_tn(cap_ref[:, rows], dcap_ref[...]).astype(out_ref.dtype)
+
+    @pl.when((block >= first) & (block < both))
+    def _():
+        rows = pl.ds(pl.multiple_of((block - first) * GL, GL), GL)
+        out_ref[0] = mm_tn(act_ref[:, rows], draw_ref[...]).astype(out_ref.dtype)
+
+    @pl.when(block >= both)
+    def _():
+        out_ref[0] = jnp.zeros((GL, D), out_ref.dtype)
+
+
+def cap_grad(spot, arrays, blocks, away, dtype):
+    return pl.pallas_call(
+        partial(cap_grad_kernel, away),
+        grid_spec=pltpu.PrefetchScalarGridSpec(
+            num_scalar_prefetch=1,
+            grid=(blocks // 2,),
+            in_specs=[pl.BlockSpec(a.shape, lambda j, spot_ref: (0, 0)) for a in arrays],
+            out_specs=pl.BlockSpec((1, GL, D), lambda j, spot_ref: (j, 0, 0)),
+        ),
+        out_shape=jax.ShapeDtypeStruct((blocks // 2, GL, D), dtype),
+        compiler_params=pltpu.CompilerParams(
+            dimension_semantics=("arbitrary",), vmem_limit_bytes=LIMIT
+        ),
+        cost_estimate=QUICK,
     )(spot, *arrays)
 
 
@@ -643,10 +1013,7 @@
         compiler_params=pltpu.CompilerParams(
             dimension_semantics=("arbitrary",), vmem_limit_bytes=LIMIT
         ),
-        cost_estimate=pl.CostEstimate(
-            flops=4 * n_tok * n_txt * WIN * XHEADS, bytes_accessed=5 * 2**20,
-            transcendentals=n_tok * n_txt * XHEADS
-        ),
+        cost_estimate=QUICK,
     )(q, keys, values, token_seg, text_seg)
 
 
@@ -697,10 +1064,7 @@
         compiler_params=pltpu.CompilerParams(
             dimension_semantics=("arbitrary",), vmem_limit_bytes=LIMIT
         ),
-        cost_estimate=pl.CostEstimate(
-            flops=10 * n_tok * n_txt * WIN * XHEADS, bytes_accessed=12 * 2**20,
-            transcendentals=n_tok * n_txt * XHEADS
-        ),
+        cost_estimate=QUICK,
     )(q, keys, values, d_cross, token_seg, text_seg)
 
 
@@ -813,9 +1177,7 @@
         compiler_params=pltpu.CompilerParams(
             dimension_semantics=("arbitrary",), vmem_limit_bytes=LIMIT
         ),
-        cost_estimate=pl.CostEstimate(
-            flops=16 * n_tok * D * GL, bytes_accessed=8 * 2**20, transcendentals=0
-        ),
+        cost_estimate=QUICK,
     )
 
 
@@ -1015,6 +1377,7 @@
     d_shift_seg, d_shift_o = by_segment(d_final)
     d_scale_seg, d_scale_o = by_segment(d_final * hat_o)
     d_emb_mine = d_shift_seg + d_scale_seg
+    d_emb = d_emb_mine + place.swap(d_emb_mine, 1)
     d_state_f = layer_norm_back(d_final * (1.0 + scale_o), hat_o, inv_o)
 
     split_dp = (2,) * place.dp_bits
@@ -1025,17 +1388,18 @@
             "x": ("abs", lead + place.dp_bits - 1, place.x_mask),
             "y": ("rel", lead - 1, 2),
         }
-        return [table[o] for o in order] + [("abs", lead + axis, mask) for axis, mask in far]
+        rest = [("abs", lead + axis, mask) for axis, mask in far]
+        return [table[o] if o in table else rest.pop(0) for o in order] + rest
 
     def ff_flow(left, right, orders):
         shape = (1, 2) + split_dp + (dl, FFB)
-        away = ff_grad(spot, left, right, 1, BF16)
-        flows = [
-            Flow(place, away[i].reshape(shape), stages(2, order)) for i, order in enumerate(orders)
-        ]
-        left, right, away = lax.optimization_barrier((left, right, away))
+        flows = []
+        for i, order in enumerate(orders):
+            away = ff_grad(spot, left, right, i, 1, BF16)
+            flows.append(Flow(place, away.reshape(shape), stages(2, order)))
+            left, right, away = lax.optimization_barrier((left, right, away))
         for i, flow in enumerate(flows):
-            flow.keep = ff_grad(spot, left, right[i : i + 1], 0, F32).reshape(shape)
+            flow.keep = ff_grad(spot, left, right, i, 0, F32).reshape(shape)
         return flows
 
     def unit_flow(arrays, pairs, order):
@@ -1066,7 +1430,11 @@
     conv_grad = from_ff(jnp.where(c == 1, unflipped, d_taps))
     flow_up = ff_flow(normed_f, d_upper, ["xy", "yx"])
     ffn_flows = [flow_dn] + flow_up
-    d_normed_f = settle(d_normed_f, flow_up)
+    soon = jnp.concatenate([conv_grad.reshape(-1, D), d_out_rows], axis=0)
+    soon_masks = [1, 2] + [n_mp << b for b in range(place.dp_bits)]
+    soon_sent = place.swap(soon, soon_masks[0])
+    d_normed_f, soon_sent = settle((d_normed_f, soon_sent), flow_up)
+    soon = soon + soon_sent
     d_state_c = d_state_f + layer_norm_back(d_normed_f * (1.0 + mods[4]), hat_f, inv_f)
     d_mods = [None] * 6
     d_mods[5] = by_segment(d_state_f * branch_f)
@@ -1075,13 +1443,15 @@
 
     d_branch_c = bf(d_state_c)
     d_cross = bf(mm(d_branch_c, w_o1))
-    conv_sent = place.swap(conv_grad, 1)
-    d_xq_b, d_keys, d_values, conv_sent = tick(
-        tuple(cross_backward(xq, keys, values, d_cross, token_seg, text_segment[None, :]))
-        + (conv_sent,),
+    soon_sent = place.swap(soon, soon_masks[1])
+    (d_xq_b, d_keys, d_values), soon_sent = tick(
+        (
+            cross_backward(xq, keys, values, d_cross, token_seg, text_segment[None, :]),
+            soon_sent,
+        ),
         ffn_flows,
     )
-    conv_grad = conv_grad + conv_sent
+    soon = soon + soon_sent
     half_txt = TXT // 2
     d_kv = jnp.stack([d_keys, d_values])
     d_kv = d_kv[:, :half_txt] + place.swap(d_kv[:, half_txt:], 1)
@@ -1089,48 +1459,27 @@
     early = unit_flow(
         [state_b, d_xq_b, d_branch_c, cross_b, text_b, d_kv_b[0], d_kv_b[1]],
         ((0, 1), (2, 3), (4, 5), (4, 6)),
-        "yx",
+        "yzx",
     )
     d_state_a = d_state_c + mm_nt(d_xq_b, w_xq)
-    d_state_a = settle(d_state_a, [early])
-
-    d_text = mm_nt(d_kv_b[0], w_xk) + mm_nt(d_kv_b[1], w_xv)
-    d_gain = jnp.sum(d_text * text_hat, axis=0)
-    d_hat = d_text * gain
-    d_text_raw = text_inv * (d_hat - text_hat * jnp.mean(d_hat * text_hat, -1, keepdims=True))
-    d_text_raw_b = bf(d_text_raw)
-    g_cap2 = mm_tn(cap_act_b, d_text_raw_b)
-    d_cap_b = bf(gelu_pull(mm_nt(d_text_raw_b, w_cap2))[0])
-    conv_sent = place.swap(conv_grad, 2)
-    d_cap_b, conv_sent, d_state_a = tick((d_cap_b, conv_sent, d_state_a), ffn_flows)
-    conv_grad = conv_grad + conv_sent
-    g_cap1 = mm_tn(caption, d_cap_b)
-    g_cap = jnp.concatenate(
-        [g_cap1, g_cap2, jnp.zeros((place.n * cap_chunk - CAP_ROWS, D), F32)], axis=0
-    ).reshape(split_dp + (2, 2, cap_chunk, D))
-    b = place.dp_bits
-    cap_flow = Flow(
-        place,
-        bf(lax.dynamic_slice_in_dim(g_cap, 1 - c, 1, b + 1)),
-        [("abs", b - 1, place.x_mask), ("abs", b, 2)] + [("abs",) + pair_ for pair_ in far],
-    )
-    cap_flow.keep = lax.dynamic_slice_in_dim(g_cap, c, 1, b + 1)
-    d_state_a = settle(d_state_a, [cap_flow])
+    soon_sent = place.swap(soon, soon_masks[2])
+    d_state_a, d_kv_b, soon_sent = settle((d_state_a, d_kv_b, soon_sent), [early])
+    soon = soon + soon_sent
 
     d_branch_a = bf(mods[2] * d_state_a)
     d_mods[2] = by_segment(d_state_a * branch_a)
     d_attn = mm(d_branch_a, w_o0)
-    conv_sent = place.swap(conv_grad, place.x_mask)
-    dq_b, d_state, d_sum, conv_sent = tick(
-        tuple(group_call(
+    soon_sent = place.swap(soon, soon_masks[3])
+    (dq_b, d_state, d_sum), soon_sent = tick(
+        (group_call(
             attend_back_kernel,
             ins=("tok", "tok", "seg", "kv", "ks"),
             outs=("tok", "kv", "ks"),
             out_types=(BF16, F32, F32),
-        )(q, d_attn, second_wide, state, key_sum)) + (conv_sent,),
-        ffn_flows + [early],
-    )
-    conv_grad = conv_grad + conv_sent
+        )(q, d_attn, second_wide, state, key_sum), soon_sent),
+        ffn_flows,
+    )
+    soon = soon + soon_sent
     d_state, d_sum = shared(d_state, d_sum)
     dk_b, dv_b = group_call(
         state_back_kernel,
@@ -1138,49 +1487,98 @@
         outs=("tok", "tok"),
         out_types=(BF16, BF16),
     )(k, v, second_wide, d_state, d_sum)
-    dk_b, dv_b = tick((dk_b, dv_b), flow_up)
+    d_normed_a = mm_nt(dq_b, w_q) + mm_nt(dk_b, w_k) + mm_nt(dv_b, w_v)
+    d_mods[0] = by_segment(d_normed_a)
+    d_mods[1] = by_segment(d_normed_a * hat_a)
+
+    d_mod = jnp.stack([table for table, _ in d_mods], axis=1).reshape(4, 6 * D)
+    d_mod = jnp.pad(d_mod, ((0, 0), (BLOCK_AT, 0)))
+    d_mod = d_mod.reshape(4, place.n, owner_rows).transpose(1, 0, 2)
+    d_mod, dq_b, dk_b, dv_b = lax.optimization_barrier((d_mod, dq_b, dk_b, dv_b))
+    d_mod = lax.all_to_all(d_mod, AXES, 0, 0)
     late = unit_flow(
         [normed_a, dq_b, dk_b, dv_b, d_branch_a, attn_b],
         ((0, 1), (0, 2), (0, 3), (4, 5)),
         "xy",
     )
-    dq_b, dk_b, dv_b = settle((dq_b, dk_b, dv_b), [late])
-    dq_b, dk_b, dv_b = tick((dq_b, dk_b, dv_b), [early, cap_flow])
-    d_normed_a = mm_nt(dq_b, w_q) + mm_nt(dk_b, w_k) + mm_nt(dv_b, w_v)
-    d_mods[0] = by_segment(d_normed_a)
-    d_mods[1] = by_segment(d_normed_a * hat_a)
     d_embed = d_state_a + layer_norm_back(d_normed_a * (1.0 + mods[1]), hat_a, inv_a)
     g_patch = mm_tn(mixed_in, d_embed, HIGH)
+    d_mod, d_kv_b, g_patch, late.keep, late.moving, early.moving = lax.optimization_barrier(
+        (d_mod, d_kv_b, g_patch, late.keep, late.moving, early.moving)
+    )
+    near_far = [stage for stage in stages(1, "") if stage[1] != 1]
+    late_flows = late.split(
+        1, [stages(1, order)[:2] + near_far for order in ("xy", "yx")]
+    )
+    d_mod, d_kv_b = tick((d_mod, d_kv_b), ffn_flows)
+    for flow in late_flows + [early]:
+        flow.land()
+    for mask in soon_masks[4:]:
+        soon = soon + place.swap(soon, mask)
+    conv_grad = soon[: conv_grad.size // D].reshape(conv_grad.shape)
+    d_out_rows = soon[conv_grad.size // D :]
+    d_mod = d_mod.reshape(slots // 4, 2, 4, owner_rows).sum(1).reshape(slots, owner_rows)
+    d_silu = mm(d_mod, wide(cond_b), HIGH)
+    g_block = mm_tn(d_mod, wide(silu_b), HIGH)
+
+    d_text = mm_nt(d_kv_b[0], w_xk) + mm_nt(d_kv_b[1], w_xv)
+    d_gain = jnp.sum(d_text * text_hat, axis=0)
+    d_hat = d_text * gain
+    d_text_raw = text_inv * (d_hat - text_hat * jnp.mean(d_hat * text_hat, -1, keepdims=True))
+    d_text_raw_b = bf(d_text_raw)
+    d_cap_b = bf(gelu_pull(mm_nt(d_text_raw_b, w_cap2))[0])
+    cap_shape = split_dp + (2, 1, cap_chunk, D)
+    if cap_chunk == GL:
+        cap_parts = [caption, cap_act_b, d_cap_b, d_text_raw_b]
+        cap_sends = cap_grad(spot, cap_parts, place.n, 1, BF16).reshape(cap_shape)
+        cap_keep = partial(cap_grad, spot, cap_parts, place.n, 0, F32)
+    else:
+        g_cap = jnp.concatenate(
+            [
+                mm_tn(caption, d_cap_b),
+                mm_tn(cap_act_b, d_text_raw_b),
+                jnp.zeros((place.n * cap_chunk - CAP_ROWS, D), F32),
+            ],
+            axis=0,
+        ).reshape(split_dp + (2, 2, cap_chunk, D))
+        cap_sends = bf(lax.dynamic_slice_in_dim(g_cap, 1 - c, 1, place.dp_bits + 1))
+        cap_keep = partial(lax.dynamic_slice_in_dim, g_cap, c, 1, place.dp_bits + 1)
+
     d_rows_six = jnp.stack([total for _, total in d_mods])
     tables_grad = jnp.concatenate(
-        [d_rows_six, d_shift_o[None], d_scale_o[None], d_gain[None], g_patch, d_out_rows], axis=0
-    )
-    for b in range(place.dp_bits + 2):
-        tables_grad = tables_grad + place.swap(tables_grad, 1 << b)
-        if (1 << b) > place.x_mask:
-            conv_grad = conv_grad + place.swap(conv_grad, 1 << b)
-
-    d_mod = jnp.stack([table for table, _ in d_mods], axis=1).reshape(4, 6 * D)
-    d_mod = jnp.pad(d_mod, ((0, 0), (BLOCK_AT, 0)))
-    d_mod = d_mod.reshape(4, place.n, owner_rows).transpose(1, 0, 2)
-    d_mod = lax.all_to_all(d_mod, AXES, 0, 0)
-    d_mod = d_mod.reshape(slots // 4, 2, 4, owner_rows).sum(1).reshape(slots, owner_rows)
-    g_block = mm_tn(d_mod, wide(silu_b), HIGH)
-    d_silu = mm(d_mod, wide(cond_b), HIGH)
-    d_silu = d_silu.reshape(split_dp + (2, 4, D))
-    for axis, mask in [(place.dp_bits, 2), (place.dp_bits - 1, place.x_mask)] + far:
-        bit = place.bit(mask)
-        away = lax.dynamic_slice_in_dim(d_silu, 1 - bit, 1, axis)
-        d_silu = lax.dynamic_slice_in_dim(d_silu, bit, 1, axis) + place.swap(away, mask)
-    d_silu = d_silu.reshape(4, D)
-    pair_sum = jnp.stack([d_silu, d_emb_mine])
-    d_silu, d_emb = pair_sum + place.swap(pair_sum, 1)
+        [d_rows_six, d_shift_o[None], d_scale_o[None], d_gain[None], g_patch], axis=0
+    )
+    masks = [1, 2] + [n_mp << b for b in range(place.dp_bits)]
+    d_silu = jnp.broadcast_to(d_silu.reshape(n_dp, 2, 1, 4 * D), (n_dp, 2, 2, 4 * D))
+    d_silu = lax.all_to_all(d_silu.reshape(place.n, 4 * D), AXES, 0, 0).sum(0).reshape(4, D)
+    cap_flow = Flow(
+        place,
+        cap_sends,
+        [("abs", place.dp_bits, 2), ("abs", place.dp_bits - 1, place.x_mask)]
+        + [("abs",) + pair_ for pair_ in far],
+    )
+    cap_flow.keep = cap_keep().reshape(cap_shape)
     d_time = d_silu * silu_grad(emb_mine) + d_emb
     d_hidden = mm_nt(d_time, wide(w_time[FREQ:]), HIGH)
     hidden_mine = lax.dynamic_slice_in_dim(time_hidden, canvas * 4, 4, 0)
-    d_times = jnp.stack([d_time, d_hidden * silu_grad(hidden_mine)])
-    for mask in [2] + [n_mp << b for b in range(place.dp_bits)]:
-        d_times = ordered(place.bit(mask), d_times, place.swap(d_times, mask), 1)
+    d_times = jnp.concatenate([d_time, d_hidden * silu_grad(hidden_mine)], axis=0)
+    cap_far = [stage for stage in [("abs",) + pair_ for pair_ in far] if stage[1] != 0]
+    cap_y, cap_x = ("abs", place.dp_bits, 2), ("abs", place.dp_bits - 1, place.x_mask)
+    cap_flows = cap_flow.split(0, [[cap_y, cap_x] + cap_far, cap_far[:1] + [cap_y, cap_x] + cap_far[1:]])
+    last = late_flows + cap_flows + [early]
+    for flow in cap_flows:
+        flow.land()
+    ff_own = [flow.drain().reshape(dl, FFB)[:, : FF // 4] for flow in ffn_flows]
+    part_sq = sum(jnp.sum(grad * grad) for grad in [g_block] + ff_own)
+    row = lax.broadcasted_iota(jnp.int32, (8, 128), 0)
+    scalars = jnp.where(row == 0, part_sq, loss)
+    small = jnp.pad(tables_grad, ((0, -tables_grad.shape[0] % 8), (0, 0)))
+    top = n_mp << place.dp_bits - 1
+    joined, cap_own, small, d_times, scalars = finish(
+        n_mp, last, top, masks, small, d_times[None], scalars
+    )
+    tables_grad = jnp.concatenate([small[: tables_grad.shape[0]], d_out_rows], axis=0)
+    d_times = d_times.reshape(-1, 2, 4, D).transpose(1, 0, 2, 3).reshape(2, slots, D)
     g_time2 = mm_tn(wide(hidden_b), d_times[0], HIGH)
     g_time1 = mm_tn(wide(freq_b), d_times[1], HIGH)
     spots = -(-TIME_ROWS // owner_rows)
@@ -1191,23 +1589,16 @@
         g_time, jnp.minimum(place.me, spots) * owner_rows, owner_rows, 0
     )
 
-    ff_own = [flow.drain().reshape(dl, FFB)[:, : FF // 4] for flow in ffn_flows]
-    early_own = early.drain().reshape(dl, D)
-    g_cap = collect_rows(
-        place, cap_flow.drain().reshape(cap_chunk, D), owner_rows, TIME_ROWS, CAP_ROWS
-    )
+    cap_own = cap_own.reshape(cap_chunk, D)
+    g_cap = collect_rows(place, cap_own, owner_rows, TIME_ROWS, CAP_ROWS)
     g_cond = g_cap + g_block + g_time
-    mine = jnp.stack([late.drain().reshape(dl, D), early_own])
-    owned_sq = sum(jnp.sum(grad * grad) for grad in [mine, g_cond] + ff_own)
-    g_in, g_out = from_units(unit_join(place, mine))
+    g_in, g_out = from_units(joined.transpose(1, 0, 2, 3).reshape(8, dl, D // 4))
     g_upper = jnp.stack(ff_own[1:], axis=1)
     g_lower = ff_own[0].T
     owned = (g_in, g_out, g_upper, g_lower, g_cond)
 
-    sums = jnp.stack([owned_sq, loss]).reshape(1, 2)
-    for b in range(place.dp_bits + 2):
-        sums = sums + place.swap(sums, 1 << b)
-    squares, loss = sums[0, 0], sums[0, 1]
+    squares, loss = scalars[0, 0], scalars[1, 0]
+    squares = squares + jnp.sum(g_time1 * g_time1) + jnp.sum(g_time2 * g_time2)
     norm = jnp.sqrt(squares + jnp.sum(conv_grad * conv_grad) + jnp.sum(tables_grad * tables_grad))
     factor = CLIP / jnp.maximum(norm, CLIP)
     rate = STEP_SCALE * math.sqrt(PARAMS) / CLIP

time: 1290 us -> 1180 us (0.915)
  waiting for transfers between devices: 470 us -> 262 us
  Pallas kernels: 245 us -> 436 us
  starting transfers between devices: 145 us -> 85.5 us
  local copies, waits for them, and re-layouts: 139 us -> 124 us
  other arithmetic: 160 us -> 146 us
    ppermute x84 -> x52, waiting for transfers between devices: 338 us -> 121 us  [swap(): return lax.ppermute(value, AXES, [(i, i ^ mask) for i in range(self.n)])]
    pallas_call x0 -> x3, Pallas kernels: none -> 187 us  [the longest x1 169 us: finish(): pl.pallas_call(partial(finish_kernel, n_mp, plan, top, masks, masks[1:]),...]
    ppermute x84 -> x52, starting transfers between devices: 113 us -> 43.8 us  [swap(): return lax.ppermute(value, AXES, [(i, i ^ mask) for i in range(self.n)])]
    add x41 -> x20, other arithmetic: 79.3 us -> 60.1 us  [the longest x15 56.8 us: part(): return take(self.keep) + wide(take(self.moving))]
    convert_element_type x21 -> x1, local copies, waits for them, and re-layouts: 18.7 us -> 0.03 us  [bf(): return value.astype(BF16)]
    slice x10 -> x9, local copies, waits for them, and re-layouts: 28.6 us -> 20.4 us  [the longest x2 7.17 us: split(): flow.keep = lax.slice_in_dim(self.keep, i, i + 1, axis=axis)]
    pallas_call x5 -> x6, Pallas kernels: 26.9 us -> 31.3 us  [ff_grad(): pl.pallas_call(ff_grad_kernel, grid_spec=pltpu.PrefetchScalarGridSpec(num...]
    dot_general x34 -> x32, matrix products: 88.2 us -> 84.7 us  [dot(): lax.dot_general(left, right, (dims, ((), ())), precision=precision, prefe...]
  transfers between devices with their start and end apart: 107 -> 74, of which waited for: 45 -> 23; matrix products, arithmetic and copies ran while one was open for 22% -> 21% of each run, Pallas kernels for 14% -> 16%
where the time goes in v2:
time: 1180 us; the launch traced here: 1170 us
  Pallas kernels  436 us (37%)
  waiting for transfers between devices  262 us (22%)
  other arithmetic  146 us (12%)
  local copies, waits for them, and re-layouts  124 us (11%)
  starting transfers between devices  85.5 us (7%)
  matrix products  84.7 us (7%)
  between operations  28.3 us (2%)
    pallas_call x1, Pallas kernels, finish(): pl.pallas_call(partial(finish_kernel, n_mp, plan, top, masks, masks[1:]),...  169 us
    ppermute x52, waiting for transfers between devices, swap(): return lax.ppermute(value, AXES, [(i, i ^ mask) for i in range(self.n)])  121 us
    dot_general x32, matrix products, dot(): lax.dot_general(left, right, (dims, ((), ())), precision=precision, prefe...  84.7 us
    pallas_call x1, Pallas kernels, ffn_backward(): pl.pallas_call(ffn_backward_kernel, grid=(FFP // CB,), in_specs=[whole_sp...  60.3 us
    add x15, other arithmetic, part(): return take(self.keep) + wide(take(self.moving))  56.8 us
    all_gather x1, waiting for transfers between devices, local(): ffw = lax.all_gather(ff_b.reshape(3 * dl, FFB), AXES, axis=0)  56.6 us
    all_gather x1, waiting for transfers between devices, local(): got = lax.all_gather(packed, AXES, axis=0)  49.8 us
    pallas_call x1, Pallas kernels, ffn_forward(): pl.pallas_call(ffn_forward_kernel, grid=(FFP // CB,), in_specs=[whole_spe...  45.7 us
  transfers between devices with their start and end apart: 74, of which 23 were waited for; matrix products, arithmetic and copies ran while one was open for 21% of the time, Pallas kernels for 16%

profile of v2, /device:TPU:28, one launch (start us, length us, event | category | flops | bytes accessed | tf_op | source)
XLA Modules:
  0.0 1167.3 jit_solution(10788400574213757730)
XLA Ops:
  29.9 11.0 collective-permute-done.12
  80.9 8.4 collective-permute-done.16
  93.6 10.4 collective-permute-done.22
  104.1 16.1 %collective-permute-start.23 = (bf16[2,48,1152]{2,1,0:T(8,128)(2,1)S(1)}, bf16[2,48,1152]{2,1,0:T(8,128)(2,1)S(1)}, u32[]{:S(2)}, u32[]{:S(2)}) collective-permute-start(bf16[2,48,1152]{2,1,0:T(8,128)(2,1)S(1)} %pad_maximum_fusion.18), channel_id=1, source_target_pairs={{0,16},{1,17},{2,18},{3,19},{4,20},{5,21},{6,22},{7,23},{8,24},{9,... | collective-permute-start | bytes 663560 | tf_op jit(solution)/shard_map/ppermute | solution.py:79
  123.6 21.6 %collective-permute-done.23 = bf16[2,48,1152]{2,1,0:T(8,128)(2,1)S(1)} collective-permute-done((bf16[2,48,1152]{2,1,0:T(8,128)(2,1)S(1)}, bf16[2,48,1152]{2,1,0:T(8,128)(2,1)S(1)}, u32[]{:S(2)}, u32[]{:S(2)}) %collective-permute-start.23) | collective-permute-done | bytes 221216 | tf_op jit(solution)/shard_map/ppermute | solution.py:79
  146.2 11.6 collective-permute-done.24
  160.4 20.0 %collective-permute-done.26 = bf16[4,48,1152]{2,1,0:T(8,128)(2,1)S(1)} collective-permute-done((bf16[4,48,1152]{2,1,0:T(8,128)(2,1)S(1)}, bf16[4,48,1152]{2,1,0:T(8,128)(2,1)S(1)}, u32[]{:S(2)}, u32[]{:S(2)}) %collective-permute-start.26) | collective-permute-done | bytes 442400 | tf_op jit(solution)/shard_map/ppermute | solution.py:79
  194.2 7.7 all-to-all-done
  206.8 49.8 %all-gather.6.cloned.1.call-done = bf16[13312,1152]{1,0:T(8,128)(2,1)} async-done(((bf16[416,1152]{1,0:T(8,128)(2,1)}), bf16[13312,1152]{1,0:T(8,128)(2,1)}) %all-gather.6.cloned.1.call-update) | async-done | bytes 30670864 | tf_op jit(solution)/shard_map/all_gather | solution.py:1214
  267.8 14.2 %fusion.160 = (bf16[8,1,1,144,1152]{4,3,2,1,0:T(8,128)(2,1)}, bf16[8,1,1,144,1152]{4,3,2,1,0:T(8,128)(2,1)S(1)}, bf16[8,1,1,144,1152]{4,3,2,1,0:T(8,128)(2,1)S(1...) fusion(bf16[8,2,2,416,1152]{4,3,2,1,0:T(8,128)(2,1)} %bitcast.355), kind=kLoop, calls=%fused_computation.492 | loop fusion | bytes 42467328 | tf_op jit(solution)/shard_map/slice | solution.py:1217
  308.6 17.9 %shard_map.436.refs_3_ = bf16[512,1152]{1,0:T(8,128)(2,1)S(1)} custom-call(bf16[512,1152]{1,0:T(8,128)(2,1)S(1)} %convolution_convert_fusion.1.q_ref, bf16[512,1152]{1,0:T(8,128)(2,1)S(1)} %pad_maximum_fusion.5.k_ref, bf16[512,1152]{1,0:T(8,128)(2,1)S(1)} %pad_maximum_fusion.6.v_ref, s32[512,1]{1,0:T(8,128)S(1)} %fusion.85.tok_ref, s32[1,512]{1,0:T(1,128)S(1)} %bitcast.335), custom_call_target="tpu_custom_call" | custom-call | flops 1048576 | bytes 65536 | tf_op jit(solution)/shard_map/pallas_call | solution.py:1004
  338.6 56.6 %all-gather.4.cloned.1.call-done = bf16[32,432,768]{2,1,0:T(8,128)(2,1)} async-done(((bf16[1,432,768]{2,1,0:T(8,128)(2,1)}), bf16[32,432,768]{2,1,0:T(8,128)(2,1)}) %all-gather.4.cloned.1.call-update) | async-done | bytes 21233680 | tf_op jit(solution)/shard_map/all_gather | solution.py:1222
  398.3 45.7 %shard_map.437 = (f32[2,544,3072]{2,1,0:T(8,128)}, f32[2,512,3072]{2,1,0:T(8,128)}, bf16[512,3072]{1,0:T(8,128)(2,1)}, f32[512,1152]{1,0:T(8,128)S(1)}) custom-call(bf16[544,1152]{1,0:T(8,128)(2,1)S(1)} %copy-done.17, bf16[8,4,432,768]{3,2,1,0:T(8,128)(2,1)} %bitcast.337, bf16[8,4,432,768]{3,2,1,0:T(8,128)(2,1)} %bitcast.338, ...), custom_call_target="tpu_custom_call" | custom-call | flops 1048576 | bytes 65536 | tf_op jit(solution)/shard_map/pallas_call | solution.py:399
  477.8 60.3 %shard_map.440 = (bf16[2,512,3072]{2,1,0:T(8,128)(2,1)}, f32[2,10,3072]{2,1,0:T(8,128)S(1)}, f32[512,1152]{1,0:T(8,128)S(1)}) custom-call(bf16[544,1152]{1,0:T(8,128)(2,1)S(1)} %pad_maximum_fusion.2.d_ref, bf16[8,4,432,768]{3,2,1,0:T(8,128)(2,1)} %bitcast.340, bf16[8,4,432,768]{3,2,1,0:T(8,128)(2,1)} %bitcast.341, bf16[8,4,432,768]{3,2,1,0:T(8,128)(2,1)} %bitcast.342, ...), custom_call_target="tpu_custom_call" | custom-call | flops 1048576 | bytes 65536 | tf_op jit(solution)/shard_map/pallas_call | solution.py:510
  598.3 37.9 %shard_map.445 = (bf16[512,1152]{1,0:T(8,128)(2,1)S(1)}, f32[512,1152]{1,0:T(8,128)}, f32[512,1152]{1,0:T(8,128)}) custom-call(bf16[512,1152]{1,0:T(8,128)(2,1)S(1)} %convolution_convert_fusion.1.q_ref, bf16[512,1152]{1,0:T(8,128)(2,1)S(1)} %pad_maximum_fusion.5.k_ref, bf16[512,1152]{1,0:T(8,128)(2,1)S(1)} %copy-done.10, ...), custom_call_target="tpu_custom_call" | custom-call | flops 1048576 | bytes 65536 | tf_op jit(solution)/shard_map/pallas_call | solution.py:1050
  686.3 9.5 slice_add_fusion
  701.0 11.9 %shard_map.448 = (bf16[512,1152]{1,0:T(8,128)(2,1)S(1)}, f32[9,2,128,128]{3,2,1,0:T(8,128)S(1)}, f32[9,2,8,128]{3,2,1,0:T(8,128)S(1)}) custom-call(bf16[512,1152]{1,0:T(8,128)(2,1)S(1)} %copy-done.32, f32[512,1152]{1,0:T(8,128)} %fusion.172.da_ref, f32[512,128]{1,0:T(8,128)S(1)} %copy-done.14, f32[9,2,128,128]{3,2,1,0:T(8,128)S(1)} %copy-done.8, ...), custom_call_target="tpu_custom_call" | custom-call | flops 1048576 | bytes 65536 | tf_op jit(solution)/shard_map/pallas_call | solution.py:1474
  724.2 7.3 shard_map.449
  777.7 19.1 %collective-permute-done.64 = f32[82,1152]{1,0:T(8,128)S(1)} collective-permute-done((f32[82,1152]{1,0:T(8,128)S(1)}, f32[82,1152]{1,0:T(8,128)S(1)}, u32[]{:S(2)}, u32[]{:S(2)}) %collective-permute-start.64) | collective-permute-done | bytes 377888 | tf_op jit(solution)/shard_map/ppermute | solution.py:79
  814.7 7.9 shard_map.451
  841.3 8.4 shard_map.453
  849.7 9.5 shard_map.452
  899.9 8.3 collective-permute-done.63
  929.6 169.1 %shard_map.454 = (f32[4,2,144,288]{3,2,1,0:T(8,128)}, f32[128,1152]{1,0:T(8,128)}, f32[48,1152]{1,0:T(8,128)}, f32[16,8,1152]{2,1,0:T(8,128)}, f32[8,128]{1,0:T(8,128)}) custom-call(bf16[4,144,1152]{2,1,0:T(8,128)(2,1)} %bitcast.388, bf16[4,144,1152]{2,1,0:T(8,128)(2,1)} %bitcast.389, bf16[4,128,1152]{2,1,0:T(8,128)(2,1)} %bitcast.394, ...), custom_call_target="tpu_custom_call" | custom-call | tf_op jit(solution)/shard_map/pallas_call | solution.py:913
  (963 shorter events, 498.8 us)
Async XLA Ops:
  7.2 249.4 %all-gather.6.cloned.1.call-start = ((), (), s32[]{:S(2)}) async-start(), calls=%async_computation.4 | async-start | bytes 31629312 | tf_op jit(solution)/shard_map/all_gather | solution.py:1214
  49.4 345.8 %all-gather.4.cloned.1.call-start = ((), (), s32[]{:S(2)}) async-start(), calls=%async_computation.3 | async-start | bytes 21897216 | tf_op jit(solution)/shard_map/all_gather | solution.py:1222
  91.6 171.1 %collective-permute-start.32 = (bf16[128,2304]{1,0:T(8,128)(2,1)}, bf16[128,2304]{1,0:T(8,128)(2,1)}, u32[]{:S(2)}, u32[]{:S(2)}) collective-permute-start(bf16[128,2304]{1,0:T(8,128)(2,1)} %get-tuple-element.562), channel_id=1, source_target_pairs={{0,2},{1,3},{2,0},{3,1},{4,6},{5,7},{6,4},{7,5},{8,10},{9,11},{10,... | collective-permute-start | bytes 1769480 | tf_op jit(solution)/shard_map/ppermute | solution.py:79
  104.1 41.1 %collective-permute-start.23 = (bf16[2,48,1152]{2,1,0:T(8,128)(2,1)S(1)}, bf16[2,48,1152]{2,1,0:T(8,128)(2,1)S(1)}, u32[]{:S(2)}, u32[]{:S(2)}) collective-permute-start(bf16[2,48,1152]{2,1,0:T(8,128)(2,1)S(1)} %pad_maximum_fusion.18), channel_id=1, source_target_pairs={{0,16},{1,17},{2,18},{3,19},{4,20},{5,21},{6,22},{7,23},{8,24},{9,... | collective-permute-start | bytes 663560 | tf_op jit(solution)/shard_map/ppermute | solution.py:79
  473.7 64.4 %collective-permute-start.39 = (bf16[1,1,2,2,2,144,768]{6,5,4,3,2,1,0:T(8,128)(2,1)}, bf16[1,1,2,2,2,144,768]{6,5,4,3,2,1,0:T(8,128)(2,1)}, u32[]{:S(2)}, u32[]{:S(2)}) collective-permute-start(bf16[1,1,2,2,2,144,768]{6,5,4,3,2,1,0:T(8,128)(2,1)} %get-tuple-element.171), channel_id=1, source_target_pairs={{0,2},{1,3},{2,0},{3,1},{4,6},{5,7},{6,4},{7,5},{8,10},{9,11},{10,... | collective-permute-start | bytes 5308424 | tf_op jit(solution)/shard_map/ppermute | solution.py:79
  564.6 71.6 %collective-permute-start.44 = (bf16[1,1,2,2,1,144,768]{6,5,4,3,2,1,0:T(8,128)(2,1)}, bf16[1,1,2,2,1,144,768]{6,5,4,3,2,1,0:T(8,128)(2,1)S(1)}, u32[]{:S(2)}, u32[]{:S(2)}) collective-permute-start(bf16[1,1,2,2,1,144,768]{6,5,4,3,2,1,0:T(8,128)(2,1)} %get-tuple-element.196), channel_id=1, source_target_pairs={{0,4},{1,5},{2,6},{3,7},{4,0},{5,1},{6,2},{7,3},{8,12},{9,13},{10,... | collective-permute-start | bytes 2654216 | tf_op jit(solution)/shard_map/ppermute | solution.py:79
  591.5 44.7 %collective-permute-start.43 = (f32[82,1152]{1,0:T(8,128)S(1)}, f32[82,1152]{1,0:T(8,128)S(1)}, u32[]{:S(2)}, u32[]{:S(2)}) collective-permute-start(f32[82,1152]{1,0:T(8,128)S(1)} %fusion.151), channel_id=1, source_target_pairs={{0,2},{1,3},{2,0},{3,1},{4,6},{5,7},{6,4},{7,5},{8,10},{9,11},{10,... | collective-permute-start | bytes 1133576 | tf_op jit(solution)/shard_map/ppermute | solution.py:79
  592.1 44.1 %collective-permute-start.45 = (bf16[1,2,2,2,1,144,768]{6,5,4,3,2,1,0:T(8,128)(2,1)}, bf16[1,2,2,2,1,144,768]{6,5,4,3,2,1,0:T(8,128)(2,1)}, u32[]{:S(2)}, u32[]{:S(2)}) collective-permute-start(bf16[1,2,2,2,1,144,768]{6,5,4,3,2,1,0:T(8,128)(2,1)} %get-tuple-element.197), channel_id=1, source_target_pairs={{0,4},{1,5},{2,6},{3,7},{4,0},{5,1},{6,2},{7,3},{8,12},{9,13},{10,... | collective-permute-start | bytes 5308424 | tf_op jit(solution)/shard_map/ppermute | solution.py:79
  593.6 47.3 %collective-permute-start.46 = (bf16[1,1,2,2,2,144,768]{6,5,4,3,2,1,0:T(8,128)(2,1)}, bf16[1,1,2,2,2,144,768]{6,5,4,3,2,1,0:T(8,128)(2,1)}, u32[]{:S(2)}, u32[]{:S(2)}) collective-permute-start(bf16[1,1,2,2,2,144,768]{6,5,4,3,2,1,0:T(8,128)(2,1)} %get-tuple-element.198), channel_id=1, source_target_pairs={{0,2},{1,3},{2,0},{3,1},{4,6},{5,7},{6,4},{7,5},{8,10},{9,11},{10,... | collective-permute-start | bytes 5308424 | tf_op jit(solution)/shard_map/ppermute | solution.py:79
  670.6 42.3 %collective-permute-start.51 = (bf16[1,1,2,1,1,144,768]{6,5,4,3,2,1,0:T(8,128)(2,1)}, bf16[1,1,2,1,1,144,768]{6,5,4,3,2,1,0:T(8,128)(2,1)S(1)}, u32[]{:S(2)}, u32[]{:S(2)}) collective-permute-start(bf16[1,1,2,1,1,144,768]{6,5,4,3,2,1,0:T(8,128)(2,1)} %get-tuple-element.230), channel_id=1, source_target_pairs={{0,8},{1,9},{2,10},{3,11},{4,12},{5,13},{6,14},{7,15},{8,0},{9,1},... | collective-permute-start | bytes 1327112 | tf_op jit(solution)/shard_map/ppermute | solution.py:79
  672.1 40.8 %collective-permute-start.52 = (bf16[1,1,2,2,1,144,768]{6,5,4,3,2,1,0:T(8,128)(2,1)}, bf16[1,1,2,2,1,144,768]{6,5,4,3,2,1,0:T(8,128)(2,1)S(1)}, u32[]{:S(2)}, u32[]{:S(2)}) collective-permute-start(bf16[1,1,2,2,1,144,768]{6,5,4,3,2,1,0:T(8,128)(2,1)} %get-tuple-element.231), channel_id=1, source_target_pairs={{0,2},{1,3},{2,0},{3,1},{4,6},{5,7},{6,4},{7,5},{8,10},{9,11},{10,... | collective-permute-start | bytes 2654216 | tf_op jit(solution)/shard_map/ppermute | solution.py:79
  673.6 39.3 %collective-permute-start.53 = (bf16[1,1,2,2,1,144,768]{6,5,4,3,2,1,0:T(8,128)(2,1)}, bf16[1,1,2,2,1,144,768]{6,5,4,3,2,1,0:T(8,128)(2,1)S(1)}, u32[]{:S(2)}, u32[]{:S(2)}) collective-permute-start(bf16[1,1,2,2,1,144,768]{6,5,4,3,2,1,0:T(8,128)(2,1)} %get-tuple-element.232), channel_id=1, source_target_pairs={{0,4},{1,5},{2,6},{3,7},{4,0},{5,1},{6,2},{7,3},{8,12},{9,13},{10,... | collective-permute-start | bytes 2654216 | tf_op jit(solution)/shard_map/ppermute | solution.py:79
  761.7 62.6 %collective-permute-start.55 = (bf16[2,2,2,2,144,1152]{5,4,3,2,1,0:T(8,128)(2,1)}, bf16[2,2,2,2,144,1152]{5,4,3,2,1,0:T(8,128)(2,1)}, u32[]{:S(2)}, u32[]{:S(2)}) collective-permute-start(bf16[2,2,2,2,144,1152]{5,4,3,2,1,0:T(8,128)(2,1)} %bitcast.386), channel_id=1, source_target_pairs={{0,1},{1,0},{2,3},{3,2},{4,5},{5,4},{6,7},{7,6},{8,9},{9,8},{10,11... | collective-permute-start | bytes 15925256 | tf_op jit(solution)/shard_map/ppermute | solution.py:79
  761.7 62.6 %collective-permute-start.56 = (bf16[1,2,2,2,144,1152]{5,4,3,1,2,0:T(8,128)(2,1)}, bf16[1,2,2,2,144,1152]{5,4,3,1,2,0:T(8,128)(2,1)}, u32[]{:S(2)}, u32[]{:S(2)}) collective-permute-start(bf16[1,2,2,2,144,1152]{5,4,3,1,2,0:T(8,128)(2,1)} %get-tuple-element.256), channel_id=1, source_target_pairs={{0,2},{1,3},{2,0},{3,1},{4,6},{5,7},{6,4},{7,5},{8,10},{9,11},{10,... | collective-permute-start | bytes 7962632 | tf_op jit(solution)/shard_map/ppermute | solution.py:79
  775.6 48.7 %collective-permute-start.57 = (bf16[1,1,1,1,1,144,768]{6,5,4,3,2,1,0:T(8,128)(2,1)}, bf16[1,1,1,1,1,144,768]{6,5,4,3,2,1,0:T(8,128)(2,1)}, u32[]{:S(2)}, u32[]{:S(2)}) collective-permute-start(bf16[1,1,1,1,1,144,768]{6,5,4,3,2,1,0:T(8,128)(2,1)} %add_convert_fusion.17), channel_id=1, source_target_pairs={{0,16},{1,17},{2,18},{3,19},{4,20},{5,21},{6,22},{7,23},{8,24},{9,... | collective-permute-start | bytes 663560 | tf_op jit(solution)/shard_map/ppermute | solution.py:79
  777.1 47.2 %collective-permute-start.58 = (bf16[1,1,2,1,1,144,768]{6,5,4,3,2,1,0:T(8,128)(2,1)}, bf16[1,1,2,1,1,144,768]{6,5,4,3,2,1,0:T(8,128)(2,1)}, u32[]{:S(2)}, u32[]{:S(2)}) collective-permute-start(bf16[1,1,2,1,1,144,768]{6,5,4,3,2,1,0:T(8,128)(2,1)} %get-tuple-element.262), channel_id=1, source_target_pairs={{0,8},{1,9},{2,10},{3,11},{4,12},{5,13},{6,14},{7,15},{8,0},{9,1},... | collective-permute-start | bytes 1327112 | tf_op jit(solution)/shard_map/ppermute | solution.py:79
  824.2 91.2 %collective-permute-start.61 = (f32[4,1152]{1,0:T(4,128)}, f32[4,1152]{1,0:T(4,128)}, u32[]{:S(2)}, u32[]{:S(2)}) collective-permute-start(f32[4,1152]{1,0:T(4,128)} %add_add_fusion.2), channel_id=1, source_target_pairs={{0,1},{1,0},{2,3},{3,2},{4,5},{5,4},{6,7},{7,6},{8,9},{9,8},{10,11... | collective-permute-start | bytes 55304 | tf_op jit(solution)/shard_map/ppermute | solution.py:79
  859.4 37.0 %collective-permute-start.62 = (bf16[1,1,1,1,1,144,768]{6,5,4,3,2,1,0:T(8,128)(2,1)}, bf16[1,1,1,1,1,144,768]{6,5,4,3,2,1,0:T(8,128)(2,1)}, u32[]{:S(2)}, u32[]{:S(2)}) collective-permute-start(bf16[1,1,1,1,1,144,768]{6,5,4,3,2,1,0:T(8,128)(2,1)} %add_convert_fusion.16), channel_id=1, source_target_pairs={{0,16},{1,17},{2,18},{3,19},{4,20},{5,21},{6,22},{7,23},{8,24},{9,... | collective-permute-start | bytes 663560 | tf_op jit(solution)/shard_map/ppermute | solution.py:79
  862.8 49.2 %all-to-all-start.2 = ((f32[32,1,4608]{2,1,0:T(1,128)}), f32[32,1,4608]{2,1,0:T(1,128)}, u32[]{:S(2)}, u32[]{:S(2)}) async-start(f32[32,1,4608]{2,1,0:T(1,128)} %all_to_all.18), calls=%async_computation.2 | async-start | bytes 1179648 | tf_op jit(solution)/shard_map/all_to_all | solution.py:1553
  874.1 45.9 %collective-permute-start.60 = (bf16[2,2,2,2,1,128,1152]{6,5,3,2,4,1,0:T(8,128)(2,1)}, bf16[2,2,2,2,1,128,1152]{6,5,3,2,4,1,0:T(8,128)(2,1)}, u32[]{:S(2)}, u32[]{:S(2)}) collective-permute-start(bf16[2,2,2,2,1,128,1152]{6,5,3,2,4,1,0:T(8,128)(2,1)} %bitcast.112), channel_id=1, source_target_pairs={{0,1},{1,0},{2,3},{3,2},{4,5},{5,4},{6,7},{7,6},{8,9},{9,8},{10,11... | collective-permute-start | bytes 14155784 | tf_op jit(solution)/shard_map/ppermute | solution.py:79
  1100.6 52.7 %collective-permute-start.68 = (bf16[128,1152]{1,0:T(8,128)(2,1)}, bf16[128,1152]{1,0:T(8,128)(2,1)}, u32[]{:S(2)}, u32[]{:S(2)}) collective-permute-start(bf16[128,1152]{1,0:T(8,128)(2,1)} %convert_element_type.455), channel_id=1, source_target_pairs={{0,3},{3,4},{6,5},{9,6},{17,9},{20,10},{23,11},{26,12},{29,13}} | collective-permute-start | bytes 884744 | tf_op jit(solution)/shard_map/ppermute | solution.py:165
  1103.8 49.5 %collective-permute-start.67 = (bf16[128,1152]{1,0:T(8,128)(2,1)}, bf16[128,1152]{1,0:T(8,128)(2,1)}, u32[]{:S(2)}, u32[]{:S(2)}) collective-permute-start(bf16[128,1152]{1,0:T(8,128)(2,1)} %convert_element_type.455), channel_id=1, source_target_pairs={{2,4},{5,5},{8,6},{11,7},{14,8},{16,9},{19,10},{22,11},{25,12},{28... | collective-permute-start | bytes 884744 | tf_op jit(solution)/shard_map/ppermute | solution.py:165
  1105.2 48.1 %collective-permute-start.66 = (bf16[128,1152]{1,0:T(8,128)(2,1)}, bf16[128,1152]{1,0:T(8,128)(2,1)}, u32[]{:S(2)}, u32[]{:S(2)}) collective-permute-start(bf16[128,1152]{1,0:T(8,128)(2,1)} %convert_element_type.455), channel_id=1, source_target_pairs={{1,4},{4,5},{7,6},{10,7},{13,8},{15,9},{18,10},{21,11},{24,12},{27... | collective-permute-start | bytes 884744 | tf_op jit(solution)/shard_map/ppermute | solution.py:165
  1106.6 46.7 %collective-permute-start.65 = (bf16[128,1152]{1,0:T(8,128)(2,1)}, bf16[128,1152]{1,0:T(8,128)(2,1)}, u32[]{:S(2)}, u32[]{:S(2)}) collective-permute-start(bf16[128,1152]{1,0:T(8,128)(2,1)} %convert_element_type.455), channel_id=1, source_target_pairs={{0,4},{3,5},{6,6},{9,7},{12,8},{14,9},{17,10},{20,11},{23,12},{26,... | collective-permute-start | bytes 884744 | tf_op jit(solution)/shard_map/ppermute | solution.py:165
  (297 other events, 4228.4 us)
Sparse Core Ops, SparseCore 0:
  49.6 207.0 all-gather.5
  260.1 135.0 all-gather.3

commit v3 on v2

--- a/solution.py
+++ b/solution.py
@@ -138,9 +138,8 @@
     return tables
 
 
-def chunk_of(place, rows):
+def chunk_of(place, rows, unit=16):
     chunk = -(-rows // place.n)
-    unit = 128 if chunk > 64 else 8
     return -(-chunk // unit) * unit
 
 
@@ -267,7 +266,7 @@
         self.sends = None
 
     def part(self, take):
-        return take(self.keep) + wide(take(self.moving))
+        return wide(take(self.keep)) + wide(take(self.moving))
 
     def land(self):
         if not self.stages:
@@ -580,11 +579,16 @@
         def _():
             for i in range(3):
                 rows = pl.ds(i * step, step)
-                value = mm_tn(refs[left][:, rows], refs[right][...])
-                out_ref[0, rows] = value.astype(out_ref.dtype)
-
-
-def unit_grad(spot, arrays, pairs, away, dtype):
+                value = mm_tn(refs[left][:, rows], refs[right][...]).astype(out_ref.dtype)
+                height = out_ref.shape[2]
+                for block in range(i * step // height, -(-(i + 1) * step // height)):
+                    low, high = max(block * height, i * step), min((block + 1) * height, (i + 1) * step)
+                    out_ref[0, block, low - block * height : high - block * height] = value[
+                        low - i * step : high - i * step
+                    ]
+
+
+def unit_grad(spot, arrays, pairs, away, dtype, blocks):
     n_tok = arrays[0].shape[0]
     return pl.pallas_call(
         partial(unit_grad_kernel, pairs, away),
@@ -592,9 +596,9 @@
             num_scalar_prefetch=1,
             grid=(2,),
             in_specs=[pl.BlockSpec(a.shape, lambda r, spot_ref: (0, 0)) for a in arrays],
-            out_specs=pl.BlockSpec((1, D, D), lambda r, spot_ref: (r, 0, 0)),
+            out_specs=pl.BlockSpec((1, blocks, D // blocks, D), lambda r, spot_ref: (r, 0, 0, 0)),
         ),
-        out_shape=jax.ShapeDtypeStruct((2, D, D), dtype),
+        out_shape=jax.ShapeDtypeStruct((2, blocks, D // blocks, D), dtype),
         compiler_params=pltpu.CompilerParams(
             dimension_semantics=("arbitrary",), vmem_limit_bytes=LIMIT
         ),
@@ -631,9 +635,11 @@
         return {"dp": dp + mask // n_mp * (1 - 2 * bit(mask))}
 
     sends, keeps = refs[:count], refs[count : 2 * count]
-    part_ref, mine_ref, scalar_ref = refs[2 * count : 2 * count + 3]
-    join_ref, cap_ref, sum_ref, all_ref, total_ref = refs[2 * count + 3 : 2 * count + 8]
-    scratch = list(refs[2 * count + 8 :])
+    part_ref, mine_ref, scalar_ref, soon_ref = refs[2 * count : 2 * count + 4]
+    join_ref, cap_ref, sum_ref, all_ref, total_ref, soon_out = refs[2 * count + 4 : 2 * count + 10]
+    scratch = list(refs[2 * count + 10 :])
+    soon_sem = scratch.pop()
+    soon_got = scratch.pop()
     (
         send_sem, recv_sem, sum_send, sum_recv, all_send, all_recv, one_send, one_recv,
         join_send, join_recv
@@ -794,12 +800,24 @@
 
         return cut
 
+    def soon_copy():
+        return pltpu.make_async_remote_copy(
+            src_ref=soon_ref,
+            dst_ref=soon_got,
+            send_sem=soon_sem.at[0],
+            recv_sem=soon_sem.at[1],
+            device_id=partner(top),
+            device_id_type=pl.DeviceIdType.MESH,
+        )
+
     merge_at = [len(courses[0].stages), len(courses[2].stages)]
     canvas = dp * 2 + mp // 2
+    soon_copy().start()
     sum_copy(0).start()
     all_copy(0).start()
     state = []
     turns = (0, 1, 4, 2, 3)
+    join_turn = max(merge_at[0] + 1, len(courses[4].stages))
     lag = (0, 0, 1, 1, 0)
     for f, course in enumerate(courses):
         if not lag[f]:
@@ -824,6 +842,20 @@
             if turn == merge_at[pair] + lag[2 * pair] + 1:
                 merge_copy(pair).wait_recv()
                 own[...] = jnp.where(high, both[1], both[0]) + wide(came[...])
+        if turn == 1:
+            soon_copy().wait_recv()
+            soon_out[...] = soon_ref[...] + soon_got[...]
+        if turn == join_turn:
+            b0, b1 = bit(1), bit(2)
+            for number, (f0, f1) in enumerate(((1, 0), (0, 1), (1, 1))):
+                other = b0 + f0 * (1 - 2 * b0) + 2 * (b1 + f1 * (1 - 2 * b1))
+                cut = lanes_of(other)
+                join_buf[number, 0] = cut(owns.at[3])
+                join_buf[number, 1] = cut(owns.at[2])
+                join_copy(number).start()
+            cut = lanes_of(mp)
+            join_ref[mp, 0] = cut(owns.at[3])
+            join_ref[mp, 1] = cut(owns.at[2])
         if turn < len(sum_masks):
             sum_copy(turn).wait_recv()
             total = (part_ref[...] if turn == 0 else sum_buf[turn - 1]) + sum_got[turn]
@@ -841,16 +873,6 @@
     row = lax.broadcasted_iota(jnp.int32, (8, 128), 0)
     one_buf[0] = scalar_ref[...] + jnp.where(row == 0, square, 0.0)
     one_copy(0).start()
-    b0, b1 = bit(1), bit(2)
-    for number, (f0, f1) in enumerate(((1, 0), (0, 1), (1, 1))):
-        other = b0 + f0 * (1 - 2 * b0) + 2 * (b1 + f1 * (1 - 2 * b1))
-        cut = lanes_of(other)
-        join_buf[number, 0] = cut(owns.at[3])
-        join_buf[number, 1] = cut(owns.at[2])
-        join_copy(number).start()
-    cut = lanes_of(mp)
-    join_ref[mp, 0] = cut(owns.at[3])
-    join_ref[mp, 1] = cut(owns.at[2])
     for stage in range(len(sum_masks)):
         one_copy(stage).wait_recv()
         total = one_buf[stage] + one_got[stage]
@@ -867,6 +889,7 @@
         sum_copy(stage).wait_send()
     for stage in range(len(gather_masks)):
         all_copy(stage).wait_send()
+    soon_copy().wait_send()
     for pair in range(2):
         merge_copy(pair).wait_send()
     for f, course in enumerate(courses):
@@ -874,7 +897,7 @@
             copy(f, stage).wait_send()
 
 
-def finish(n_mp, flows, top, masks, part, mine, scalars):
+def finish(n_mp, flows, top, masks, part, mine, scalars, soon):
     budget = 3000
     height = lambda flow: flow.keep.size // D // flow.keep.shape[-2] * (-(-flow.keep.shape[-2] // 16) * 16)
     while sum(height(flow) for flow in flows) > budget:
@@ -904,22 +927,23 @@
     scratch += [pltpu.SemaphoreType.DMA((len(courses), most))] * 2
     scratch += [pltpu.SemaphoreType.DMA((len(masks),))] * 6
     scratch += [pltpu.SemaphoreType.DMA((3,))] * 2
+    scratch += [pltpu.VMEM(soon.shape, F32), pltpu.SemaphoreType.DMA((2,))]
     plan = [
         Plan(course.count, course.block, course.first, tuple(course.stages)) for course in courses
     ]
     vmem = pl.BlockSpec(memory_space=pltpu.VMEM)
     outs = [(4, 2, late[0], D // 4), courses[2].block, part.shape]
-    outs += [(canvases,) + mine.shape[1:], (8, 128)]
+    outs += [(canvases,) + mine.shape[1:], (8, 128), soon.shape]
     return pl.pallas_call(
         partial(finish_kernel, n_mp, plan, top, masks, masks[1:]),
-        in_specs=[pl.BlockSpec(memory_space=pl.ANY)] * len(courses) + [vmem] * (len(courses) + 3),
+        in_specs=[pl.BlockSpec(memory_space=pl.ANY)] * len(courses) + [vmem] * (len(courses) + 4),
         out_specs=[vmem] * len(outs),
         out_shape=[jax.ShapeDtypeStruct(shape, F32) for shape in outs],
         scratch_shapes=scratch,
         compiler_params=pltpu.CompilerParams(
             collective_id=0, has_side_effects=True, vmem_limit_bytes=58 * 1024 * 1024
         ),
-    )(*[course.sends for course in courses], *[course.keep for course in courses], part, mine, scalars)
+    )(*[course.sends for course in courses], *[course.keep for course in courses], part, mine, scalars, soon)
 
 
 class Plan:
@@ -1205,7 +1229,7 @@
 
     cond_b = bf(cond)
     units_b = unit_split(place, as_units(bf(in_proj), bf(out_proj)))
-    cap_chunk = chunk_of(place, CAP_ROWS)
+    cap_chunk = chunk_of(place, CAP_ROWS, GL if place.n <= 32 else 16)
     cap_mine = spread_rows(place, cond_b, TIME_ROWS, CAP_ROWS)
     packed = jnp.concatenate([units_b.reshape(-1, D), cap_mine], axis=0)
     ff_b = jnp.stack([bf(w_up[:, 0]), bf(w_up[:, 1]), bf(w_down).T])
@@ -1399,15 +1423,16 @@
             flows.append(Flow(place, away.reshape(shape), stages(2, order)))
             left, right, away = lax.optimization_barrier((left, right, away))
         for i, flow in enumerate(flows):
-            flow.keep = ff_grad(spot, left, right, i, 0, F32).reshape(shape)
+            flow.keep = ff_grad(spot, left, right, i, 0, BF16).reshape(shape)
         return flows
 
     def unit_flow(arrays, pairs, order):
         shape = (2,) + split_dp + (dl, D)
-        away = unit_grad(spot, arrays, pairs, 1, BF16)
+        blocks = n_dp if dl % 16 == 0 else 1
+        away = unit_grad(spot, arrays, pairs, 1, BF16, blocks)
         flow = Flow(place, away.reshape(shape), stages(1, order))
         arrays, away = lax.optimization_barrier((arrays, away))
-        flow.keep = unit_grad(spot, arrays, pairs, 0, F32).reshape(shape)
+        flow.keep = unit_grad(spot, arrays, pairs, 0, BF16, blocks).reshape(shape)
         return flow
 
     def settle(value, flows):
@@ -1503,20 +1528,16 @@
     )
     d_embed = d_state_a + layer_norm_back(d_normed_a * (1.0 + mods[1]), hat_a, inv_a)
     g_patch = mm_tn(mixed_in, d_embed, HIGH)
-    d_mod, d_kv_b, g_patch, late.keep, late.moving, early.moving = lax.optimization_barrier(
-        (d_mod, d_kv_b, g_patch, late.keep, late.moving, early.moving)
+    d_mod, d_kv_b, g_patch, late.keep, late.moving = lax.optimization_barrier(
+        (d_mod, d_kv_b, g_patch, late.keep, late.moving)
     )
     near_far = [stage for stage in stages(1, "") if stage[1] != 1]
     late_flows = late.split(
         1, [stages(1, order)[:2] + near_far for order in ("xy", "yx")]
     )
     d_mod, d_kv_b = tick((d_mod, d_kv_b), ffn_flows)
-    for flow in late_flows + [early]:
+    for flow in late_flows:
         flow.land()
-    for mask in soon_masks[4:]:
-        soon = soon + place.swap(soon, mask)
-    conv_grad = soon[: conv_grad.size // D].reshape(conv_grad.shape)
-    d_out_rows = soon[conv_grad.size // D :]
     d_mod = d_mod.reshape(slots // 4, 2, 4, owner_rows).sum(1).reshape(slots, owner_rows)
     d_silu = mm(d_mod, wide(cond_b), HIGH)
     g_block = mm_tn(d_mod, wide(silu_b), HIGH)
@@ -1531,7 +1552,7 @@
     if cap_chunk == GL:
         cap_parts = [caption, cap_act_b, d_cap_b, d_text_raw_b]
         cap_sends = cap_grad(spot, cap_parts, place.n, 1, BF16).reshape(cap_shape)
-        cap_keep = partial(cap_grad, spot, cap_parts, place.n, 0, F32)
+        cap_keep = partial(cap_grad, spot, cap_parts, place.n, 0, BF16)
     else:
         g_cap = jnp.concatenate(
             [
@@ -1544,6 +1565,11 @@
         cap_sends = bf(lax.dynamic_slice_in_dim(g_cap, 1 - c, 1, place.dp_bits + 1))
         cap_keep = partial(lax.dynamic_slice_in_dim, g_cap, c, 1, place.dp_bits + 1)
 
+    for mask in soon_masks[4:-1]:
+        soon = soon + place.swap(soon, mask)
+    soon_rows = soon.shape[0]
+    soon = jnp.pad(soon, ((0, -soon_rows % 8), (0, 0)))
+
     d_rows_six = jnp.stack([total for _, total in d_mods])
     tables_grad = jnp.concatenate(
         [d_rows_six, d_shift_o[None], d_scale_o[None], d_gain[None], g_patch], axis=0
@@ -1568,15 +1594,19 @@
     last = late_flows + cap_flows + [early]
     for flow in cap_flows:
         flow.land()
+    d_times, early.moving = lax.optimization_barrier((d_times, early.moving))
+    early.land()
     ff_own = [flow.drain().reshape(dl, FFB)[:, : FF // 4] for flow in ffn_flows]
     part_sq = sum(jnp.sum(grad * grad) for grad in [g_block] + ff_own)
     row = lax.broadcasted_iota(jnp.int32, (8, 128), 0)
     scalars = jnp.where(row == 0, part_sq, loss)
     small = jnp.pad(tables_grad, ((0, -tables_grad.shape[0] % 8), (0, 0)))
     top = n_mp << place.dp_bits - 1
-    joined, cap_own, small, d_times, scalars = finish(
-        n_mp, last, top, masks, small, d_times[None], scalars
-    )
+    joined, cap_own, small, d_times, scalars, soon = finish(
+        n_mp, last, top, masks, small, d_times[None], scalars, soon
+    )
+    conv_grad = soon[: conv_grad.size // D].reshape(conv_grad.shape)
+    d_out_rows = soon[conv_grad.size // D : soon_rows]
     tables_grad = jnp.concatenate([small[: tables_grad.shape[0]], d_out_rows], axis=0)
     d_times = d_times.reshape(-1, 2, 4, D).transpose(1, 0, 2, 3).reshape(2, slots, D)
     g_time2 = mm_tn(wide(hidden_b), d_times[0], HIGH)

time: 1180 us -> 1130 us (0.958)
  waiting for transfers between devices: 262 us -> 229 us
  Pallas kernels: 436 us -> 416 us
    ppermute x52 -> x51, waiting for transfers between devices: 121 us -> 94.5 us  [swap(): return lax.ppermute(value, AXES, [(i, i ^ mask) for i in range(self.n)])]
    pallas_call x1, Pallas kernels: 169 us -> 156 us  [finish(): pl.pallas_call(partial(finish_kernel, n_mp, plan, top, masks, masks[1:]),...]
    unnamed x516 -> x494, local copies, waits for them, and re-layouts: 37.8 us -> 33.1 us
    ppermute x13 -> x14, waiting for transfers between devices: 25.8 us -> 23.9 us  [spread_rows(): got = lax.ppermute(piece, AXES, pairs)]
    ppermute x52 -> x51, starting transfers between devices: 43.8 us -> 44.8 us  [swap(): return lax.ppermute(value, AXES, [(i, i ^ mask) for i in range(self.n)])]
    add x16 -> x15, other arithmetic: 56.8 us -> 56 us  [part(): return wide(take(self.keep)) + wide(take(self.moving))]
  transfers between devices with their start and end apart: 74 -> 74, of which waited for: 23 -> 20; matrix products, arithmetic and copies ran while one was open for 21% -> 22% of each run, Pallas kernels for 16% -> 16%
where the time goes in v3:
time: 1130 us; the launch traced here: 1120 us
  Pallas kernels  416 us (37%)
  waiting for transfers between devices  229 us (20%)
  other arithmetic  148 us (13%)
  local copies, waits for them, and re-layouts  117 us (10%)
  matrix products  93.3 us (8%)
  starting transfers between devices  91.1 us (8%)
  between operations  28 us (2%)
    pallas_call x1, Pallas kernels, finish(): pl.pallas_call(partial(finish_kernel, n_mp, plan, top, masks, masks[1:]),...  156 us
    ppermute x51, waiting for transfers between devices, swap(): return lax.ppermute(value, AXES, [(i, i ^ mask) for i in range(self.n)])  94.5 us
    dot_general x32, matrix products, dot(): lax.dot_general(left, right, (dims, ((), ())), precision=precision, prefe...  93.3 us
    pallas_call x1, Pallas kernels, ffn_backward(): pl.pallas_call(ffn_backward_kernel, grid=(FFP // CB,), in_specs=[whole_sp...  60.3 us
    add x15, other arithmetic, part(): return wide(take(self.keep)) + wide(take(self.moving))  56 us
    all_gather x1, waiting for transfers between devices, local(): ffw = lax.all_gather(ff_b.reshape(3 * dl, FFB), AXES, axis=0)  51 us
    all_gather x1, waiting for transfers between devices, local(): got = lax.all_gather(packed, AXES, axis=0)  48 us
    pallas_call x1, Pallas kernels, ffn_forward(): pl.pallas_call(ffn_forward_kernel, grid=(FFP // CB,), in_specs=[whole_spe...  45.7 us
  transfers between devices with their start and end apart: 74, of which 20 were waited for; matrix products, arithmetic and copies ran while one was open for 22% of the time, Pallas kernels for 16%

profile of v3, /device:TPU:28, one launch (start us, length us, event | category | flops | bytes accessed | tf_op | source)
XLA Modules:
  0.0 1122.5 jit_solution(2577469702592421820)
XLA Ops:
  29.2 7.6 collective-permute-done.12
  77.0 9.7 collective-permute-done.17
  92.5 9.9 collective-permute-done.23
  102.5 16.7 %collective-permute-start.24 = (bf16[2,48,1152]{2,1,0:T(8,128)(2,1)S(1)}, bf16[2,48,1152]{2,1,0:T(8,128)(2,1)S(1)}, u32[]{:S(2)}, u32[]{:S(2)}) collective-permute-start(bf16[2,48,1152]{2,1,0:T(8,128)(2,1)S(1)} %pad_maximum_fusion.18), channel_id=1, source_target_pairs={{0,16},{1,17},{2,18},{3,19},{4,20},{5,21},{6,22},{7,23},{8,24},{9,... | collective-permute-start | bytes 663560 | tf_op jit(solution)/shard_map/ppermute | solution.py:79
  122.6 20.9 %collective-permute-done.24 = bf16[2,48,1152]{2,1,0:T(8,128)(2,1)S(1)} collective-permute-done((bf16[2,48,1152]{2,1,0:T(8,128)(2,1)S(1)}, bf16[2,48,1152]{2,1,0:T(8,128)(2,1)S(1)}, u32[]{:S(2)}, u32[]{:S(2)}) %collective-permute-start.24) | collective-permute-done | bytes 221216 | tf_op jit(solution)/shard_map/ppermute | solution.py:79
  144.3 8.5 collective-permute-done.25
  155.3 20.0 %collective-permute-done.27 = bf16[4,48,1152]{2,1,0:T(8,128)(2,1)S(1)} collective-permute-done((bf16[4,48,1152]{2,1,0:T(8,128)(2,1)S(1)}, bf16[4,48,1152]{2,1,0:T(8,128)(2,1)S(1)}, u32[]{:S(2)}, u32[]{:S(2)}) %collective-permute-start.27) | collective-permute-done | bytes 442400 | tf_op jit(solution)/shard_map/ppermute | solution.py:79
  200.6 48.0 %all-gather.6.cloned.1.call-done = bf16[12800,1152]{1,0:T(8,128)(2,1)} async-done(((bf16[400,1152]{1,0:T(8,128)(2,1)}), bf16[12800,1152]{1,0:T(8,128)(2,1)}) %all-gather.6.cloned.1.call-update) | async-done | bytes 29491216 | tf_op jit(solution)/shard_map/all_gather | solution.py:1238
  248.6 7.2 slice.542
  264.8 13.6 %fusion.166 = (bf16[8,1,1,144,1152]{4,3,2,1,0:T(8,128)(2,1)}, bf16[8,1,1,144,1152]{4,3,2,1,0:T(8,128)(2,1)S(1)}, bf16[8,1,1,144,1152]{4,3,2,1,0:T(8,128)(2,1)S(1...) fusion(bf16[8,2,2,400,1152]{4,3,2,1,0:T(8,128)(2,1)} %bitcast.341), kind=kLoop, calls=%fused_computation.497 | loop fusion | bytes 42467328 | tf_op jit(solution)/shard_map/slice | solution.py:1241
  305.6 17.9 %shard_map.436.refs_3_ = bf16[512,1152]{1,0:T(8,128)(2,1)S(1)} custom-call(bf16[512,1152]{1,0:T(8,128)(2,1)S(1)} %convolution_convert_fusion.1.q_ref, bf16[512,1152]{1,0:T(8,128)(2,1)S(1)} %pad_maximum_fusion.5.k_ref, bf16[512,1152]{1,0:T(8,128)(2,1)S(1)} %pad_maximum_fusion.6.v_ref, s32[512,1]{1,0:T(8,128)S(1)} %fusion.92.tok_ref, s32[1,512]{1,0:T(1,128)S(1)} %bitcast.332), custom_call_target="tpu_custom_call" | custom-call | flops 1048576 | bytes 65536 | tf_op jit(solution)/shard_map/pallas_call | solution.py:1028
  336.2 51.0 %all-gather.4.cloned.1.call-done = bf16[32,432,768]{2,1,0:T(8,128)(2,1)} async-done(((bf16[1,432,768]{2,1,0:T(8,128)(2,1)}), bf16[32,432,768]{2,1,0:T(8,128)(2,1)}) %all-gather.4.cloned.1.call-update) | async-done | bytes 21233680 | tf_op jit(solution)/shard_map/all_gather | solution.py:1246
  390.3 45.7 %shard_map.437 = (f32[2,544,3072]{2,1,0:T(8,128)}, f32[2,512,3072]{2,1,0:T(8,128)}, bf16[512,3072]{1,0:T(8,128)(2,1)}, f32[512,1152]{1,0:T(8,128)S(1)}) custom-call(bf16[544,1152]{1,0:T(8,128)(2,1)S(1)} %copy-done.19, bf16[8,4,432,768]{3,2,1,0:T(8,128)(2,1)} %bitcast.334, bf16[8,4,432,768]{3,2,1,0:T(8,128)(2,1)} %bitcast.335, ...), custom_call_target="tpu_custom_call" | custom-call | flops 1048576 | bytes 65536 | tf_op jit(solution)/shard_map/pallas_call | solution.py:398
  468.8 60.3 %shard_map.440 = (bf16[2,512,3072]{2,1,0:T(8,128)(2,1)}, f32[2,10,3072]{2,1,0:T(8,128)S(1)}, f32[512,1152]{1,0:T(8,128)S(1)}) custom-call(bf16[544,1152]{1,0:T(8,128)(2,1)S(1)} %pad_maximum_fusion.2.d_ref, bf16[8,4,432,768]{3,2,1,0:T(8,128)(2,1)} %bitcast.337, bf16[8,4,432,768]{3,2,1,0:T(8,128)(2,1)} %bitcast.338, bf16[8,4,432,768]{3,2,1,0:T(8,128)(2,1)} %bitcast.339, ...), custom_call_target="tpu_custom_call" | custom-call | flops 1048576 | bytes 65536 | tf_op jit(solution)/shard_map/pallas_call | solution.py:509
  586.1 37.9 %shard_map.445 = (bf16[512,1152]{1,0:T(8,128)(2,1)S(1)}, f32[512,1152]{1,0:T(8,128)}, f32[512,1152]{1,0:T(8,128)}) custom-call(bf16[512,1152]{1,0:T(8,128)(2,1)S(1)} %convolution_convert_fusion.1.q_ref, bf16[512,1152]{1,0:T(8,128)(2,1)S(1)} %copy-done.8, bf16[512,1152]{1,0:T(8,128)(2,1)S(1)} %copy-done.10, ...), custom_call_target="tpu_custom_call" | custom-call | flops 1048576 | bytes 65536 | tf_op jit(solution)/shard_map/pallas_call | solution.py:1074
  686.6 11.9 %shard_map.448 = (bf16[512,1152]{1,0:T(8,128)(2,1)S(1)}, f32[9,2,128,128]{3,2,1,0:T(8,128)S(1)}, f32[9,2,8,128]{3,2,1,0:T(8,128)S(1)}) custom-call(bf16[512,1152]{1,0:T(8,128)(2,1)S(1)} %copy-done.35, f32[512,1152]{1,0:T(8,128)} %fusion.178.da_ref, f32[512,128]{1,0:T(8,128)S(1)} %copy-done.14, f32[9,2,128,128]{3,2,1,0:T(8,128)S(1)} %copy.365.kv_ref, ...), custom_call_target="tpu_custom_call" | custom-call | flops 1048576 | bytes 65536 | tf_op jit(solution)/shard_map/pallas_call | solution.py:1499
  709.7 7.3 shard_map.449
  740.0 7.2 shard_map.450
  779.5 6.8 shard_map.451
  822.1 8.4 shard_map.453
  833.4 8.6 shard_map.452
  859.1 8.0 collective-permute-done.64
  891.5 156.0 %shard_map.454 = (f32[4,2,144,288]{3,2,1,0:T(8,128)}, f32[128,1152]{1,0:T(8,128)}, f32[48,1152]{1,0:T(8,128)}, f32[16,8,1152]{2,1,0:T(8,128)}, f32[8,128]{1,0:T(8,128)}, /*index=5*/f32[88,1152]{1,0:T(8,128)}) custom-call(bf16[4,144,1152]{2,1,0:T(8,128)(2,1)} %bitcast.375, bf16[4,144,1152]{2,1,0:T(8,128)(2,1)} %bitcast.376, bf16[4,128,1152]{2,1,0:T(8,128)(2,1)} %bitcast.382, ...), custom_call_target="tpu_custom_call" | custom-call | tf_op jit(solution)/shard_map/pallas_call | solution.py:937
  1059.5 7.8 collective-permute-start.65
  (936 shorter events, 497.3 us)
Async XLA Ops:
  7.2 241.4 %all-gather.6.cloned.1.call-start = ((), (), s32[]{:S(2)}) async-start(), calls=%async_computation.4 | async-start | bytes 30412800 | tf_op jit(solution)/shard_map/all_gather | solution.py:1238
  45.5 341.7 %all-gather.4.cloned.1.call-start = ((), (), s32[]{:S(2)}) async-start(), calls=%async_computation.3 | async-start | bytes 21897216 | tf_op jit(solution)/shard_map/all_gather | solution.py:1246
  89.0 166.8 %collective-permute-start.33 = (bf16[128,2304]{1,0:T(8,128)(2,1)}, bf16[128,2304]{1,0:T(8,128)(2,1)}, u32[]{:S(2)}, u32[]{:S(2)}) collective-permute-start(bf16[128,2304]{1,0:T(8,128)(2,1)} %get-tuple-element.566), channel_id=1, source_target_pairs={{0,2},{1,3},{2,0},{3,1},{4,6},{5,7},{6,4},{7,5},{8,10},{9,11},{10,... | collective-permute-start | bytes 1769480 | tf_op jit(solution)/shard_map/ppermute | solution.py:79
  102.5 41.1 %collective-permute-start.24 = (bf16[2,48,1152]{2,1,0:T(8,128)(2,1)S(1)}, bf16[2,48,1152]{2,1,0:T(8,128)(2,1)S(1)}, u32[]{:S(2)}, u32[]{:S(2)}) collective-permute-start(bf16[2,48,1152]{2,1,0:T(8,128)(2,1)S(1)} %pad_maximum_fusion.18), channel_id=1, source_target_pairs={{0,16},{1,17},{2,18},{3,19},{4,20},{5,21},{6,22},{7,23},{8,24},{9,... | collective-permute-start | bytes 663560 | tf_op jit(solution)/shard_map/ppermute | solution.py:79
  143.9 31.6 %collective-permute-start.28 = (bf16[4,48,1152]{2,1,0:T(8,128)(2,1)S(1)}, bf16[4,48,1152]{2,1,0:T(8,128)(2,1)S(1)}, u32[]{:S(2)}, u32[]{:S(2)}) collective-permute-start(bf16[4,48,1152]{2,1,0:T(8,128)(2,1)S(1)} %pad_maximum_fusion.12), channel_id=1, source_target_pairs={{0,1},{1,0},{2,3},{3,2},{4,5},{5,4},{6,7},{7,6},{8,9},{9,8},{10,11... | collective-permute-start | bytes 1327112 | tf_op jit(solution)/shard_map/ppermute | solution.py:79
  464.7 64.4 %collective-permute-start.40 = (bf16[1,1,2,2,2,144,768]{6,5,4,3,2,1,0:T(8,128)(2,1)}, bf16[1,1,2,2,2,144,768]{6,5,4,3,2,1,0:T(8,128)(2,1)}, u32[]{:S(2)}, u32[]{:S(2)}) collective-permute-start(bf16[1,1,2,2,2,144,768]{6,5,4,3,2,1,0:T(8,128)(2,1)} %get-tuple-element.173), channel_id=1, source_target_pairs={{0,2},{1,3},{2,0},{3,1},{4,6},{5,7},{6,4},{7,5},{8,10},{9,11},{10,... | collective-permute-start | bytes 5308424 | tf_op jit(solution)/shard_map/ppermute | solution.py:79
  555.7 68.3 %collective-permute-start.45 = (bf16[1,1,2,2,1,144,768]{6,5,4,3,2,1,0:T(8,128)(2,1)}, bf16[1,1,2,2,1,144,768]{6,5,4,3,2,1,0:T(8,128)(2,1)}, u32[]{:S(2)}, u32[]{:S(2)}) collective-permute-start(bf16[1,1,2,2,1,144,768]{6,5,4,3,2,1,0:T(8,128)(2,1)} %get-tuple-element.198), channel_id=1, source_target_pairs={{0,4},{1,5},{2,6},{3,7},{4,0},{5,1},{6,2},{7,3},{8,12},{9,13},{10,... | collective-permute-start | bytes 2654216 | tf_op jit(solution)/shard_map/ppermute | solution.py:79
  579.3 44.7 %collective-permute-start.44 = (f32[82,1152]{1,0:T(8,128)S(1)}, f32[82,1152]{1,0:T(8,128)S(1)}, u32[]{:S(2)}, u32[]{:S(2)}) collective-permute-start(f32[82,1152]{1,0:T(8,128)S(1)} %fusion.158), channel_id=1, source_target_pairs={{0,2},{1,3},{2,0},{3,1},{4,6},{5,7},{6,4},{7,5},{8,10},{9,11},{10,... | collective-permute-start | bytes 1133576 | tf_op jit(solution)/shard_map/ppermute | solution.py:79
  579.9 44.1 %collective-permute-start.46 = (bf16[1,2,2,2,1,144,768]{6,5,4,3,2,1,0:T(8,128)(2,1)}, bf16[1,2,2,2,1,144,768]{6,5,4,3,2,1,0:T(8,128)(2,1)}, u32[]{:S(2)}, u32[]{:S(2)}) collective-permute-start(bf16[1,2,2,2,1,144,768]{6,5,4,3,2,1,0:T(8,128)(2,1)} %get-tuple-element.199), channel_id=1, source_target_pairs={{0,4},{1,5},{2,6},{3,7},{4,0},{5,1},{6,2},{7,3},{8,12},{9,13},{10,... | collective-permute-start | bytes 5308424 | tf_op jit(solution)/shard_map/ppermute | solution.py:79
  581.4 47.3 %collective-permute-start.47 = (bf16[1,1,2,2,2,144,768]{6,5,4,3,2,1,0:T(8,128)(2,1)}, bf16[1,1,2,2,2,144,768]{6,5,4,3,2,1,0:T(8,128)(2,1)}, u32[]{:S(2)}, u32[]{:S(2)}) collective-permute-start(bf16[1,1,2,2,2,144,768]{6,5,4,3,2,1,0:T(8,128)(2,1)} %get-tuple-element.200), channel_id=1, source_target_pairs={{0,2},{1,3},{2,0},{3,1},{4,6},{5,7},{6,4},{7,5},{8,10},{9,11},{10,... | collective-permute-start | bytes 5308424 | tf_op jit(solution)/shard_map/ppermute | solution.py:79
  659.9 38.7 %collective-permute-start.52 = (bf16[1,1,2,1,1,144,768]{6,5,4,3,2,1,0:T(8,128)(2,1)}, bf16[1,1,2,1,1,144,768]{6,5,4,3,2,1,0:T(8,128)(2,1)S(1)}, u32[]{:S(2)}, u32[]{:S(2)}) collective-permute-start(bf16[1,1,2,1,1,144,768]{6,5,4,3,2,1,0:T(8,128)(2,1)} %get-tuple-element.232), channel_id=1, source_target_pairs={{0,8},{1,9},{2,10},{3,11},{4,12},{5,13},{6,14},{7,15},{8,0},{9,1},... | collective-permute-start | bytes 1327112 | tf_op jit(solution)/shard_map/ppermute | solution.py:79
  661.5 37.1 %collective-permute-start.53 = (bf16[1,1,2,2,1,144,768]{6,5,4,3,2,1,0:T(8,128)(2,1)}, bf16[1,1,2,2,1,144,768]{6,5,4,3,2,1,0:T(8,128)(2,1)S(1)}, u32[]{:S(2)}, u32[]{:S(2)}) collective-permute-start(bf16[1,1,2,2,1,144,768]{6,5,4,3,2,1,0:T(8,128)(2,1)} %get-tuple-element.233), channel_id=1, source_target_pairs={{0,2},{1,3},{2,0},{3,1},{4,6},{5,7},{6,4},{7,5},{8,10},{9,11},{10,... | collective-permute-start | bytes 2654216 | tf_op jit(solution)/shard_map/ppermute | solution.py:79
  662.9 35.7 %collective-permute-start.54 = (bf16[1,1,2,2,1,144,768]{6,5,4,3,2,1,0:T(8,128)(2,1)}, bf16[1,1,2,2,1,144,768]{6,5,4,3,2,1,0:T(8,128)(2,1)S(1)}, u32[]{:S(2)}, u32[]{:S(2)}) collective-permute-start(bf16[1,1,2,2,1,144,768]{6,5,4,3,2,1,0:T(8,128)(2,1)} %get-tuple-element.234), channel_id=1, source_target_pairs={{0,4},{1,5},{2,6},{3,7},{4,0},{5,1},{6,2},{7,3},{8,12},{9,13},{10,... | collective-permute-start | bytes 2654216 | tf_op jit(solution)/shard_map/ppermute | solution.py:79
  747.2 39.1 %collective-permute-start.56 = (bf16[2,2,2,2,144,1152]{5,4,3,2,1,0:T(8,128)(2,1)}, bf16[2,2,2,2,144,1152]{5,4,3,2,1,0:T(8,128)(2,1)}, u32[]{:S(2)}, u32[]{:S(2)}) collective-permute-start(bf16[2,2,2,2,144,1152]{5,4,3,2,1,0:T(8,128)(2,1)} %bitcast.374), channel_id=1, source_target_pairs={{0,1},{1,0},{2,3},{3,2},{4,5},{5,4},{6,7},{7,6},{8,9},{9,8},{10,11... | collective-permute-start | bytes 15925256 | tf_op jit(solution)/shard_map/ppermute | solution.py:79
  754.6 117.2 %collective-permute-start.61 = (f32[4,1152]{1,0:T(4,128)}, f32[4,1152]{1,0:T(4,128)}, u32[]{:S(2)}, u32[]{:S(2)}) collective-permute-start(f32[4,1152]{1,0:T(4,128)} %add_add_fusion.2), channel_id=1, source_target_pairs={{0,1},{1,0},{2,3},{3,2},{4,5},{5,4},{6,7},{7,6},{8,9},{9,8},{10,11... | collective-permute-start | bytes 55304 | tf_op jit(solution)/shard_map/ppermute | solution.py:79
  759.5 31.7 %collective-permute-start.57 = (bf16[1,1,1,1,1,144,768]{6,5,4,3,2,1,0:T(8,128)(2,1)}, bf16[1,1,1,1,1,144,768]{6,5,4,3,2,1,0:T(8,128)(2,1)}, u32[]{:S(2)}, u32[]{:S(2)}) collective-permute-start(bf16[1,1,1,1,1,144,768]{6,5,4,3,2,1,0:T(8,128)(2,1)} %add_convert_fusion.18), channel_id=1, source_target_pairs={{0,16},{1,17},{2,18},{3,19},{4,20},{5,21},{6,22},{7,23},{8,24},{9,... | collective-permute-start | bytes 663560 | tf_op jit(solution)/shard_map/ppermute | solution.py:79
  786.3 91.1 %collective-permute-start.62 = (bf16[1,2,2,2,144,1152]{5,4,3,1,2,0:T(8,128)(2,1)}, bf16[1,2,2,2,144,1152]{5,4,3,1,2,0:T(8,128)(2,1)}, u32[]{:S(2)}, u32[]{:S(2)}) collective-permute-start(bf16[1,2,2,2,144,1152]{5,4,3,1,2,0:T(8,128)(2,1)} %get-tuple-element.271), channel_id=1, source_target_pairs={{0,2},{1,3},{2,0},{3,1},{4,6},{5,7},{6,4},{7,5},{8,10},{9,11},{10,... | collective-permute-start | bytes 7962632 | tf_op jit(solution)/shard_map/ppermute | solution.py:79
  804.4 51.3 %collective-permute-start.63 = (bf16[1,1,1,1,1,144,768]{6,5,4,3,2,1,0:T(8,128)(2,1)}, bf16[1,1,1,1,1,144,768]{6,5,4,3,2,1,0:T(8,128)(2,1)}, u32[]{:S(2)}, u32[]{:S(2)}) collective-permute-start(bf16[1,1,1,1,1,144,768]{6,5,4,3,2,1,0:T(8,128)(2,1)} %add_convert_fusion.17), channel_id=1, source_target_pairs={{0,16},{1,17},{2,18},{3,19},{4,20},{5,21},{6,22},{7,23},{8,24},{9,... | collective-permute-start | bytes 663560 | tf_op jit(solution)/shard_map/ppermute | solution.py:79
  807.5 62.9 %all-to-all-start.2 = ((f32[32,1,4608]{2,1,0:T(1,128)}), f32[32,1,4608]{2,1,0:T(1,128)}, u32[]{:S(2)}, u32[]{:S(2)}) async-start(f32[32,1,4608]{2,1,0:T(1,128)} %all_to_all.18), calls=%async_computation.2 | async-start | bytes 1179648 | tf_op jit(solution)/shard_map/all_to_all | solution.py:1579
  830.5 52.6 %collective-permute-start.60 = (bf16[2,2,2,2,1,128,1152]{6,5,3,2,4,1,0:T(8,128)(2,1)}, bf16[2,2,2,2,1,128,1152]{6,5,3,2,4,1,0:T(8,128)(2,1)}, u32[]{:S(2)}, u32[]{:S(2)}) collective-permute-start(bf16[2,2,2,2,1,128,1152]{6,5,3,2,4,1,0:T(8,128)(2,1)} %bitcast.383), channel_id=1, source_target_pairs={{0,1},{1,0},{2,3},{3,2},{4,5},{5,4},{6,7},{7,6},{8,9},{9,8},{10,11... | collective-permute-start | bytes 14155784 | tf_op jit(solution)/shard_map/ppermute | solution.py:79
  1051.9 56.9 %collective-permute-start.68 = (bf16[128,1152]{1,0:T(8,128)(2,1)}, bf16[128,1152]{1,0:T(8,128)(2,1)}, u32[]{:S(2)}, u32[]{:S(2)}) collective-permute-start(bf16[128,1152]{1,0:T(8,128)(2,1)} %convert_element_type.521), channel_id=1, source_target_pairs={{0,3},{3,4},{6,5},{9,6},{17,9},{20,10},{23,11},{26,12},{29,13}} | collective-permute-start | bytes 884744 | tf_op jit(solution)/shard_map/ppermute | solution.py:164
  1056.7 52.0 %collective-permute-start.67 = (bf16[128,1152]{1,0:T(8,128)(2,1)}, bf16[128,1152]{1,0:T(8,128)(2,1)}, u32[]{:S(2)}, u32[]{:S(2)}) collective-permute-start(bf16[128,1152]{1,0:T(8,128)(2,1)} %convert_element_type.521), channel_id=1, source_target_pairs={{2,4},{5,5},{8,6},{11,7},{14,8},{16,9},{19,10},{22,11},{25,12},{28... | collective-permute-start | bytes 884744 | tf_op jit(solution)/shard_map/ppermute | solution.py:164
  1058.1 50.6 %collective-permute-start.66 = (bf16[128,1152]{1,0:T(8,128)(2,1)}, bf16[128,1152]{1,0:T(8,128)(2,1)}, u32[]{:S(2)}, u32[]{:S(2)}) collective-permute-start(bf16[128,1152]{1,0:T(8,128)(2,1)} %convert_element_type.521), channel_id=1, source_target_pairs={{1,4},{4,5},{7,6},{10,7},{13,8},{15,9},{18,10},{21,11},{24,12},{27... | collective-permute-start | bytes 884744 | tf_op jit(solution)/shard_map/ppermute | solution.py:164
  1059.5 49.2 %collective-permute-start.65 = (bf16[128,1152]{1,0:T(8,128)(2,1)}, bf16[128,1152]{1,0:T(8,128)(2,1)}, u32[]{:S(2)}, u32[]{:S(2)}) collective-permute-start(bf16[128,1152]{1,0:T(8,128)(2,1)} %convert_element_type.521), channel_id=1, source_target_pairs={{0,4},{3,5},{6,6},{9,7},{12,8},{14,9},{17,10},{20,11},{23,12},{26,... | collective-permute-start | bytes 884744 | tf_op jit(solution)/shard_map/ppermute | solution.py:164
  (286 other events, 4045.2 us)
Sparse Core Ops, SparseCore 0:
  45.6 202.9 all-gather.5
  252.1 135.0 all-gather.3

commit v4 on v3

--- a/solution.py
+++ b/solution.py
@@ -348,13 +348,13 @@
             act_l[k, at] = pltpu.roll(a, 1, 0) * left_ref[...]
             act_r[k, at] = pltpu.roll(a, ROW - 1, 0) * right_ref[...]
 
-    @pl.loop(0, rows)
+    @pl.loop(0, rows, unroll=2)
     def _(r):
         fill(r, 1.0)
 
     fill(rows, on)
 
-    @pl.loop(0, rows)
+    @pl.loop(0, rows, unroll=2)
     def _(r):
         z = []
         for k in range(2):
@@ -454,7 +454,7 @@
     def fold(value):
         return value[0:8] + value[8:16] + value[16:24] + value[24:32]
 
-    @pl.loop(0, rows)
+    @pl.loop(0, rows, unroll=2)
     def _(r):
         at = pl.ds(pl.multiple_of(r * ROW, ROW), ROW)
         fill(r, z_ref[0, at], z_ref[1, at], 1.0, True)
@@ -477,7 +477,7 @@
                         acc[k, dr * 3 + dc] += fold(value * a)
             du_ref[k, at] = bf(total * (gate + a * (1.0 - gate)))
 
-    @pl.loop(0, rows - 1)
+    @pl.loop(0, rows - 1, unroll=3)
     def _(r):
         back(r, (0, 1, 2))
 
@@ -992,7 +992,7 @@
 
 WIN = 256
 QROWS = 512
-BROWS = 256
+BROWS = 512
 
 
 def head_window(h):

time: 1130 us -> 1130 us (level)
  Pallas kernels: 416 us -> 400 us
    ppermute x51, waiting for transfers between devices: 94.5 us -> 106 us  [swap(): return lax.ppermute(value, AXES, [(i, i ^ mask) for i in range(self.n)])]
    pallas_call x1, Pallas kernels: 37.9 us -> 26.5 us  [cross_backward(): pl.pallas_call(cross_backward_kernel, grid=(XHEADS,), in_specs=[whole_spe...]
  transfers between devices with their start and end apart: 74 -> 74, of which waited for: 20 -> 21; matrix products, arithmetic and copies ran while one was open for 22% -> 22% of each run, Pallas kernels for 16% -> 15%
where the time goes in v4:
time: 1130 us; the launch traced here: 1120 us
  Pallas kernels  400 us (35%)
  waiting for transfers between devices  240 us (21%)
  other arithmetic  148 us (13%)
  local copies, waits for them, and re-layouts  117 us (10%)
  matrix products  93.2 us (8%)
  starting transfers between devices  91.1 us (8%)
  between operations  28 us (2%)
    pallas_call x1, Pallas kernels, finish(): pl.pallas_call(partial(finish_kernel, n_mp, plan, top, masks, masks[1:]),...  156 us
    ppermute x51, waiting for transfers between devices, swap(): return lax.ppermute(value, AXES, [(i, i ^ mask) for i in range(self.n)])  106 us
    dot_general x32, matrix products, dot(): lax.dot_general(left, right, (dims, ((), ())), precision=precision, prefe...  93.2 us
    pallas_call x1, Pallas kernels, ffn_backward(): pl.pallas_call(ffn_backward_kernel, grid=(FFP // CB,), in_specs=[whole_sp...  57.5 us
    add x15, other arithmetic, part(): return wide(take(self.keep)) + wide(take(self.moving))  56 us
    all_gather x1, waiting for transfers between devices, local(): ffw = lax.all_gather(ff_b.reshape(3 * dl, FFB), AXES, axis=0)  50.9 us
    all_gather x1, waiting for transfers between devices, local(): got = lax.all_gather(packed, AXES, axis=0)  48 us
    ppermute x51, starting transfers between devices, swap(): return lax.ppermute(value, AXES, [(i, i ^ mask) for i in range(self.n)])  44.9 us
  transfers between devices with their start and end apart: 74, of which 21 were waited for; matrix products, arithmetic and copies ran while one was open for 22% of the time, Pallas kernels for 15%

profile of v4, /device:TPU:28, one launch (start us, length us, event | category | flops | bytes accessed | tf_op | source)
XLA Modules:
  0.0 1117.3 jit_solution(14770143031679167971)
XLA Ops:
  29.2 7.6 collective-permute-done.12
  77.0 9.7 collective-permute-done.17
  92.5 9.9 collective-permute-done.23
  102.5 16.7 %collective-permute-start.24 = (bf16[2,48,1152]{2,1,0:T(8,128)(2,1)S(1)}, bf16[2,48,1152]{2,1,0:T(8,128)(2,1)S(1)}, u32[]{:S(2)}, u32[]{:S(2)}) collective-permute-start(bf16[2,48,1152]{2,1,0:T(8,128)(2,1)S(1)} %pad_maximum_fusion.18), channel_id=1, source_target_pairs={{0,16},{1,17},{2,18},{3,19},{4,20},{5,21},{6,22},{7,23},{8,24},{9,... | collective-permute-start | bytes 663560 | tf_op jit(solution)/shard_map/ppermute | solution.py:79
  122.6 20.9 %collective-permute-done.24 = bf16[2,48,1152]{2,1,0:T(8,128)(2,1)S(1)} collective-permute-done((bf16[2,48,1152]{2,1,0:T(8,128)(2,1)S(1)}, bf16[2,48,1152]{2,1,0:T(8,128)(2,1)S(1)}, u32[]{:S(2)}, u32[]{:S(2)}) %collective-permute-start.24) | collective-permute-done | bytes 221216 | tf_op jit(solution)/shard_map/ppermute | solution.py:79
  144.3 8.5 collective-permute-done.25
  155.3 20.0 %collective-permute-done.27 = bf16[4,48,1152]{2,1,0:T(8,128)(2,1)S(1)} collective-permute-done((bf16[4,48,1152]{2,1,0:T(8,128)(2,1)S(1)}, bf16[4,48,1152]{2,1,0:T(8,128)(2,1)S(1)}, u32[]{:S(2)}, u32[]{:S(2)}) %collective-permute-start.27) | collective-permute-done | bytes 442400 | tf_op jit(solution)/shard_map/ppermute | solution.py:79
  200.6 48.0 %all-gather.6.cloned.1.call-done = bf16[12800,1152]{1,0:T(8,128)(2,1)} async-done(((bf16[400,1152]{1,0:T(8,128)(2,1)}), bf16[12800,1152]{1,0:T(8,128)(2,1)}) %all-gather.6.cloned.1.call-update) | async-done | bytes 29491216 | tf_op jit(solution)/shard_map/all_gather | solution.py:1238
  264.8 13.6 %fusion.166 = (bf16[8,1,1,144,1152]{4,3,2,1,0:T(8,128)(2,1)}, bf16[8,1,1,144,1152]{4,3,2,1,0:T(8,128)(2,1)S(1)}, bf16[8,1,1,144,1152]{4,3,2,1,0:T(8,128)(2,1)S(1...) fusion(bf16[8,2,2,400,1152]{4,3,2,1,0:T(8,128)(2,1)} %bitcast.341), kind=kLoop, calls=%fused_computation.497 | loop fusion | bytes 42467328 | tf_op jit(solution)/shard_map/slice | solution.py:1241
  305.6 17.9 %shard_map.436.refs_3_ = bf16[512,1152]{1,0:T(8,128)(2,1)S(1)} custom-call(bf16[512,1152]{1,0:T(8,128)(2,1)S(1)} %convolution_convert_fusion.1.q_ref, bf16[512,1152]{1,0:T(8,128)(2,1)S(1)} %pad_maximum_fusion.5.k_ref, bf16[512,1152]{1,0:T(8,128)(2,1)S(1)} %pad_maximum_fusion.6.v_ref, s32[512,1]{1,0:T(8,128)S(1)} %fusion.92.tok_ref, s32[1,512]{1,0:T(1,128)S(1)} %bitcast.332), custom_call_target="tpu_custom_call" | custom-call | flops 1048576 | bytes 65536 | tf_op jit(solution)/shard_map/pallas_call | solution.py:1028
  336.2 50.9 %all-gather.4.cloned.1.call-done = bf16[32,432,768]{2,1,0:T(8,128)(2,1)} async-done(((bf16[1,432,768]{2,1,0:T(8,128)(2,1)}), bf16[32,432,768]{2,1,0:T(8,128)(2,1)}) %all-gather.4.cloned.1.call-update) | async-done | bytes 21233680 | tf_op jit(solution)/shard_map/all_gather | solution.py:1246
  390.3 43.4 %shard_map.437 = (f32[2,544,3072]{2,1,0:T(8,128)}, f32[2,512,3072]{2,1,0:T(8,128)}, bf16[512,3072]{1,0:T(8,128)(2,1)}, f32[512,1152]{1,0:T(8,128)S(1)}) custom-call(bf16[544,1152]{1,0:T(8,128)(2,1)S(1)} %copy-done.19, bf16[8,4,432,768]{3,2,1,0:T(8,128)(2,1)} %bitcast.334, bf16[8,4,432,768]{3,2,1,0:T(8,128)(2,1)} %bitcast.335, ...), custom_call_target="tpu_custom_call" | custom-call | flops 1048576 | bytes 65536 | tf_op jit(solution)/shard_map/pallas_call | solution.py:398
  466.4 57.5 %shard_map.440 = (bf16[2,512,3072]{2,1,0:T(8,128)(2,1)}, f32[2,10,3072]{2,1,0:T(8,128)S(1)}, f32[512,1152]{1,0:T(8,128)S(1)}) custom-call(bf16[544,1152]{1,0:T(8,128)(2,1)S(1)} %pad_maximum_fusion.2.d_ref, bf16[8,4,432,768]{3,2,1,0:T(8,128)(2,1)} %bitcast.337, bf16[8,4,432,768]{3,2,1,0:T(8,128)(2,1)} %bitcast.338, bf16[8,4,432,768]{3,2,1,0:T(8,128)(2,1)} %bitcast.339, ...), custom_call_target="tpu_custom_call" | custom-call | flops 1048576 | bytes 65536 | tf_op jit(solution)/shard_map/pallas_call | solution.py:509
  580.9 26.5 %shard_map.445 = (bf16[512,1152]{1,0:T(8,128)(2,1)S(1)}, f32[512,1152]{1,0:T(8,128)}, f32[512,1152]{1,0:T(8,128)}) custom-call(bf16[512,1152]{1,0:T(8,128)(2,1)S(1)} %convolution_convert_fusion.1.q_ref, bf16[512,1152]{1,0:T(8,128)(2,1)S(1)} %copy-done.8, bf16[512,1152]{1,0:T(8,128)(2,1)S(1)} %copy-done.10, ...), custom_call_target="tpu_custom_call" | custom-call | flops 1048576 | bytes 65536 | tf_op jit(solution)/shard_map/pallas_call | solution.py:1074
  607.5 7.9 collective-permute-done.46
  615.4 8.2 collective-permute-done.47
  681.5 11.9 %shard_map.448 = (bf16[512,1152]{1,0:T(8,128)(2,1)S(1)}, f32[9,2,128,128]{3,2,1,0:T(8,128)S(1)}, f32[9,2,8,128]{3,2,1,0:T(8,128)S(1)}) custom-call(bf16[512,1152]{1,0:T(8,128)(2,1)S(1)} %copy-done.35, f32[512,1152]{1,0:T(8,128)} %fusion.178.da_ref, f32[512,128]{1,0:T(8,128)S(1)} %copy-done.14, f32[9,2,128,128]{3,2,1,0:T(8,128)S(1)} %copy.365.kv_ref, ...), custom_call_target="tpu_custom_call" | custom-call | flops 1048576 | bytes 65536 | tf_op jit(solution)/shard_map/pallas_call | solution.py:1499
  704.6 7.3 shard_map.449
  734.9 7.2 shard_map.450
  817.0 8.4 shard_map.453
  828.3 8.6 shard_map.452
  854.0 8.0 collective-permute-done.64
  886.3 156.0 %shard_map.454 = (f32[4,2,144,288]{3,2,1,0:T(8,128)}, f32[128,1152]{1,0:T(8,128)}, f32[48,1152]{1,0:T(8,128)}, f32[16,8,1152]{2,1,0:T(8,128)}, f32[8,128]{1,0:T(8,128)}, /*index=5*/f32[88,1152]{1,0:T(8,128)}) custom-call(bf16[4,144,1152]{2,1,0:T(8,128)(2,1)} %bitcast.375, bf16[4,144,1152]{2,1,0:T(8,128)(2,1)} %bitcast.376, bf16[4,128,1152]{2,1,0:T(8,128)(2,1)} %bitcast.382, ...), custom_call_target="tpu_custom_call" | custom-call | tf_op jit(solution)/shard_map/pallas_call | solution.py:937
  1054.4 7.8 collective-permute-start.65
  (936 shorter events, 506.8 us)
Async XLA Ops:
  7.2 241.4 %all-gather.6.cloned.1.call-start = ((), (), s32[]{:S(2)}) async-start(), calls=%async_computation.4 | async-start | bytes 30412800 | tf_op jit(solution)/shard_map/all_gather | solution.py:1238
  45.5 341.7 %all-gather.4.cloned.1.call-start = ((), (), s32[]{:S(2)}) async-start(), calls=%async_computation.3 | async-start | bytes 21897216 | tf_op jit(solution)/shard_map/all_gather | solution.py:1246
  89.0 166.8 %collective-permute-start.33 = (bf16[128,2304]{1,0:T(8,128)(2,1)}, bf16[128,2304]{1,0:T(8,128)(2,1)}, u32[]{:S(2)}, u32[]{:S(2)}) collective-permute-start(bf16[128,2304]{1,0:T(8,128)(2,1)} %get-tuple-element.566), channel_id=1, source_target_pairs={{0,2},{1,3},{2,0},{3,1},{4,6},{5,7},{6,4},{7,5},{8,10},{9,11},{10,... | collective-permute-start | bytes 1769480 | tf_op jit(solution)/shard_map/ppermute | solution.py:79
  102.5 41.1 %collective-permute-start.24 = (bf16[2,48,1152]{2,1,0:T(8,128)(2,1)S(1)}, bf16[2,48,1152]{2,1,0:T(8,128)(2,1)S(1)}, u32[]{:S(2)}, u32[]{:S(2)}) collective-permute-start(bf16[2,48,1152]{2,1,0:T(8,128)(2,1)S(1)} %pad_maximum_fusion.18), channel_id=1, source_target_pairs={{0,16},{1,17},{2,18},{3,19},{4,20},{5,21},{6,22},{7,23},{8,24},{9,... | collective-permute-start | bytes 663560 | tf_op jit(solution)/shard_map/ppermute | solution.py:79
  143.9 31.6 %collective-permute-start.28 = (bf16[4,48,1152]{2,1,0:T(8,128)(2,1)S(1)}, bf16[4,48,1152]{2,1,0:T(8,128)(2,1)S(1)}, u32[]{:S(2)}, u32[]{:S(2)}) collective-permute-start(bf16[4,48,1152]{2,1,0:T(8,128)(2,1)S(1)} %pad_maximum_fusion.12), channel_id=1, source_target_pairs={{0,1},{1,0},{2,3},{3,2},{4,5},{5,4},{6,7},{7,6},{8,9},{9,8},{10,11... | collective-permute-start | bytes 1327112 | tf_op jit(solution)/shard_map/ppermute | solution.py:79
  462.3 61.6 %collective-permute-start.40 = (bf16[1,1,2,2,2,144,768]{6,5,4,3,2,1,0:T(8,128)(2,1)}, bf16[1,1,2,2,2,144,768]{6,5,4,3,2,1,0:T(8,128)(2,1)}, u32[]{:S(2)}, u32[]{:S(2)}) collective-permute-start(bf16[1,1,2,2,2,144,768]{6,5,4,3,2,1,0:T(8,128)(2,1)} %get-tuple-element.173), channel_id=1, source_target_pairs={{0,2},{1,3},{2,0},{3,1},{4,6},{5,7},{6,4},{7,5},{8,10},{9,11},{10,... | collective-permute-start | bytes 5308424 | tf_op jit(solution)/shard_map/ppermute | solution.py:79
  550.6 56.8 %collective-permute-start.45 = (bf16[1,1,2,2,1,144,768]{6,5,4,3,2,1,0:T(8,128)(2,1)}, bf16[1,1,2,2,1,144,768]{6,5,4,3,2,1,0:T(8,128)(2,1)}, u32[]{:S(2)}, u32[]{:S(2)}) collective-permute-start(bf16[1,1,2,2,1,144,768]{6,5,4,3,2,1,0:T(8,128)(2,1)} %get-tuple-element.198), channel_id=1, source_target_pairs={{0,4},{1,5},{2,6},{3,7},{4,0},{5,1},{6,2},{7,3},{8,12},{9,13},{10,... | collective-permute-start | bytes 2654216 | tf_op jit(solution)/shard_map/ppermute | solution.py:79
  574.1 33.3 %collective-permute-start.44 = (f32[82,1152]{1,0:T(8,128)S(1)}, f32[82,1152]{1,0:T(8,128)S(1)}, u32[]{:S(2)}, u32[]{:S(2)}) collective-permute-start(f32[82,1152]{1,0:T(8,128)S(1)} %fusion.158), channel_id=1, source_target_pairs={{0,2},{1,3},{2,0},{3,1},{4,6},{5,7},{6,4},{7,5},{8,10},{9,11},{10,... | collective-permute-start | bytes 1133576 | tf_op jit(solution)/shard_map/ppermute | solution.py:79
  574.7 40.6 %collective-permute-start.46 = (bf16[1,2,2,2,1,144,768]{6,5,4,3,2,1,0:T(8,128)(2,1)}, bf16[1,2,2,2,1,144,768]{6,5,4,3,2,1,0:T(8,128)(2,1)}, u32[]{:S(2)}, u32[]{:S(2)}) collective-permute-start(bf16[1,2,2,2,1,144,768]{6,5,4,3,2,1,0:T(8,128)(2,1)} %get-tuple-element.199), channel_id=1, source_target_pairs={{0,4},{1,5},{2,6},{3,7},{4,0},{5,1},{6,2},{7,3},{8,12},{9,13},{10,... | collective-permute-start | bytes 5308424 | tf_op jit(solution)/shard_map/ppermute | solution.py:79
  576.2 47.3 %collective-permute-start.47 = (bf16[1,1,2,2,2,144,768]{6,5,4,3,2,1,0:T(8,128)(2,1)}, bf16[1,1,2,2,2,144,768]{6,5,4,3,2,1,0:T(8,128)(2,1)}, u32[]{:S(2)}, u32[]{:S(2)}) collective-permute-start(bf16[1,1,2,2,2,144,768]{6,5,4,3,2,1,0:T(8,128)(2,1)} %get-tuple-element.200), channel_id=1, source_target_pairs={{0,2},{1,3},{2,0},{3,1},{4,6},{5,7},{6,4},{7,5},{8,10},{9,11},{10,... | collective-permute-start | bytes 5308424 | tf_op jit(solution)/shard_map/ppermute | solution.py:79
  654.8 38.7 %collective-permute-start.52 = (bf16[1,1,2,1,1,144,768]{6,5,4,3,2,1,0:T(8,128)(2,1)}, bf16[1,1,2,1,1,144,768]{6,5,4,3,2,1,0:T(8,128)(2,1)S(1)}, u32[]{:S(2)}, u32[]{:S(2)}) collective-permute-start(bf16[1,1,2,1,1,144,768]{6,5,4,3,2,1,0:T(8,128)(2,1)} %get-tuple-element.232), channel_id=1, source_target_pairs={{0,8},{1,9},{2,10},{3,11},{4,12},{5,13},{6,14},{7,15},{8,0},{9,1},... | collective-permute-start | bytes 1327112 | tf_op jit(solution)/shard_map/ppermute | solution.py:79
  656.3 37.1 %collective-permute-start.53 = (bf16[1,1,2,2,1,144,768]{6,5,4,3,2,1,0:T(8,128)(2,1)}, bf16[1,1,2,2,1,144,768]{6,5,4,3,2,1,0:T(8,128)(2,1)S(1)}, u32[]{:S(2)}, u32[]{:S(2)}) collective-permute-start(bf16[1,1,2,2,1,144,768]{6,5,4,3,2,1,0:T(8,128)(2,1)} %get-tuple-element.233), channel_id=1, source_target_pairs={{0,2},{1,3},{2,0},{3,1},{4,6},{5,7},{6,4},{7,5},{8,10},{9,11},{10,... | collective-permute-start | bytes 2654216 | tf_op jit(solution)/shard_map/ppermute | solution.py:79
  657.8 35.7 %collective-permute-start.54 = (bf16[1,1,2,2,1,144,768]{6,5,4,3,2,1,0:T(8,128)(2,1)}, bf16[1,1,2,2,1,144,768]{6,5,4,3,2,1,0:T(8,128)(2,1)S(1)}, u32[]{:S(2)}, u32[]{:S(2)}) collective-permute-start(bf16[1,1,2,2,1,144,768]{6,5,4,3,2,1,0:T(8,128)(2,1)} %get-tuple-element.234), channel_id=1, source_target_pairs={{0,4},{1,5},{2,6},{3,7},{4,0},{5,1},{6,2},{7,3},{8,12},{9,13},{10,... | collective-permute-start | bytes 2654216 | tf_op jit(solution)/shard_map/ppermute | solution.py:79
  742.1 39.1 %collective-permute-start.56 = (bf16[2,2,2,2,144,1152]{5,4,3,2,1,0:T(8,128)(2,1)}, bf16[2,2,2,2,144,1152]{5,4,3,2,1,0:T(8,128)(2,1)}, u32[]{:S(2)}, u32[]{:S(2)}) collective-permute-start(bf16[2,2,2,2,144,1152]{5,4,3,2,1,0:T(8,128)(2,1)} %bitcast.374), channel_id=1, source_target_pairs={{0,1},{1,0},{2,3},{3,2},{4,5},{5,4},{6,7},{7,6},{8,9},{9,8},{10,11... | collective-permute-start | bytes 15925256 | tf_op jit(solution)/shard_map/ppermute | solution.py:79
  749.5 117.2 %collective-permute-start.61 = (f32[4,1152]{1,0:T(4,128)}, f32[4,1152]{1,0:T(4,128)}, u32[]{:S(2)}, u32[]{:S(2)}) collective-permute-start(f32[4,1152]{1,0:T(4,128)} %add_add_fusion.2), channel_id=1, source_target_pairs={{0,1},{1,0},{2,3},{3,2},{4,5},{5,4},{6,7},{7,6},{8,9},{9,8},{10,11... | collective-permute-start | bytes 55304 | tf_op jit(solution)/shard_map/ppermute | solution.py:79
  754.4 31.7 %collective-permute-start.57 = (bf16[1,1,1,1,1,144,768]{6,5,4,3,2,1,0:T(8,128)(2,1)}, bf16[1,1,1,1,1,144,768]{6,5,4,3,2,1,0:T(8,128)(2,1)}, u32[]{:S(2)}, u32[]{:S(2)}) collective-permute-start(bf16[1,1,1,1,1,144,768]{6,5,4,3,2,1,0:T(8,128)(2,1)} %add_convert_fusion.18), channel_id=1, source_target_pairs={{0,16},{1,17},{2,18},{3,19},{4,20},{5,21},{6,22},{7,23},{8,24},{9,... | collective-permute-start | bytes 663560 | tf_op jit(solution)/shard_map/ppermute | solution.py:79
  781.2 91.1 %collective-permute-start.62 = (bf16[1,2,2,2,144,1152]{5,4,3,1,2,0:T(8,128)(2,1)}, bf16[1,2,2,2,144,1152]{5,4,3,1,2,0:T(8,128)(2,1)}, u32[]{:S(2)}, u32[]{:S(2)}) collective-permute-start(bf16[1,2,2,2,144,1152]{5,4,3,1,2,0:T(8,128)(2,1)} %get-tuple-element.271), channel_id=1, source_target_pairs={{0,2},{1,3},{2,0},{3,1},{4,6},{5,7},{6,4},{7,5},{8,10},{9,11},{10,... | collective-permute-start | bytes 7962632 | tf_op jit(solution)/shard_map/ppermute | solution.py:79
  799.3 51.4 %collective-permute-start.63 = (bf16[1,1,1,1,1,144,768]{6,5,4,3,2,1,0:T(8,128)(2,1)}, bf16[1,1,1,1,1,144,768]{6,5,4,3,2,1,0:T(8,128)(2,1)}, u32[]{:S(2)}, u32[]{:S(2)}) collective-permute-start(bf16[1,1,1,1,1,144,768]{6,5,4,3,2,1,0:T(8,128)(2,1)} %add_convert_fusion.17), channel_id=1, source_target_pairs={{0,16},{1,17},{2,18},{3,19},{4,20},{5,21},{6,22},{7,23},{8,24},{9,... | collective-permute-start | bytes 663560 | tf_op jit(solution)/shard_map/ppermute | solution.py:79
  802.4 62.9 %all-to-all-start.2 = ((f32[32,1,4608]{2,1,0:T(1,128)}), f32[32,1,4608]{2,1,0:T(1,128)}, u32[]{:S(2)}, u32[]{:S(2)}) async-start(f32[32,1,4608]{2,1,0:T(1,128)} %all_to_all.18), calls=%async_computation.2 | async-start | bytes 1179648 | tf_op jit(solution)/shard_map/all_to_all | solution.py:1579
  825.4 52.6 %collective-permute-start.60 = (bf16[2,2,2,2,1,128,1152]{6,5,3,2,4,1,0:T(8,128)(2,1)}, bf16[2,2,2,2,1,128,1152]{6,5,3,2,4,1,0:T(8,128)(2,1)}, u32[]{:S(2)}, u32[]{:S(2)}) collective-permute-start(bf16[2,2,2,2,1,128,1152]{6,5,3,2,4,1,0:T(8,128)(2,1)} %bitcast.383), channel_id=1, source_target_pairs={{0,1},{1,0},{2,3},{3,2},{4,5},{5,4},{6,7},{7,6},{8,9},{9,8},{10,11... | collective-permute-start | bytes 14155784 | tf_op jit(solution)/shard_map/ppermute | solution.py:79
  1046.8 56.9 %collective-permute-start.68 = (bf16[128,1152]{1,0:T(8,128)(2,1)}, bf16[128,1152]{1,0:T(8,128)(2,1)}, u32[]{:S(2)}, u32[]{:S(2)}) collective-permute-start(bf16[128,1152]{1,0:T(8,128)(2,1)} %convert_element_type.521), channel_id=1, source_target_pairs={{0,3},{3,4},{6,5},{9,6},{17,9},{20,10},{23,11},{26,12},{29,13}} | collective-permute-start | bytes 884744 | tf_op jit(solution)/shard_map/ppermute | solution.py:164
  1051.6 52.0 %collective-permute-start.67 = (bf16[128,1152]{1,0:T(8,128)(2,1)}, bf16[128,1152]{1,0:T(8,128)(2,1)}, u32[]{:S(2)}, u32[]{:S(2)}) collective-permute-start(bf16[128,1152]{1,0:T(8,128)(2,1)} %convert_element_type.521), channel_id=1, source_target_pairs={{2,4},{5,5},{8,6},{11,7},{14,8},{16,9},{19,10},{22,11},{25,12},{28... | collective-permute-start | bytes 884744 | tf_op jit(solution)/shard_map/ppermute | solution.py:164
  1053.0 50.6 %collective-permute-start.66 = (bf16[128,1152]{1,0:T(8,128)(2,1)}, bf16[128,1152]{1,0:T(8,128)(2,1)}, u32[]{:S(2)}, u32[]{:S(2)}) collective-permute-start(bf16[128,1152]{1,0:T(8,128)(2,1)} %convert_element_type.521), channel_id=1, source_target_pairs={{1,4},{4,5},{7,6},{10,7},{13,8},{15,9},{18,10},{21,11},{24,12},{27... | collective-permute-start | bytes 884744 | tf_op jit(solution)/shard_map/ppermute | solution.py:164
  1054.4 49.2 %collective-permute-start.65 = (bf16[128,1152]{1,0:T(8,128)(2,1)}, bf16[128,1152]{1,0:T(8,128)(2,1)}, u32[]{:S(2)}, u32[]{:S(2)}) collective-permute-start(bf16[128,1152]{1,0:T(8,128)(2,1)} %convert_element_type.521), channel_id=1, source_target_pairs={{0,4},{3,5},{6,6},{9,7},{12,8},{14,9},{17,10},{20,11},{23,12},{26,... | collective-permute-start | bytes 884744 | tf_op jit(solution)/shard_map/ppermute | solution.py:164
  (286 other events, 4058.6 us)
Sparse Core Ops, SparseCore 0:
  45.6 202.9 all-gather.5
  252.1 135.0 all-gather.3
